TPU v7x, 256 devices: a whole 4x4x8 slice. The times are simulated.
256 devices in a mesh: dp: 32 (over x_lo, z, core), tensor: 8 (over y, x_hi).
Axes of the slice: x: 4 (x_hi: 2, x_lo: 2; x = x_hi * 2 + x_lo), y: 4, z: 8, core: 2. Of those that a mesh axis runs over, the one named last changes fastest.
Arguments:
- hidden: bfloat16 [8192, 18432], P('dp', 'tensor'), may hold values from -6 to 6
- down_weight: bfloat16 [18432, 2304], P('tensor', 'dp'), may hold values from -0.046875 to 0.046875
- norm_gain: float32 [2304], replicated, may hold values from 0.25 to 1.75
- teacher: bfloat16 [8192, 2304], P(('dp', 'tensor')), may hold values from -6 to 6
- error_memory: bfloat16 [32, 18432, 2304], P('dp', 'tensor'), may hold values from -0.59765625 to 0.59765625
- start_basis: bfloat16 [2304, 64], replicated, may hold values from -6 to 6
Outputs:
- normed: bfloat16 [8192, 2304], P(('dp', 'tensor'))
- left_basis: bfloat16 [18432, 64], P('tensor')
- right_factor: bfloat16 [2304, 64], replicated
All inputs are finite; a program needn't handle non-finite values.
Results may differ from a plain program's by a relative error of at most 0.0075.
Values may be sent and summed in bfloat16 or wider, within the bound.
No kernel may reach another device: no remote copies, remote signals or barrier semaphores. Data moves between devices by JAX's collectives and lax.ppermute only.
A program may use at most 128 MiB of HBM per device.

v0:
```python
import math

import jax
import jax.numpy as jnp
from jax import lax
from jax.sharding import PartitionSpec as P

FF = 18432
TOK_DEV = 256


def norm_head(mixed, norm_gain, target, tok_count):
    scale = lax.rsqrt(jnp.mean(mixed * mixed, axis=1, keepdims=True) + 1e-06)
    unit = mixed * scale
    normed_full = unit * norm_gain
    diff = normed_full - target.astype(jnp.float32)
    delta = diff / tok_count * norm_gain
    grad_f = scale * (delta - unit * jnp.mean(delta * unit, axis=1, keepdims=True))
    return (normed_full, grad_f.astype(jnp.bfloat16))


def orthonormal(rows, gram):
    lower = jnp.linalg.cholesky(gram)
    solved = lax.linalg.triangular_solve(lower, rows, left_side=False, lower=True, transpose_a=True)
    return (solved * math.sqrt(FF)).astype(jnp.bfloat16)


def per_device(hidden, down_weight, norm_gain, teacher, error_memory, start_basis):
    tok_rows = hidden.shape[0]
    memory = error_memory[0]
    partial_out = jnp.dot(
        hidden,
        lax.all_gather(down_weight, "dp", axis=1, tiled=True),
        preferred_element_type=jnp.float32,
    )
    share = tok_rows // lax.axis_size("tensor")
    mixed = lax.psum(partial_out, "tensor")
    target_all = lax.all_gather(teacher, "tensor", axis=0, tiled=True)
    normed_all, grad_out = norm_head(mixed, norm_gain, target_all, TOK_DEV)
    offset = lax.axis_index("tensor") * share
    normed_rows = lax.dynamic_slice_in_dim(normed_all, offset, share, 0)
    normed = normed_rows.astype(jnp.bfloat16)
    probe = jnp.dot(grad_out, start_basis, preferred_element_type=jnp.float32).astype(jnp.bfloat16)
    term = lax.dot_general(
        hidden, probe, (((0,), (0,)), ((), ())), preferred_element_type=jnp.float32
    )
    term = term + jnp.dot(memory, start_basis, preferred_element_type=jnp.float32)
    left_sum = lax.psum(term, "dp")
    gram = lax.psum(jnp.dot(left_sum.T, left_sum, precision=lax.Precision.HIGHEST), "tensor")
    left_basis = orthonormal(left_sum, gram)
    image = jnp.dot(hidden, left_basis, preferred_element_type=jnp.float32).astype(jnp.bfloat16)
    right_term = lax.dot_general(
        grad_out, image, (((0,), (0,)), ((), ())), preferred_element_type=jnp.float32
    )
    right_term = right_term + lax.dot_general(
        memory, left_basis, (((0,), (0,)), ((), ())), preferred_element_type=jnp.float32
    )
    right_total = lax.psum(right_term, ("dp", "tensor"))
    right_factor = (right_total / math.sqrt(FF)).astype(jnp.bfloat16)
    return (normed, left_basis, right_factor)


def solution(mesh):
    in_specs = (
        P("dp", "tensor"),
        P("tensor", "dp"),
        P(),
        P(("dp", "tensor"), None),
        P("dp", "tensor", None),
        P(),
    )
    out_specs = (P(("dp", "tensor"), None), P("tensor", None), P())
    return jax.shard_map(
        per_device, mesh=mesh, in_specs=in_specs, out_specs=out_specs, check_vma=False
    )
```

profile of v0, /device:TPU:1, one launch (start us, length us, event | category | flops | bytes accessed | tf_op | source)
XLA Modules:
  0.0 806.0 jit_solution(17334350454879639986)
XLA Ops:
  7.2 0.7 all-gather.3.cloned.1.call-update
  8.0 81.7 %all-gather.3.cloned.1.call-done = bf16[2304,2304]{0,1:T(8,128)(2,1)} async-done(((bf16[2304,72]{0,1:T(8,128)(2,1)}), bf16[2304,2304]{0,1:T(8,128)(2,1)}) %all-gather.3.cloned.1.call-update) | async-done | bytes 10616848 | tf_op jit(solution)/shard_map/all_gather | solution.py:33
  89.7 8.4 %fusion.12 = f32[256,2304]{1,0:T(8,128)} fusion(bf16[256,2304]{1,0:T(8,128)(2,1)S(1)} %copy-done, bf16[2304,2304]{0,1:T(8,128)(2,1)} %all-gather.3.cloned.1.call-done), kind=kOutput, calls=%fused_computation.31 | convolution fusion | flops 2717908992 | bytes 14155776 | tf_op jit(solution)/shard_map/dot_general | solution.py:31
  98.1 0.7 all-gather.5.cloned.1.call-update
  99.5 8.1 %fusion.2 = f32[2304,64]{0,1:T(8,128)} fusion(bf16[2304,64]{0,1:T(8,128)(2,1)S(1)} %copy-done.5, bf16[1,2304,2304]{2,1,0:T(8,128)(2,1)} %param.10), kind=kOutput, calls=%fused_computation.2 | convolution fusion | flops 679477248 | bytes 11501568 | tf_op jit(solution)/shard_map/dot_general | solution.py:47
  107.6 110.4 %all-reduce.4.cloned.1.call-done = f32[256,2304]{1,0:T(8,128)} async-done(((f32[256,2304]{1,0:T(8,128)}), f32[256,2304]{1,0:T(8,128)}) %all-reduce.4.cloned.1.call-update) | async-done | bytes 2359312 | tf_op jit(solution)/shard_map/psum | solution.py:37
  218.0 2.1 multiply_reduce_fusion.1
  220.0 50.2 %all-gather.5.cloned.1.call-done = bf16[256,2304]{1,0:T(8,128)(2,1)} async-done(((bf16[32,2304]{1,0:T(8,128)(2,1)}), bf16[256,2304]{1,0:T(8,128)(2,1)}) %all-gather.5.cloned.1.call-update) | async-done | bytes 1179664 | tf_op jit(solution)/shard_map/all_gather | solution.py:38
  270.2 2.1 multiply_reduce_fusion
  272.3 2.0 multiply_convert_fusion
  274.3 3.4 fusion.4
  277.7 1.3 multiply_multiply_fusion
  279.0 210.1 %all-reduce.6.cloned.1.call-done = f32[2304,64]{0,1:T(8,128)} async-done(((f32[2304,64]{0,1:T(8,128)}), f32[2304,64]{0,1:T(8,128)}) %all-reduce.6.cloned.1.call-update) | async-done | bytes 589840 | tf_op jit(solution)/shard_map/psum | solution.py:48
  489.2 1.9 fusion.13
  491.0 34.6 %psum.30 = f32[64,64]{0,1:T(8,128)S(1)} all-reduce(f32[64,64]{0,1:T(8,128)S(1)} %fusion.13), channel_id=1, replica_groups=mesh['dp'=32,'tensor'=8] {'tensor'}, use_global_device_ids=true, to_apply=%region_4.0 | all-reduce | flops 4096 | bytes 32768 | tf_op jit(solution)/shard_map/psum | solution.py:49
  525.7 5.8 cholesky.16
  532.2 0.7 fusion.9
  532.9 4.9 custom-call.6
  537.8 1.7 fusion.8
  539.5 6.1 fusion.5
  545.7 1.9 convolution_add_fusion
  547.6 1.6 dynamic-slice_convert_fusion
  549.1 248.5 %all-reduce.8.cloned.1.call-done = f32[2304,64]{0,1:T(8,128)} async-done(((f32[2304,64]{0,1:T(8,128)}), f32[2304,64]{0,1:T(8,128)}) %all-reduce.8.cloned.1.call-update) | async-done | bytes 589840 | tf_op jit(solution)/shard_map/psum | solution.py:58
  797.6 1.8 multiply_convert_fusion.1
  (31 shorter events, 1.7 us)
Async XLA Ops:
  7.2 82.5 %copy-start = (bf16[256,2304]{1,0:T(8,128)(2,1)S(1)}, bf16[256,2304]{1,0:T(8,128)(2,1)}, u32[]{:S(2)}) copy-start(bf16[256,2304]{1,0:T(8,128)(2,1)} %param.6) | copy-start | bytes 3538948
  7.2 82.5 %all-gather.3.cloned.1.call-start = ((), (), s32[]{:S(2)}) async-start(), calls=%async_computation | async-start | bytes 10948608 | tf_op jit(solution)/shard_map/all_gather | solution.py:33
  7.9 210.1 %all-reduce.4.cloned.1.call-start = ((), (), s32[]{:S(2)}) async-start(), calls=%async_computation.1 | async-start | bytes 4718592 | tf_op jit(solution)/shard_map/psum | solution.py:37
  98.0 0.8 copy-start.6
  98.0 1.4 copy-start.5
  98.1 172.1 %all-gather.5.cloned.1.call-start = ((), (), s32[]{:S(2)}) async-start(), calls=%async_computation.2 | async-start | bytes 1327104 | tf_op jit(solution)/shard_map/all_gather | solution.py:38
  98.8 390.4 %all-reduce.6.cloned.1.call-start = ((), (), s32[]{:S(2)}) async-start(), calls=%async_computation.3 | async-start | bytes 1179648 | tf_op jit(solution)/shard_map/psum | solution.py:48
  218.0 52.2 %copy-start.1 = (f32[256,2304]{1,0:T(8,128)S(1)}, f32[256,2304]{1,0:T(8,128)}, u32[]{:S(2)}) copy-start(f32[256,2304]{1,0:T(8,128)} %all-reduce.4.cloned.1.call-done) | copy-start | bytes 7077892
  270.2 2.1 copy-start.3
  270.2 2.1 copy-start.7
  277.7 520.0 %all-reduce.8.cloned.1.call-start = ((), (), s32[]{:S(2)}) async-start(), calls=%async_computation.4 | async-start | bytes 1179648 | tf_op jit(solution)/shard_map/psum | solution.py:58
  539.5 6.1 copy-start.4
  539.5 6.1 copy-start.2
Sparse Core Ops, SparseCore 0:
  9.9 79.7 all-gather.2
  98.2 119.7 all-reduce.3
  220.6 49.5 all-gather.4
  277.8 211.3 all-reduce.5
  547.7 249.9 all-reduce.7
where the time goes:
time: 806 us
  waiting for transfers between devices  702 us (87%)
  blocking collectives  34.6 us (4%)
  matrix products  31.5 us (4%)
  other arithmetic  21.9 us (3%)
  between operations  13.9 us (2%)
    psum x1, waiting for transfers between devices, per_device(): right_total = lax.psum(right_term, ('dp', 'tensor'))  248 us
    psum x1, waiting for transfers between devices, per_device(): left_sum = lax.psum(term, 'dp')  210 us
    psum x1, waiting for transfers between devices, per_device(): mixed = lax.psum(partial_out, 'tensor')  110 us
    all_gather x1, waiting for transfers between devices, per_device(): lax.all_gather(down_weight, 'dp', axis=1, tiled=True)  81.7 us
    all_gather x1, waiting for transfers between devices, per_device(): target_all = lax.all_gather(teacher, 'tensor', axis=0, tiled=True)  50.2 us
    psum x1, blocking collectives, per_device(): lax.psum(jnp.dot(left_sum.T, left_sum, precision=lax.Precision.HIGHEST),...  34.6 us
  transfers between devices with their start and end apart: 5, of which 5 were waited for; matrix products, arithmetic and copies ran while one was open for 2% of the time, Pallas kernels for 0%

commit v1 on v0

v1 whole, which is shorter than its diff:
```python
import math

import jax
import jax.numpy as jnp
from jax import lax
from jax.sharding import Mesh
from jax.sharding import PartitionSpec as P

DP = ("xl", "z", "c")
TENSOR = ("y", "xh")
SWAP = [(0, 1), (1, 0)]
F32 = jnp.float32
BF16 = jnp.bfloat16


def dot(a, b, dims, precision=None):
    return lax.dot_general(a, b, (dims, ((), ())), precision=precision, preferred_element_type=F32)


def split_bf16(x):
    high = lax.reduce_precision(x, 8, 7)
    low = x - high
    return jnp.concatenate([high.astype(BF16), low.astype(BF16)], axis=0)


def share_out(x, axes):
    n = lax.axis_size(axes)
    return lax.all_to_all(jnp.broadcast_to(x[None], (n,) + x.shape), axes, 0, 0)


def pair(x, axis):
    other = lax.ppermute(x, axis, SWAP)
    first = lax.axis_index(axis) == 0
    return jnp.where(first, jnp.stack([x, other]), jnp.stack([other, x]))


def sum_pair_halves(x, axis):
    half = x.shape[-1] // 2
    first = lax.axis_index(axis) == 0
    mine = jnp.where(first, x[..., :half], x[..., half:])
    theirs = jnp.where(first, x[..., half:], x[..., :half])
    return mine + lax.ppermute(theirs, axis, SWAP)


def per_device(hidden, down_weight, norm_gain, teacher, error_memory, start_basis):
    memory = error_memory[0]
    tokens, units = hidden.shape
    feats, rank = start_basis.shape
    block = down_weight.shape[1]
    n_z = lax.axis_size("z")
    n_t = lax.axis_size(TENSOR)
    share = tokens // n_t
    all_units = units * n_t

    columns = lax.all_gather(down_weight.T, "z", axis=0, tiled=True)
    rows = pair(hidden, "xl")
    rows = jnp.swapaxes(pair(rows, "c"), 0, 1)
    partial_out = dot(rows.reshape(4 * tokens, units), columns, ((1,), (1,))).astype(BF16)
    parts = lax.all_to_all(
        partial_out.reshape(4 * n_t, share, n_z * block), ("xl", "c") + TENSOR, 0, 0
    )
    mixed = jnp.sum(parts.reshape(2, 2, n_t, share, n_z, block).astype(F32), axis=2)
    mixed = jnp.transpose(mixed, (2, 0, 3, 1, 4)).reshape(share, feats)

    scale = lax.rsqrt(jnp.mean(mixed * mixed, axis=1, keepdims=True) + 1e-06)
    unit = mixed * scale
    normed_full = unit * norm_gain
    delta = (normed_full - teacher.astype(F32)) / tokens * norm_gain
    grad = (scale * (delta - unit * jnp.mean(delta * unit, axis=1, keepdims=True))).astype(BF16)
    normed = normed_full.astype(BF16)
    grad_all = lax.all_gather(grad, TENSOR, axis=0, tiled=True)

    probe = dot(grad, start_basis, ((1,), (0,))).astype(BF16)
    probe_all = share_out(probe, TENSOR).reshape(tokens, rank)
    term = dot(start_basis, memory, ((0,), (1,))) + dot(probe_all, hidden, ((0,), (0,)))
    half = sum_pair_halves(term, "c")
    pieces = lax.all_to_all(half.reshape(2 * n_z, rank // (2 * n_z), units // 2), ("xl", "z"), 0, 0)
    piece = jnp.sum(pieces, axis=0)
    half = share_out(piece, ("xl", "z")).reshape(rank, units // 2)
    left = jnp.transpose(pair(half, "c"), (1, 0, 2)).reshape(rank, units)

    left2 = split_bf16(left)
    gram = dot(left, left, ((1,), (1,)), lax.Precision.HIGHEST)
    image = dot(left2, hidden, ((1,), (1,)))
    image = image[:rank] + image[rank:]
    pulled = dot(left2, memory, ((1,), (0,)))
    pulled = pulled[:rank] + pulled[rank:]
    lines = rank // n_t
    message = jnp.concatenate(
        [
            pulled.reshape(n_t, lines, feats),
            image.reshape(n_t, lines, tokens),
            jnp.broadcast_to(gram.reshape(1, lines, n_t * rank), (n_t, lines, n_t * rank)),
        ],
        axis=2,
    )
    message = jnp.sum(lax.all_to_all(message, TENSOR, 0, 0), axis=0)
    pulled = message[:, :feats]
    image = message[:, feats : feats + tokens]
    gram = message[:, feats + tokens :].reshape(rank, rank)

    right = dot(split_bf16(image), grad_all, ((1,), (0,)))
    right = right[:lines] + right[lines:] + pulled
    right = jnp.sum(share_out(sum_pair_halves(right, "c"), ("xl", "z")), axis=0)
    right = share_out(right, ("c",) + TENSOR)
    right = jnp.transpose(right.reshape(2, rank, feats // 2), (1, 0, 2)).reshape(rank, feats)

    lower = jnp.linalg.cholesky(gram)
    inverse = lax.linalg.triangular_solve(lower, jnp.eye(rank, dtype=F32), left_side=True, lower=True)
    left_basis = dot(left, inverse, ((0,), (1,)), lax.Precision.HIGHEST) * math.sqrt(all_units)
    right_factor = dot(right, inverse, ((0,), (1,)), lax.Precision.HIGHEST)
    return normed, left_basis.astype(BF16), right_factor.astype(BF16)


def solution(mesh):
    fine = Mesh(mesh.devices.reshape(2, 8, 2, 4, 2), DP + TENSOR)
    in_specs = (
        P(DP, TENSOR),
        P(TENSOR, DP),
        P(),
        P(DP + TENSOR, None),
        P(DP, TENSOR, None),
        P(),
    )
    out_specs = (P(DP + TENSOR, None), P(TENSOR, None), P())
    return jax.shard_map(
        per_device, mesh=fine, in_specs=in_specs, out_specs=out_specs, check_vma=False
    )
```

time: 806 us -> 255 us (0.32)
  waiting for transfers between devices: 702 us -> 90 us
  starting transfers between devices: 0.2 us -> 39 us
  blocking collectives: 34.6 us -> 48 us
    psum x3 -> x0, waiting for transfers between devices: 569 us -> none  [the longest x1 248 us: per_device(): right_total = lax.psum(right_term, ('dp', 'tensor'))]
    all_gather x2, waiting for transfers between devices: 132 us -> 25.1 us  [the longest x1 23 us: per_device(): grad_all = lax.all_gather(grad, TENSOR, axis=0, tiled=True)]
    all_to_all x0 -> x3, blocking collectives: none -> 48 us  [the longest x1 20.3 us: per_device(): message = jnp.sum(lax.all_to_all(message, TENSOR, 0, 0), axis=0)]
    psum x1 -> x0, blocking collectives: 34.6 us -> none  [per_device(): lax.psum(jnp.dot(left_sum.T, left_sum, precision=lax.Precision.HIGHEST),...]
    all_to_all x0 -> x4, waiting for transfers between devices: none -> 32.5 us  [the longest x1 19.9 us: per_device(): lax.all_to_all(partial_out.reshape(4 * n_t, share, n_z * block), ('xl', '...]
    ppermute x0 -> x5, waiting for transfers between devices: none -> 31.7 us  [the longest x3 29.6 us: pair(): other = lax.ppermute(x, axis, SWAP)]
    all_to_all x0 -> x4, starting transfers between devices: none -> 27.7 us  [the longest x3 17.3 us: share_out(): return lax.all_to_all(jnp.broadcast_to(x[None], (n,) + x.shape), axes, 0, 0)]
    ppermute x0 -> x5, starting transfers between devices: none -> 11.2 us  [the longest x3 7.73 us: pair(): other = lax.ppermute(x, axis, SWAP)]
  transfers between devices with their start and end apart: 5 -> 11, of which waited for: 5 -> 10; matrix products, arithmetic and copies ran while one was open for 2% -> 16% of each run, Pallas kernels for 0% -> 0%
where the time goes in v1:
time: 255 us; the launch traced here: 254 us
  waiting for transfers between devices  90 us (35%)
  blocking collectives  48 us (19%)
  starting transfers between devices  39 us (15%)
  other arithmetic  28.1 us (11%)
  matrix products  25.2 us (10%)
  between operations  14.4 us (6%)
  local copies, waits for them, and re-layouts  9.43 us (4%)
    ppermute x3, waiting for transfers between devices, pair(): other = lax.ppermute(x, axis, SWAP)  29.6 us
    dot_general x10, matrix products, dot(): lax.dot_general(a, b, (dims, ((), ())), precision=precision, preferred_el...  25 us
    all_gather x1, waiting for transfers between devices, per_device(): grad_all = lax.all_gather(grad, TENSOR, axis=0, tiled=True)  23 us
    all_to_all x1, blocking collectives, per_device(): message = jnp.sum(lax.all_to_all(message, TENSOR, 0, 0), axis=0)  20.3 us
    all_to_all x1, waiting for transfers between devices, per_device(): lax.all_to_all(partial_out.reshape(4 * n_t, share, n_z * block), ('xl', '...  19.9 us
    all_to_all x3, starting transfers between devices, share_out(): return lax.all_to_all(jnp.broadcast_to(x[None], (n,) + x.shape), axes, 0, 0)  17.3 us
    all_to_all x1, blocking collectives, share_out(): return lax.all_to_all(jnp.broadcast_to(x[None], (n,) + x.shape), axes, 0, 0)  14.1 us
    all_to_all x1, blocking collectives, per_device(): lax.all_to_all(half.reshape(2 * n_z, rank // (2 * n_z), units // 2), ('xl...  13.7 us
  transfers between devices with their start and end apart: 11, of which 10 were waited for; matrix products, arithmetic and copies ran while one was open for 16% of the time, Pallas kernels for 0%

profile of v1, /device:TPU:1, one launch (start us, length us, event | category | flops | bytes accessed | tf_op | source)
XLA Modules:
  0.0 254.1 jit_solution(13690276622927986422)
XLA Ops:
  10.0 24.7 %collective-permute-done = bf16[256,2304]{1,0:T(8,128)(2,1)S(1)} collective-permute-done((bf16[256,2304]{1,0:T(8,128)(2,1)}, bf16[256,2304]{1,0:T(8,128)(2,1)S(1)}, u32[]{:S(2)}, u32[]{:S(2)}) %collective-permute-start) | collective-permute-done | bytes 1179680 | tf_op jit(solution)/shard_map/ppermute | solution.py:32
  34.7 3.6 %maximum_select_fusion.1 = bf16[2,256,2304]{2,1,0:T(8,128)(2,1)} fusion(bf16[1,256,2304]{2,1,0:T(8,128)(2,1)S(1)} %bitcast.67, bf16[1,256,2304]{2,1,0:T(8,128)(2,1)} %bitcast.63, pred[]{:T(512)S(6)} %eq.5), kind=kLoop, calls=%fused_computation.12 | loop fusion | flops 3538944 | bytes 4718593 | tf_op jit(solution)/shard_map/jit(_where)/select_n | solution.py:34
  38.3 2.5 collective-permute-start.1
  41.2 4.1 %collective-permute-done.1 = bf16[2,256,2304]{2,1,0:T(8,128)(2,1)} collective-permute-done((bf16[2,256,2304]{2,1,0:T(8,128)(2,1)}, bf16[2,256,2304]{2,1,0:T(8,128)(2,1)}, u32[]{:S(2)}, u32[]{:S(2)}) %collective-permute-start.1) | collective-permute-done | bytes 2359328 | tf_op jit(solution)/shard_map/ppermute | solution.py:32
  45.3 5.8 %maximum_select_fusion = bf16[2,2,256,2304]{3,2,0,1:T(8,128)(2,1)} fusion(bf16[1,2,256,2304]{3,2,0,1:T(8,128)(2,1)} %bitcast.6, bf16[1,2,256,2304]{3,2,0,1:T(8,128)(2,1)S(1)} %fusion.5, pred[]{:T(512)S(6)} %eq.4), kind=kLoop, calls=%fused_computation.4 | loop fusion | flops 7077888 | bytes 9437185 | tf_op jit(solution)/shard_map/jit(_where)/select_n | solution.py:34
  53.2 6.1 %convolution_convert_fusion.1 = bf16[1024,576]{0,1:T(8,128)(2,1)S(1)} fusion(bf16[1024,2304]{1,0:T(8,128)(2,1)} %bitcast.70, bf16[576,2304]{1,0:T(8,128)(2,1)} %all-gather.3.cloned.1.call-done), kind=kOutput, calls=%fused_computation.13 | convolution fusion | flops 2718498816 | bytes 8552448 | tf_op jit(solution)/shard_map/dot_general | solution.py:17
  60.8 10.3 %all-to-all-start = ((bf16[32,32,576]{2,1,0:T(8,128)(2,1)}), bf16[32,32,576]{2,1,0:T(8,128)(2,1)S(1)}, u32[]{:S(2)}, u32[]{:S(2)}) async-start(bf16[32,32,576]{2,1,0:T(8,128)(2,1)} %bitcast.10), calls=%async_computation | async-start | bytes 2621440 | tf_op jit(solution)/shard_map/all_to_all | solution.py:59
  71.2 19.9 %all-to-all-done = bf16[32,32,576]{2,1,0:T(8,128)(2,1)S(1)} async-done(((bf16[32,32,576]{2,1,0:T(8,128)(2,1)}), bf16[32,32,576]{2,1,0:T(8,128)(2,1)S(1)}, u32[]{:S(2)}, u32[]{:S(2)}) %all-to-all-start) | async-done | bytes 1179680 | tf_op jit(solution)/shard_map/all_to_all | solution.py:59
  91.1 3.2 %reshape.144 = f32[2,2,8,32,8,72]{5,4,3,2,1,0:T(8,128)} reshape(bf16[32,32,576]{2,1,0:T(8,128)(2,1)S(1)} %all-to-all-done) | data formatting | bytes 3538944 | tf_op jit(solution)/shard_map/convert_element_type | solution.py:62
  94.3 2.6 %reduce_sum.54 = f32[2,2,32,8,72]{4,3,2,1,0:T(8,128)S(1)} reduce(f32[2,2,8,32,8,72]{5,4,3,2,1,0:T(8,128)} %reshape.144, f32[]{:T(128)} %constant.57.clone.1), dimensions={2}, to_apply=%region_0.1 | reduce | flops 516096 | bytes 2654212 | tf_op jit(solution)/shard_map/reduce_sum | solution.py:62
  100.4 3.3 %all-to-all-start.1 = ((bf16[8,2,1024]{2,1,0:T(2,128)(2,1)}), bf16[8,2,1024]{2,1,0:T(2,128)(2,1)S(1)}, u32[]{:S(2)}, u32[]{:S(2)}) async-start(bf16[8,2,1024]{2,1,0:T(2,128)(2,1)} %reshape.146), calls=%async_computation.1 | async-start | bytes 65536 | tf_op jit(solution)/shard_map/all_to_all | solution.py:28
  103.8 7.3 %fusion.2 = f32[64,2304]{1,0:T(8,128)S(1)} fusion(bf16[2304,64]{0,1:T(8,128)(2,1)S(1)} %copy-done, bf16[1,2304,2304]{2,1,0:T(8,128)(2,1)} %param.10), kind=kOutput, calls=%fused_computation.2 | convolution fusion | flops 679477248 | bytes 11501568 | tf_op jit(solution)/shard_map/dot_general | solution.py:17
  114.4 13.7 %all_to_all.35 = f32[16,4,1152]{2,1,0:T(4,128)S(1)} all-to-all(f32[16,4,1152]{2,1,0:T(4,128)S(1)} %reshape.136), channel_id=1, replica_groups=mesh['xl'=2,'z'=8,'c'=2,'y'=4,'xh'=2] {'xl','z'}, dimensions={0} | all-to-all | bytes 589824 | tf_op jit(solution)/shard_map/all_to_all | solution.py:77
  128.2 14.1 %all_to_all.36 = f32[16,4,1152]{2,1,0:T(4,128)S(1)} all-to-all(f32[16,4,1152]{2,1,0:T(4,128)S(1)} %broadcast_in_dim.14), channel_id=1, replica_groups=mesh['xl'=2,'z'=8,'c'=2,'y'=4,'xh'=2] {'xl','z'}, dimensions={0} | all-to-all | bytes 589824 | tf_op jit(solution)/shard_map/all_to_all | solution.py:28
  142.4 3.1 %collective-permute-start.3 = (f32[64,1152]{1,0:T(8,128)S(1)}, f32[64,1152]{1,0:T(8,128)S(1)}, u32[]{:S(2)}, u32[]{:S(2)}) collective-permute-start(f32[64,1152]{1,0:T(8,128)S(1)} %reshape.137), channel_id=1, source_target_pairs={{0,8},{8,0},{1,9},{9,1},{2,10},{10,2},{3,11},{11,3},{4,12},{12,4},... | collective-permute-start | bytes 884744 | tf_op jit(solution)/shard_map/ppermute | solution.py:32
  147.9 5.6 %fusion = f32[128,2304]{1,0:T(8,128)S(1)} fusion(bf16[1,2304,2304]{2,1,0:T(8,128)(2,1)} %param.10, bf16[64,2304]{1,0:T(8,128)(2,1)S(1)} %get-tuple-element.4, bf16[64,2304]{1,0:T(8,128)(2,1)S(1)} %get-tuple-element.3), kind=kOutput, calls=%fused_computation | convolution fusion | flops 1360134144 | bytes 12386304 | tf_op jit(solution)/shard_map/dot_general | solution.py:17
  155.8 20.3 %all_to_all.37 = f32[8,8,3072]{2,1,0:T(8,128)S(1)} all-to-all(f32[8,8,3072]{2,1,0:T(8,128)S(1)} %pad_maximum_fusion), channel_id=1, replica_groups=mesh['xl'=2,'z'=8,'c'=2,'y'=4,'xh'=2] {'y','xh'}, dimensions={0} | all-to-all | bytes 1572864 | tf_op jit(solution)/shard_map/all_to_all | solution.py:97
  176.1 23.0 %all-gather.5.cloned.1.call-done = bf16[256,2304]{1,0:T(8,128)(2,1)} async-done(((bf16[32,2304]{1,0:T(8,128)(2,1)}), bf16[256,2304]{1,0:T(8,128)(2,1)}) %all-gather.5.cloned.1.call-update) | async-done | bytes 1179664 | tf_op jit(solution)/shard_map/all_gather | solution.py:71
  204.5 6.8 %all-to-all-start.5 = ((f32[16,8,1152]{2,1,0:T(8,128)}), f32[16,8,1152]{2,1,0:T(8,128)S(1)}, u32[]{:S(2)}, u32[]{:S(2)}) async-start(f32[16,8,1152]{2,1,0:T(8,128)} %broadcast_in_dim.17), calls=%async_computation.5 | async-start | bytes 1179648 | tf_op jit(solution)/shard_map/all_to_all | solution.py:28
  211.6 5.8 %cholesky.17 = f32[64,64]{1,0:T(8,128)S(1)} custom-call(f32[64,64]{1,0:T(8,128)S(1)} %fusion.14), custom_call_target="Cholesky" | custom-call | tf_op jit(solution)/shard_map/jit(cholesky)/cholesky | solution.py:108
  218.1 9.0 %all-to-all-done.5 = f32[16,8,1152]{2,1,0:T(8,128)S(1)} async-done(((f32[16,8,1152]{2,1,0:T(8,128)}), f32[16,8,1152]{2,1,0:T(8,128)S(1)}, u32[]{:S(2)}, u32[]{:S(2)}) %all-to-all-start.5) | async-done | bytes 589856 | tf_op jit(solution)/shard_map/all_to_all | solution.py:28
  228.0 7.1 %all-to-all-start.6 = ((f32[16,8,1152]{2,1,0:T(8,128)}), f32[16,8,1152]{2,1,0:T(8,128)S(1)}, u32[]{:S(2)}, u32[]{:S(2)}) async-start(f32[16,8,1152]{2,1,0:T(8,128)} %broadcast_in_dim.18), calls=%async_computation.6 | async-start | bytes 1179648 | tf_op jit(solution)/shard_map/all_to_all | solution.py:28
  235.8 4.9 %custom-call.6 = f32[1,64,64]{1,2,0:T(8,128)S(1)} custom-call(f32[1,64,64]{2,1,0:T(8,128)S(1)} %fusion.11), custom_call_target="InvertDiagBlocksLowerTriangular" | custom-call | tf_op jit(solution)/shard_map/triangular_solve | solution.py:109
  242.3 3.5 %all-to-all-done.6 = f32[16,8,1152]{2,1,0:T(8,128)S(1)} async-done(((f32[16,8,1152]{2,1,0:T(8,128)}), f32[16,8,1152]{2,1,0:T(8,128)S(1)}, u32[]{:S(2)}, u32[]{:S(2)}) %all-to-all-start.6) | async-done | bytes 589856 | tf_op jit(solution)/shard_map/all_to_all | solution.py:28
  (76 shorter events, 29.2 us)
Async XLA Ops:
  7.2 92.3 %copy-start = (bf16[2304,64]{0,1:T(8,128)(2,1)S(1)}, bf16[2304,64]{0,1:T(8,128)(2,1)}, u32[]{:S(2)}) copy-start(bf16[2304,64]{0,1:T(8,128)(2,1)} %param.11) | copy-start | bytes 884740
  7.2 46.1 %all-gather.3.cloned.1.call-start = ((), (), s32[]{:S(2)}) async-start(), calls=%async_computation.7 | async-start | bytes 2985984 | tf_op jit(solution)/shard_map/all_gather | solution.py:55
  7.9 26.8 %collective-permute-start = (bf16[256,2304]{1,0:T(8,128)(2,1)}, bf16[256,2304]{1,0:T(8,128)(2,1)S(1)}, u32[]{:S(2)}, u32[]{:S(2)}) collective-permute-start(bf16[256,2304]{1,0:T(8,128)(2,1)} %param.6), channel_id=1, source_target_pairs={{0,128},{128,0},{1,129},{129,1},{2,130},{130,2},{3,131},{131,3},{4... | collective-permute-start | bytes 3538952 | tf_op jit(solution)/shard_map/ppermute | solution.py:32
  34.7 6.1 %copy-start.1 = (bf16[256,2304]{1,0:T(8,128)(2,1)S(1)}, bf16[256,2304]{1,0:T(8,128)(2,1)}, u32[]{:S(2)}) copy-start(bf16[256,2304]{1,0:T(8,128)(2,1)} %param.6) | copy-start | bytes 3538948
  38.3 7.0 %collective-permute-start.1 = (bf16[2,256,2304]{2,1,0:T(8,128)(2,1)}, bf16[2,256,2304]{2,1,0:T(8,128)(2,1)}, u32[]{:S(2)}, u32[]{:S(2)}) collective-permute-start(bf16[2,256,2304]{2,1,0:T(8,128)(2,1)} %maximum_select_fusion.1), channel_id=1, source_target_pairs={{0,8},{8,0},{1,9},{9,1},{2,10},{10,2},{3,11},{11,3},{4,12},{12,4},... | collective-permute-start | bytes 7077896 | tf_op jit(solution)/shard_map/ppermute | solution.py:32
  59.4 11.8 %copy-start.4 = (f32[2304]{0:T(1024)S(1)}, f32[2304]{0:T(1024)}, u32[]{:S(2)}) copy-start(f32[2304]{0:T(1024)} %param.8) | copy-start | bytes 27652
  60.8 30.3 %all-to-all-start = ((bf16[32,32,576]{2,1,0:T(8,128)(2,1)}), bf16[32,32,576]{2,1,0:T(8,128)(2,1)S(1)}, u32[]{:S(2)}, u32[]{:S(2)}) async-start(bf16[32,32,576]{2,1,0:T(8,128)(2,1)} %bitcast.10), calls=%async_computation | async-start | bytes 2621440 | tf_op jit(solution)/shard_map/all_to_all | solution.py:59
  96.9 1.5 copy-start.3
  99.5 11.7 %copy-start.2 = (bf16[32,2304]{1,0:T(8,128)(2,1)}, bf16[32,2304]{1,0:T(8,128)(2,1)S(1)}, u32[]{:S(2)}) copy-start(bf16[32,2304]{1,0:T(8,128)(2,1)S(1)} %get-tuple-element.5) | copy-start | bytes 442372
  100.4 10.7 %all-to-all-start.1 = ((bf16[8,2,1024]{2,1,0:T(2,128)(2,1)}), bf16[8,2,1024]{2,1,0:T(2,128)(2,1)S(1)}, u32[]{:S(2)}, u32[]{:S(2)}) async-start(bf16[8,2,1024]{2,1,0:T(2,128)(2,1)} %reshape.146), calls=%async_computation.1 | async-start | bytes 65536 | tf_op jit(solution)/shard_map/all_to_all | solution.py:28
  103.8 95.3 %all-gather.5.cloned.1.call-start = ((), (), s32[]{:S(2)}) async-start(), calls=%async_computation.8 | async-start | bytes 1327104 | tf_op jit(solution)/shard_map/all_gather | solution.py:71
  111.7 2.6 %collective-permute-start.2 = (f32[64,1152]{1,0:T(8,128)S(1)}, f32[64,1152]{1,0:T(8,128)S(1)}, u32[]{:S(2)}, u32[]{:S(2)}) collective-permute-start(f32[64,1152]{1,0:T(8,128)S(1)} %slice_select_fusion), channel_id=1, source_target_pairs={{0,8},{8,0},{1,9},{9,1},{2,10},{10,2},{3,11},{11,3},{4,12},{12,4},... | collective-permute-start | bytes 884744 | tf_op jit(solution)/shard_map/ppermute | solution.py:42
  142.4 4.3 %collective-permute-start.3 = (f32[64,1152]{1,0:T(8,128)S(1)}, f32[64,1152]{1,0:T(8,128)S(1)}, u32[]{:S(2)}, u32[]{:S(2)}) collective-permute-start(f32[64,1152]{1,0:T(8,128)S(1)} %reshape.137), channel_id=1, source_target_pairs={{0,8},{8,0},{1,9},{9,1},{2,10},{10,2},{3,11},{11,3},{4,12},{12,4},... | collective-permute-start | bytes 884744 | tf_op jit(solution)/shard_map/ppermute | solution.py:32
  200.7 3.0 %collective-permute-start.4 = (f32[8,1152]{1,0:T(8,128)S(1)}, f32[8,1152]{1,0:T(8,128)S(1)}, u32[]{:S(2)}, u32[]{:S(2)}) collective-permute-start(f32[8,1152]{1,0:T(8,128)S(1)} %slice_select_fusion.1), channel_id=1, source_target_pairs={{0,8},{8,0},{1,9},{9,1},{2,10},{10,2},{3,11},{11,3},{4,12},{12,4},... | collective-permute-start | bytes 110600 | tf_op jit(solution)/shard_map/ppermute | solution.py:42
  204.5 22.6 %all-to-all-start.5 = ((f32[16,8,1152]{2,1,0:T(8,128)}), f32[16,8,1152]{2,1,0:T(8,128)S(1)}, u32[]{:S(2)}, u32[]{:S(2)}) async-start(f32[16,8,1152]{2,1,0:T(8,128)} %broadcast_in_dim.17), calls=%async_computation.5 | async-start | bytes 1179648 | tf_op jit(solution)/shard_map/all_to_all | solution.py:28
  228.0 17.8 %all-to-all-start.6 = ((f32[16,8,1152]{2,1,0:T(8,128)}), f32[16,8,1152]{2,1,0:T(8,128)S(1)}, u32[]{:S(2)}, u32[]{:S(2)}) async-start(f32[16,8,1152]{2,1,0:T(8,128)} %broadcast_in_dim.18), calls=%async_computation.6 | async-start | bytes 1179648 | tf_op jit(solution)/shard_map/all_to_all | solution.py:28
Sparse Core Ops, SparseCore 0:
  9.8 43.3 all-gather.2
  145.7 53.3 all-gather.4

commit v2 on v1

v2 whole, which is shorter than its diff:
```python
import functools
import math

import jax
import jax.numpy as jnp
from jax import lax
from jax.experimental import pallas as pl
from jax.experimental.pallas import tpu as pltpu
from jax.sharding import Mesh
from jax.sharding import PartitionSpec as P

DP = ("xl", "z", "c")
TENSOR = ("y", "xh")
SWAP = [(0, 1), (1, 0)]
F32 = jnp.float32
BF16 = jnp.bfloat16


def dot(a, b, dims, precision=None):
    return lax.dot_general(a, b, (dims, ((), ())), precision=precision, preferred_element_type=F32)


def split_bf16(x):
    high = lax.reduce_precision(x, 8, 7)
    low = x - high
    return jnp.concatenate([high.astype(BF16), low.astype(BF16)], axis=0)


def share_out(x, axes):
    n = lax.axis_size(axes)
    return lax.all_to_all(jnp.broadcast_to(x[None], (n,) + x.shape), axes, 0, 0)


def pair(x, axis):
    other = lax.ppermute(x, axis, SWAP)
    first = lax.axis_index(axis) == 0
    return jnp.concatenate([jnp.where(first, x, other), jnp.where(first, other, x)], axis=0)


def sum_pair_halves(x, axis, dim):
    low, high = jnp.split(x, 2, axis=dim)
    first = lax.axis_index(axis) == 0
    return jnp.where(first, low, high) + lax.ppermute(jnp.where(first, high, low), axis, SWAP)


def shift(x, axis, by):
    n = lax.axis_size(axis)
    return lax.ppermute(x, axis, [(i, (i + by) % n) for i in range(n)])


def columns_kernel(me_ref, *refs):
    *sources, out_ref, rows, blocks, columns, row_sems, block_sems = refs
    n_z, block, units = blocks.shape
    cut = rows.shape[1] // 4
    targets = [rows.at[k] for k in range(3)] + [rows.at[3, k * cut : (k + 1) * cut] for k in range(4)]
    targets += [blocks.at[k] for k in range(n_z) if k != n_z // 2]
    targets += [blocks.at[n_z // 2, :, : units // 2], blocks.at[n_z // 2, :, units // 2 :]]
    sems = [row_sems.at[k] for k in range(7)] + [block_sems.at[k] for k in range(n_z + 1)]
    copies = [pltpu.make_async_copy(*args) for args in zip(sources, targets, sems)]
    for copy in copies[7:] + copies[:7]:
        copy.start()
    for copy in copies[7:]:
        copy.wait()
    for k in range(n_z):
        columns[k * block : (k + 1) * block, :] = blocks[k]
    for k in range(4):
        for copy in copies[k : k + 1] if k < 3 else copies[3:7]:
            copy.wait()
        out_ref[me_ref[0] ^ k] = dot(rows[k], columns[...], ((1,), (1,))).astype(BF16)


def column_products(rows, blocks):
    tokens, units = rows[0].shape
    block = blocks[0].shape[0]
    n_z = lax.axis_size("z")
    me = 2 * lax.axis_index("xl") + lax.axis_index("c")
    return pl.pallas_call(
        columns_kernel,
        out_shape=jax.ShapeDtypeStruct((4, tokens, n_z * block), BF16),
        in_specs=[pl.BlockSpec(memory_space=pltpu.SMEM)]
        + [pl.BlockSpec(memory_space=pl.ANY)] * (len(rows) + len(blocks)),
        out_specs=pl.BlockSpec(memory_space=pltpu.VMEM),
        scratch_shapes=[
            pltpu.VMEM((4, tokens, units), BF16),
            pltpu.VMEM((n_z, block, units), BF16),
            pltpu.VMEM((n_z * block, units), BF16),
            pltpu.SemaphoreType.DMA((7,)),
            pltpu.SemaphoreType.DMA((n_z + 1,)),
        ],
        compiler_params=pltpu.CompilerParams(vmem_limit_bytes=56 * 2**20),
    )(me.reshape(1), *rows, *blocks)


def norm_kernel(z_ref, parts_ref, gain_ref, teacher_ref, basis_ref, normed_ref, sent_ref, blocks, mixed_ref, *, tokens):
    n_z, _, _, two = blocks.shape
    block = two // 2
    share, feats = mixed_ref.shape
    n_t = parts_ref.shape[0] // 4
    for x in range(2):
        for c in range(2):
            total = jnp.zeros((share, n_z * block), F32)
            for t in range(n_t):
                total += parts_ref[(2 * x + c) * n_t + t].astype(F32)
            for k in range(n_z):
                blocks[k, x, :, c * block : (c + 1) * block] = total[:, k * block : (k + 1) * block]
    for x in range(2):
        for z in range(n_z):
            at = (x * n_z + z) * two
            mixed_ref[:, at : at + two] = blocks[lax.rem(z - z_ref[0] + n_z, n_z), x]
    mixed = mixed_ref[...]
    gain = gain_ref[...]
    scale = lax.rsqrt(jnp.mean(mixed * mixed, axis=1, keepdims=True) + 1e-06)
    unit = mixed * scale
    normed_full = unit * gain
    normed_ref[...] = normed_full.astype(BF16)
    delta = (normed_full - teacher_ref[...].astype(F32)) * (gain / tokens)
    grad = (scale * (delta - unit * jnp.mean(delta * unit, axis=1, keepdims=True))).astype(BF16)
    probe = dot(grad, basis_ref[...], ((1,), (1,))).astype(BF16)
    for t in range(n_t):
        sent_ref[t, :, :feats] = grad
        sent_ref[t, :, feats:] = probe


def norm_head(parts, norm_gain, teacher, basis_t, tokens):
    share, feats = teacher.shape
    n_z = lax.axis_size("z")
    n_t = parts.shape[0] // 4
    vmem = pl.BlockSpec(memory_space=pltpu.VMEM)
    return pl.pallas_call(
        functools.partial(norm_kernel, tokens=tokens),
        out_shape=(
            jax.ShapeDtypeStruct((share, feats), BF16),
            jax.ShapeDtypeStruct((n_t, share, feats + basis_t.shape[0]), BF16),
        ),
        in_specs=[pl.BlockSpec(memory_space=pltpu.SMEM)] + [vmem] * 4,
        out_specs=(vmem, vmem),
        scratch_shapes=[
            pltpu.VMEM((n_z, 2, share, feats // (2 * n_z)), F32),
            pltpu.VMEM((share, feats), F32),
        ],
        compiler_params=pltpu.CompilerParams(vmem_limit_bytes=32 * 2**20),
    )(lax.axis_index("z").reshape(1), parts, norm_gain.reshape(1, feats), teacher, basis_t)


def per_device(hidden, down_weight, norm_gain, teacher, error_memory, start_basis):
    memory = error_memory[0]
    tokens, units = hidden.shape
    feats, rank = start_basis.shape
    block = down_weight.shape[1]
    n_z = lax.axis_size("z")
    n_t = lax.axis_size(TENSOR)
    share = tokens // n_t
    all_units = units * n_t

    block_t = down_weight.T
    x_other = lax.ppermute(hidden, "xl", SWAP)
    c_other = lax.ppermute(hidden, "c", SWAP)
    both = [lax.ppermute(x, "c", SWAP) for x in jnp.split(x_other, 4, axis=0)]
    up, down = [block_t], [block_t]
    for _ in range(n_z // 2 - 1):
        up.append(shift(up[-1], "z", 1))
        down.append(shift(down[-1], "z", -1))
    memory_term = dot(start_basis, memory, ((0,), (1,)))
    near = shift(up[-1][:, : units // 2], "z", 1)
    far = shift(down[-1][:, units // 2 :], "z", -1)
    rows = (hidden, c_other, x_other, *both)
    pieces = column_products(rows, down + up[:0:-1] + [near, far])
    pieces = pieces.reshape(4 * n_t, share, n_z * block)
    parts = lax.all_to_all(pieces, ("xl", "c") + TENSOR, 0, 0)
    parts, memory_term = lax.optimization_barrier((parts, memory_term))

    normed, sent = norm_head(parts, norm_gain, teacher, start_basis.T, tokens)
    sent = lax.all_to_all(sent, TENSOR, 0, 0)
    grad = sent[:, :, :feats].reshape(tokens, feats)
    probe = sent[:, :, feats:].reshape(tokens, rank)

    term = memory_term + dot(probe, hidden, ((0,), (0,)))
    half = sum_pair_halves(term, "c", 0)
    pieces = lax.all_to_all(half.reshape(2 * n_z, rank // (4 * n_z), units), ("xl", "z"), 0, 0)
    piece = jnp.sum(pieces, axis=0)
    left = pair(share_out(piece, ("xl", "z")).reshape(rank // 2, units), "c")

    left2 = split_bf16(left)
    gram = dot(left, left, ((1,), (1,)), lax.Precision.HIGHEST)
    image = dot(left2, hidden, ((1,), (1,)))
    image = split_bf16(image[:rank] + image[rank:])
    right = dot(image, grad, ((1,), (0,))) + dot(left2, memory, ((1,), (0,)))
    right = right[:rank] + right[rank:]

    right = sum_pair_halves(sum_pair_halves(right, "c", 0), "xl", 0)
    lines = right.shape[0] // n_t
    gram = jnp.broadcast_to(gram.reshape(1, lines, -1), (n_t, lines, rank * rank // lines))
    message = jnp.concatenate([right.reshape(n_t, lines, feats), gram], axis=2)
    message = jnp.sum(lax.all_to_all(message, TENSOR, 0, 0), axis=0)
    gram = message[:, feats:].reshape(rank, rank)
    right = jnp.sum(share_out(message[:, :feats], "z"), axis=0)
    right = share_out(right, ("c", "xl") + TENSOR).reshape(rank, feats)

    lower = jnp.linalg.cholesky(gram)
    inverse = lax.linalg.triangular_solve(lower, jnp.eye(rank, dtype=F32), left_side=True, lower=True)
    left_basis = dot(left, inverse, ((0,), (1,)), lax.Precision.HIGHEST) * math.sqrt(all_units)
    right_factor = dot(right, inverse, ((0,), (1,)), lax.Precision.HIGHEST)
    return normed, left_basis.astype(BF16), right_factor.astype(BF16)


def solution(mesh):
    fine = Mesh(mesh.devices.reshape(2, 8, 2, 4, 2), DP + TENSOR)
    in_specs = (
        P(DP, TENSOR),
        P(TENSOR, DP),
        P(),
        P(DP + TENSOR, None),
        P(DP, TENSOR, None),
        P(),
    )
    out_specs = (P(DP + TENSOR, None), P(TENSOR, None), P())
    return jax.shard_map(
        per_device, mesh=fine, in_specs=in_specs, out_specs=out_specs, check_vma=False
    )
```

time: 255 us -> 206 us (0.81)
  waiting for transfers between devices: 90 us -> 62.1 us
  other arithmetic: 28.1 us -> 12.8 us
  starting transfers between devices: 39 us -> 54 us
  between operations: 14.4 us -> 1.09 us
  Pallas kernels: 0 us -> 11.9 us
  blocking collectives: 48 us -> 39.5 us
  matrix products: 25.2 us -> 17.8 us
  local copies, waits for them, and re-layouts: 9.43 us -> 5.79 us
    ppermute x3 -> x1, waiting for transfers between devices: 29.6 us -> 1.21 us  [pair(): other = lax.ppermute(x, axis, SWAP)]
    all_gather x2 -> x0, waiting for transfers between devices: 25.1 us -> none  [the longest x1 23 us: per_device(): grad_all = lax.all_gather(grad, TENSOR, axis=0, tiled=True)]
    ppermute x2 -> x17, starting transfers between devices: 3.5 us -> 28.5 us  [the longest x8 13.8 us: shift(): return lax.ppermute(x, axis, [(i, (i + by) % n) for i in range(n)])]
    ppermute x2 -> x17, waiting for transfers between devices: 2.07 us -> 23.5 us  [the longest x8 15.9 us: shift(): return lax.ppermute(x, axis, [(i, (i + by) % n) for i in range(n)])]
    pallas_call x0 -> x2, Pallas kernels: none -> 11.9 us  [the longest x1 10 us: column_products(): pl.pallas_call(columns_kernel, out_shape=jax.ShapeDtypeStruct((4, tokens,...]
    all_to_all x1 -> x2, waiting for transfers between devices: 19.9 us -> 30.8 us  [the longest x1 18.2 us: per_device(): sent = lax.all_to_all(sent, TENSOR, 0, 0)]
    select_n x6 -> x4, other arithmetic: 10.7 us -> 0.12 us  [the longest x3 0.08 us: sum_pair_halves(): jnp.where(first, high, low)]
    all_to_all x1, blocking collectives: 20.3 us -> 10.8 us  [per_device(): message = jnp.sum(lax.all_to_all(message, TENSOR, 0, 0), axis=0)]
  transfers between devices with their start and end apart: 11 -> 22, of which waited for: 10 -> 13; matrix products, arithmetic and copies ran while one was open for 16% -> 11% of each run, Pallas kernels for 0% -> 0%
where the time goes in v2:
time: 206 us; the launch traced here: 205 us
  waiting for transfers between devices  62.1 us (30%)
  starting transfers between devices  54 us (26%)
  blocking collectives  39.5 us (19%)
  matrix products  17.8 us (9%)
  other arithmetic  12.8 us (6%)
  Pallas kernels  11.9 us (6%)
  local copies, waits for them, and re-layouts  5.79 us (3%)
    all_to_all x1, waiting for transfers between devices, per_device(): sent = lax.all_to_all(sent, TENSOR, 0, 0)  18.2 us
    dot_general x8, matrix products, dot(): lax.dot_general(a, b, (dims, ((), ())), precision=precision, preferred_el...  17.6 us
    ppermute x8, waiting for transfers between devices, shift(): return lax.ppermute(x, axis, [(i, (i + by) % n) for i in range(n)])  15.9 us
    all_to_all x1, blocking collectives, per_device(): lax.all_to_all(half.reshape(2 * n_z, rank // (4 * n_z), units), ('xl', 'z...  14.7 us
    all_to_all x1, blocking collectives, share_out(): return lax.all_to_all(jnp.broadcast_to(x[None], (n,) + x.shape), axes, 0, 0)  14.1 us
    ppermute x8, starting transfers between devices, shift(): return lax.ppermute(x, axis, [(i, (i + by) % n) for i in range(n)])  13.8 us
    all_to_all x1, waiting for transfers between devices, per_device(): parts = lax.all_to_all(pieces, ('xl', 'c') + TENSOR, 0, 0)  12.5 us
    all_to_all x2, starting transfers between devices, share_out(): return lax.all_to_all(jnp.broadcast_to(x[None], (n,) + x.shape), axes, 0, 0)  11.8 us
  transfers between devices with their start and end apart: 22, of which 13 were waited for; matrix products, arithmetic and copies ran while one was open for 11% of the time, Pallas kernels for 0%

profile of v2, /device:TPU:1, one launch (start us, length us, event | category | flops | bytes accessed | tf_op | source)
XLA Modules:
  0.0 205.1 jit_solution(2766460253943130416)
XLA Ops:
  4.4 3.9 %collective-permute-start.6 = (bf16[72,2304]{1,0:T(8,128)(2,1)}, bf16[72,2304]{1,0:T(8,128)(2,1)S(1)}, u32[]{:S(2)}, u32[]{:S(2)}) collective-permute-start(bf16[72,2304]{1,0:T(8,128)(2,1)} %bitcast.33), channel_id=1, source_target_pairs={{0,112},{16,0},{32,16},{48,32},{64,48},{80,64},{96,80},{112,96},{1... | collective-permute-start | bytes 995336 | tf_op jit(solution)/shard_map/ppermute | solution.py:48
  8.3 7.4 %collective-permute-done.9.refs_13_ = bf16[72,2304]{1,0:T(8,128)(2,1)S(1)} collective-permute-done((bf16[72,2304]{1,0:T(8,128)(2,1)}, bf16[72,2304]{1,0:T(8,128)(2,1)S(1)}, u32[]{:S(2)}, u32[]{:S(2)}) %collective-permute-start.9) | collective-permute-done | bytes 331808 | tf_op jit(solution)/shard_map/ppermute | solution.py:48
  18.4 6.3 %collective-permute-done.10.refs_12_ = bf16[72,2304]{1,0:T(8,128)(2,1)S(1)} collective-permute-done((bf16[72,2304]{1,0:T(8,128)(2,1)S(1)}, bf16[72,2304]{1,0:T(8,128)(2,1)S(1)}, u32[]{:S(2)}, u32[]{:S(2)}) %collective-permute-start.10) | collective-permute-done | bytes 331808 | tf_op jit(solution)/shard_map/ppermute | solution.py:48
  24.7 2.7 %collective-permute-start.8 = (bf16[72,2304]{1,0:T(8,128)(2,1)S(1)}, bf16[72,2304]{1,0:T(8,128)(2,1)S(1)}, u32[]{:S(2)}, u32[]{:S(2)}) collective-permute-start(bf16[72,2304]{1,0:T(8,128)(2,1)S(1)} %collective-permute-done.7.refs_9_), channel_id=1, source_target_pairs={{0,112},{16,0},{32,16},{48,32},{64,48},{80,64},{96,80},{112,96},{1... | collective-permute-start | bytes 995336 | tf_op jit(solution)/shard_map/ppermute | solution.py:48
  27.5 3.0 %collective-permute-start = (bf16[256,2304]{1,0:T(8,128)(2,1)}, bf16[256,2304]{1,0:T(8,128)(2,1)S(1)}, u32[]{:S(2)}, u32[]{:S(2)}) collective-permute-start(bf16[256,2304]{1,0:T(8,128)(2,1)} %refs_0_.1), channel_id=1, source_target_pairs={{0,8},{8,0},{1,9},{9,1},{2,10},{10,2},{3,11},{11,3},{4,12},{12,4},... | collective-permute-start | bytes 3538952 | tf_op jit(solution)/shard_map/ppermute | solution.py:157
  32.9 2.7 %collective-permute-start.13 = (bf16[72,1152]{1,0:T(8,128)(2,1)S(1)}, bf16[72,1152]{1,0:T(8,128)(2,1)S(1)}, u32[]{:S(2)}, u32[]{:S(2)}) collective-permute-start(bf16[72,1152]{1,0:T(8,128)(2,1)S(1)} %slice.51), channel_id=1, source_target_pairs={{0,112},{16,0},{32,16},{48,32},{64,48},{80,64},{96,80},{112,96},{1... | collective-permute-start | bytes 497672 | tf_op jit(solution)/shard_map/ppermute | solution.py:48
  37.0 4.0 %collective-permute-start.2 = (bf16[64,2304]{1,0:T(8,128)(2,1)}, bf16[64,2304]{1,0:T(8,128)(2,1)S(1)}, u32[]{:S(2)}, u32[]{:S(2)}) collective-permute-start(bf16[64,2304]{1,0:T(8,128)(2,1)} %get-tuple-element.14), channel_id=1, source_target_pairs={{0,8},{8,0},{1,9},{9,1},{2,10},{10,2},{3,11},{11,3},{4,12},{12,4},... | collective-permute-start | bytes 884744 | tf_op jit(solution)/shard_map/ppermute | solution.py:158
  46.0 10.0 %shard_map.85 = bf16[4,256,576]{2,1,0:T(8,128)(2,1)} custom-call(s32[1]{0:T(128)} %bitcast.1.me_ref, bf16[256,2304]{1,0:T(8,128)(2,1)} %refs_0_.1, bf16[256,2304]{1,0:T(8,128)(2,1)} %copy-done.5, bf16[256,2304]{1,0:T(8,128)(2,1)} %copy-done.4, bf16[64,2304]{1,0:T(8,128)(2,1)} %copy-done.12, bf16[64,2304]{1,0:T(8,128)(2,1)} %copy-done.13, ...), custom_call_target="tpu_custom_call" | custom-call | tf_op jit(solution)/shard_map/pallas_call | solution.py:77
  56.0 7.1 %all-to-all-start = ((bf16[32,32,576]{2,1,0:T(8,128)(2,1)}), bf16[32,32,576]{2,1,0:T(8,128)(2,1)S(1)}, u32[]{:S(2)}, u32[]{:S(2)}) async-start(bf16[32,32,576]{2,1,0:T(8,128)(2,1)} %bitcast.30), calls=%async_computation | async-start | bytes 2621440 | tf_op jit(solution)/shard_map/all_to_all | solution.py:169
  63.2 7.3 %fusion.2 = f32[64,2304]{1,0:T(8,128)S(1)} fusion(bf16[2304,64]{0,1:T(8,128)(2,1)S(1)} %copy-done, bf16[1,2304,2304]{2,1,0:T(8,128)(2,1)} %param.10), kind=kOutput, calls=%fused_computation.2 | convolution fusion | flops 679477248 | bytes 11501568 | tf_op jit(solution)/shard_map/dot_general | solution.py:20
  70.5 12.5 %all-to-all-done.parts_ref = bf16[32,32,576]{2,1,0:T(8,128)(2,1)S(1)} async-done(((bf16[32,32,576]{2,1,0:T(8,128)(2,1)}), bf16[32,32,576]{2,1,0:T(8,128)(2,1)S(1)}, u32[]{:S(2)}, u32[]{:S(2)}) %all-to-all-start) | async-done | bytes 1179680 | tf_op jit(solution)/shard_map/all_to_all | solution.py:169
  85.0 3.7 %all-to-all-start.1 = ((bf16[8,32,2368]{2,1,0:T(8,128)(2,1)}), bf16[8,32,2368]{2,1,0:T(8,128)(2,1)S(1)}, u32[]{:S(2)}, u32[]{:S(2)}) async-start(bf16[8,32,2368]{2,1,0:T(8,128)(2,1)} %get-tuple-element.10), calls=%async_computation.1 | async-start | bytes 2490368 | tf_op jit(solution)/shard_map/all_to_all | solution.py:173
  88.7 18.2 %all-to-all-done.1 = bf16[8,32,2368]{2,1,0:T(8,128)(2,1)S(1)} async-done(((bf16[8,32,2368]{2,1,0:T(8,128)(2,1)}), bf16[8,32,2368]{2,1,0:T(8,128)(2,1)S(1)}, u32[]{:S(2)}, u32[]{:S(2)}) %all-to-all-start.1) | async-done | bytes 1212448 | tf_op jit(solution)/shard_map/all_to_all | solution.py:173
  110.9 14.7 %all_to_all.35 = f32[16,2,2304]{2,1,0:T(2,128)S(1)} all-to-all(f32[16,2,2304]{2,1,0:T(2,128)S(1)} %reshape.58), channel_id=1, replica_groups=mesh['xl'=2,'z'=8,'c'=2,'y'=4,'xh'=2] {'xl','z'}, dimensions={0} | all-to-all | bytes 589824 | tf_op jit(solution)/shard_map/all_to_all | solution.py:179
  125.7 14.1 %all_to_all.36 = f32[16,2,2304]{2,1,0:T(2,128)S(1)} all-to-all(f32[16,2,2304]{2,1,0:T(2,128)S(1)} %broadcast_in_dim.11), channel_id=1, replica_groups=mesh['xl'=2,'z'=8,'c'=2,'y'=4,'xh'=2] {'xl','z'}, dimensions={0} | all-to-all | bytes 589824 | tf_op jit(solution)/shard_map/all_to_all | solution.py:31
  140.0 3.0 %collective-permute-start.15 = (f32[32,2304]{1,0:T(8,128)S(1)}, f32[32,2304]{1,0:T(8,128)S(1)}, u32[]{:S(2)}, u32[]{:S(2)}) collective-permute-start(f32[32,2304]{1,0:T(8,128)S(1)} %reshape.59), channel_id=1, source_target_pairs={{0,8},{8,0},{1,9},{9,1},{2,10},{10,2},{3,11},{11,3},{4,12},{12,4},... | collective-permute-start | bytes 884744 | tf_op jit(solution)/shard_map/ppermute | solution.py:35
  144.9 5.7 %fusion = f32[128,2304]{1,0:T(8,128)S(1)} fusion(bf16[1,2304,2304]{2,1,0:T(8,128)(2,1)} %param.10, bf16[64,2304]{1,0:T(8,128)(2,1)S(1)} %get-tuple-element.16, bf16[64,2304]{1,0:T(8,128)(2,1)S(1)} %get-tuple-element.15), kind=kOutput, calls=%fused_computation | convolution fusion | flops 1360134144 | bytes 12386304 | tf_op jit(solution)/shard_map/dot_general | solution.py:20
  154.7 3.4 %collective-permute-done.17 = f32[16,2304]{1,0:T(8,128)S(1)} collective-permute-done((f32[16,2304]{1,0:T(8,128)S(1)}, f32[16,2304]{1,0:T(8,128)S(1)}, u32[]{:S(2)}, u32[]{:S(2)}) %collective-permute-start.17) | collective-permute-done | bytes 147488 | tf_op jit(solution)/shard_map/ppermute | solution.py:43
  158.4 10.8 %all_to_all.37 = f32[8,2,4352]{2,1,0:T(2,128)S(1)} all-to-all(f32[8,2,4352]{2,1,0:T(2,128)S(1)} %pad_maximum_fusion.4), channel_id=1, replica_groups=mesh['xl'=2,'z'=8,'c'=2,'y'=4,'xh'=2] {'y','xh'}, dimensions={0} | all-to-all | bytes 557056 | tf_op jit(solution)/shard_map/all_to_all | solution.py:194
  170.0 4.1 %all-to-all-start.5 = ((f32[8,2,2304]{2,1,0:T(2,128)}), f32[8,2,2304]{2,1,0:T(2,128)S(1)}, u32[]{:S(2)}, u32[]{:S(2)}) async-start(f32[8,2,2304]{2,1,0:T(2,128)} %broadcast_in_dim.14), calls=%async_computation.5 | async-start | bytes 294912 | tf_op jit(solution)/shard_map/all_to_all | solution.py:31
  174.3 5.8 %cholesky.17 = f32[64,64]{1,0:T(8,128)S(1)} custom-call(f32[64,64]{1,0:T(8,128)S(1)} %fusion.15), custom_call_target="Cholesky" | custom-call | tf_op jit(solution)/shard_map/jit(cholesky)/cholesky | solution.py:199
  183.2 7.7 %all-to-all-start.6 = ((f32[32,2,2304]{2,1,0:T(2,128)}), f32[32,2,2304]{2,1,0:T(2,128)S(1)}, u32[]{:S(2)}, u32[]{:S(2)}) async-start(f32[32,2,2304]{2,1,0:T(2,128)} %broadcast_in_dim.15), calls=%async_computation.6 | async-start | bytes 1179648 | tf_op jit(solution)/shard_map/all_to_all | solution.py:31
  191.6 4.9 %custom-call.6 = f32[1,64,64]{1,2,0:T(8,128)S(1)} custom-call(f32[1,64,64]{2,1,0:T(8,128)S(1)} %fusion.12), custom_call_target="InvertDiagBlocksLowerTriangular" | custom-call | tf_op jit(solution)/shard_map/triangular_solve | solution.py:200
  198.1 5.2 %all-to-all-done.6 = f32[32,2,2304]{2,1,0:T(2,128)S(1)} async-done(((f32[32,2,2304]{2,1,0:T(2,128)}), f32[32,2,2304]{2,1,0:T(2,128)S(1)}, u32[]{:S(2)}, u32[]{:S(2)}) %all-to-all-start.6) | async-done | bytes 589856 | tf_op jit(solution)/shard_map/all_to_all | solution.py:31
  (112 shorter events, 35.8 us)
Async XLA Ops:
  0.6 35.0 %collective-permute-start.1 = (bf16[256,2304]{1,0:T(8,128)(2,1)}, bf16[256,2304]{1,0:T(8,128)(2,1)S(1)}, u32[]{:S(2)}, u32[]{:S(2)}) collective-permute-start(bf16[256,2304]{1,0:T(8,128)(2,1)} %refs_0_.1), channel_id=1, source_target_pairs={{0,128},{128,0},{1,129},{129,1},{2,130},{130,2},{3,131},{131,3},{4... | collective-permute-start | bytes 3538952 | tf_op jit(solution)/shard_map/ppermute | solution.py:156
  2.8 13.0 %collective-permute-start.9 = (bf16[72,2304]{1,0:T(8,128)(2,1)}, bf16[72,2304]{1,0:T(8,128)(2,1)S(1)}, u32[]{:S(2)}, u32[]{:S(2)}) collective-permute-start(bf16[72,2304]{1,0:T(8,128)(2,1)} %bitcast.32), channel_id=1, source_target_pairs={{0,16},{16,32},{32,48},{48,64},{64,80},{80,96},{96,112},{112,0},{1... | collective-permute-start | bytes 995336 | tf_op jit(solution)/shard_map/ppermute | solution.py:48
  4.4 11.4 %collective-permute-start.6 = (bf16[72,2304]{1,0:T(8,128)(2,1)}, bf16[72,2304]{1,0:T(8,128)(2,1)S(1)}, u32[]{:S(2)}, u32[]{:S(2)}) collective-permute-start(bf16[72,2304]{1,0:T(8,128)(2,1)} %bitcast.33), channel_id=1, source_target_pairs={{0,112},{16,0},{32,16},{48,32},{64,48},{80,64},{96,80},{112,96},{1... | collective-permute-start | bytes 995336 | tf_op jit(solution)/shard_map/ppermute | solution.py:48
  15.7 9.0 %collective-permute-start.10 = (bf16[72,2304]{1,0:T(8,128)(2,1)S(1)}, bf16[72,2304]{1,0:T(8,128)(2,1)S(1)}, u32[]{:S(2)}, u32[]{:S(2)}) collective-permute-start(bf16[72,2304]{1,0:T(8,128)(2,1)S(1)} %collective-permute-done.9.refs_13_), channel_id=1, source_target_pairs={{0,16},{16,32},{32,48},{48,64},{64,80},{80,96},{96,112},{112,0},{1... | collective-permute-start | bytes 995336 | tf_op jit(solution)/shard_map/ppermute | solution.py:48
  15.8 8.9 %collective-permute-start.7 = (bf16[72,2304]{1,0:T(8,128)(2,1)S(1)}, bf16[72,2304]{1,0:T(8,128)(2,1)S(1)}, u32[]{:S(2)}, u32[]{:S(2)}) collective-permute-start(bf16[72,2304]{1,0:T(8,128)(2,1)S(1)} %collective-permute-done.6.refs_8_), channel_id=1, source_target_pairs={{0,112},{16,0},{32,16},{48,32},{64,48},{80,64},{96,80},{112,96},{1... | collective-permute-start | bytes 995336 | tf_op jit(solution)/shard_map/ppermute | solution.py:48
  24.7 8.0 %collective-permute-start.11 = (bf16[72,2304]{1,0:T(8,128)(2,1)S(1)}, bf16[72,2304]{1,0:T(8,128)(2,1)S(1)}, u32[]{:S(2)}, u32[]{:S(2)}) collective-permute-start(bf16[72,2304]{1,0:T(8,128)(2,1)S(1)} %collective-permute-done.10.refs_12_), channel_id=1, source_target_pairs={{0,16},{16,32},{32,48},{48,64},{64,80},{80,96},{96,112},{112,0},{1... | collective-permute-start | bytes 995336 | tf_op jit(solution)/shard_map/ppermute | solution.py:48
  24.7 8.1 %collective-permute-start.8 = (bf16[72,2304]{1,0:T(8,128)(2,1)S(1)}, bf16[72,2304]{1,0:T(8,128)(2,1)S(1)}, u32[]{:S(2)}, u32[]{:S(2)}) collective-permute-start(bf16[72,2304]{1,0:T(8,128)(2,1)S(1)} %collective-permute-done.7.refs_9_), channel_id=1, source_target_pairs={{0,112},{16,0},{32,16},{48,32},{64,48},{80,64},{96,80},{112,96},{1... | collective-permute-start | bytes 995336 | tf_op jit(solution)/shard_map/ppermute | solution.py:48
  27.5 16.1 %collective-permute-start = (bf16[256,2304]{1,0:T(8,128)(2,1)}, bf16[256,2304]{1,0:T(8,128)(2,1)S(1)}, u32[]{:S(2)}, u32[]{:S(2)}) collective-permute-start(bf16[256,2304]{1,0:T(8,128)(2,1)} %refs_0_.1), channel_id=1, source_target_pairs={{0,8},{8,0},{1,9},{9,1},{2,10},{10,2},{3,11},{11,3},{4,12},{12,4},... | collective-permute-start | bytes 3538952 | tf_op jit(solution)/shard_map/ppermute | solution.py:157
  32.8 8.2 %collective-permute-start.12 = (bf16[72,1152]{1,0:T(8,128)(2,1)S(1)}, bf16[72,1152]{1,0:T(8,128)(2,1)S(1)}, u32[]{:S(2)}, u32[]{:S(2)}) collective-permute-start(bf16[72,1152]{1,0:T(8,128)(2,1)S(1)} %slice.50), channel_id=1, source_target_pairs={{0,16},{16,32},{32,48},{48,64},{64,80},{80,96},{96,112},{112,0},{1... | collective-permute-start | bytes 497672 | tf_op jit(solution)/shard_map/ppermute | solution.py:48
  32.9 9.9 %collective-permute-start.13 = (bf16[72,1152]{1,0:T(8,128)(2,1)S(1)}, bf16[72,1152]{1,0:T(8,128)(2,1)S(1)}, u32[]{:S(2)}, u32[]{:S(2)}) collective-permute-start(bf16[72,1152]{1,0:T(8,128)(2,1)S(1)} %slice.51), channel_id=1, source_target_pairs={{0,112},{16,0},{32,16},{48,32},{64,48},{80,64},{96,80},{112,96},{1... | collective-permute-start | bytes 497672 | tf_op jit(solution)/shard_map/ppermute | solution.py:48
  37.0 6.5 %collective-permute-start.2 = (bf16[64,2304]{1,0:T(8,128)(2,1)}, bf16[64,2304]{1,0:T(8,128)(2,1)S(1)}, u32[]{:S(2)}, u32[]{:S(2)}) collective-permute-start(bf16[64,2304]{1,0:T(8,128)(2,1)} %get-tuple-element.14), channel_id=1, source_target_pairs={{0,8},{8,0},{1,9},{9,1},{2,10},{10,2},{3,11},{11,3},{4,12},{12,4},... | collective-permute-start | bytes 884744 | tf_op jit(solution)/shard_map/ppermute | solution.py:158
  41.0 2.6 %collective-permute-start.3 = (bf16[64,2304]{1,0:T(8,128)(2,1)}, bf16[64,2304]{1,0:T(8,128)(2,1)S(1)}, u32[]{:S(2)}, u32[]{:S(2)}) collective-permute-start(bf16[64,2304]{1,0:T(8,128)(2,1)} %get-tuple-element.13), channel_id=1, source_target_pairs={{0,8},{8,0},{1,9},{9,1},{2,10},{10,2},{3,11},{11,3},{4,12},{12,4},... | collective-permute-start | bytes 884744 | tf_op jit(solution)/shard_map/ppermute | solution.py:158
  41.0 3.2 %collective-permute-start.4 = (bf16[64,2304]{1,0:T(8,128)(2,1)}, bf16[64,2304]{1,0:T(8,128)(2,1)S(1)}, u32[]{:S(2)}, u32[]{:S(2)}) collective-permute-start(bf16[64,2304]{1,0:T(8,128)(2,1)} %get-tuple-element.12), channel_id=1, source_target_pairs={{0,8},{8,0},{1,9},{9,1},{2,10},{10,2},{3,11},{11,3},{4,12},{12,4},... | collective-permute-start | bytes 884744 | tf_op jit(solution)/shard_map/ppermute | solution.py:158
  43.5 1.8 collective-permute-start.5
  56.0 27.0 %all-to-all-start = ((bf16[32,32,576]{2,1,0:T(8,128)(2,1)}), bf16[32,32,576]{2,1,0:T(8,128)(2,1)S(1)}, u32[]{:S(2)}, u32[]{:S(2)}) async-start(bf16[32,32,576]{2,1,0:T(8,128)(2,1)} %bitcast.30), calls=%async_computation | async-start | bytes 2621440 | tf_op jit(solution)/shard_map/all_to_all | solution.py:169
  85.0 22.0 %copy-start.3 = (bf16[256,2304]{1,0:T(8,128)(2,1)S(1)}, bf16[256,2304]{1,0:T(8,128)(2,1)}, u32[]{:S(2)}) copy-start(bf16[256,2304]{1,0:T(8,128)(2,1)} %refs_0_.1) | copy-start | bytes 3538948
  85.0 22.0 %all-to-all-start.1 = ((bf16[8,32,2368]{2,1,0:T(8,128)(2,1)}), bf16[8,32,2368]{2,1,0:T(8,128)(2,1)S(1)}, u32[]{:S(2)}, u32[]{:S(2)}) async-start(bf16[8,32,2368]{2,1,0:T(8,128)(2,1)} %get-tuple-element.10), calls=%async_computation.1 | async-start | bytes 2490368 | tf_op jit(solution)/shard_map/all_to_all | solution.py:173
  107.0 36.0 %copy-start.2 = (bf16[8,32,2368]{2,1,0:T(8,128)(2,1)}, bf16[8,32,2368]{2,1,0:T(8,128)(2,1)S(1)}, u32[]{:S(2)}) copy-start(bf16[8,32,2368]{2,1,0:T(8,128)(2,1)S(1)} %all-to-all-done.1) | copy-start | bytes 3637252
  107.4 3.3 %collective-permute-start.14 = (f32[32,2304]{1,0:T(8,128)S(1)}, f32[32,2304]{1,0:T(8,128)S(1)}, u32[]{:S(2)}, u32[]{:S(2)}) collective-permute-start(f32[32,2304]{1,0:T(8,128)S(1)} %slice_select_fusion.1), channel_id=1, source_target_pairs={{0,8},{8,0},{1,9},{9,1},{2,10},{10,2},{3,11},{11,3},{4,12},{12,4},... | collective-permute-start | bytes 884744 | tf_op jit(solution)/shard_map/ppermute | solution.py:43
  140.0 4.2 %collective-permute-start.15 = (f32[32,2304]{1,0:T(8,128)S(1)}, f32[32,2304]{1,0:T(8,128)S(1)}, u32[]{:S(2)}, u32[]{:S(2)}) collective-permute-start(f32[32,2304]{1,0:T(8,128)S(1)} %reshape.59), channel_id=1, source_target_pairs={{0,8},{8,0},{1,9},{9,1},{2,10},{10,2},{3,11},{11,3},{4,12},{12,4},... | collective-permute-start | bytes 884744 | tf_op jit(solution)/shard_map/ppermute | solution.py:35
  151.0 1.7 collective-permute-start.16
  152.8 5.4 %collective-permute-start.17 = (f32[16,2304]{1,0:T(8,128)S(1)}, f32[16,2304]{1,0:T(8,128)S(1)}, u32[]{:S(2)}, u32[]{:S(2)}) collective-permute-start(f32[16,2304]{1,0:T(8,128)S(1)} %slice_select_fusion.2), channel_id=1, source_target_pairs={{0,128},{128,0},{1,129},{129,1},{2,130},{130,2},{3,131},{131,3},{4... | collective-permute-start | bytes 442376 | tf_op jit(solution)/shard_map/ppermute | solution.py:43
  170.0 12.2 %all-to-all-start.5 = ((f32[8,2,2304]{2,1,0:T(2,128)}), f32[8,2,2304]{2,1,0:T(2,128)S(1)}, u32[]{:S(2)}, u32[]{:S(2)}) async-start(f32[8,2,2304]{2,1,0:T(2,128)} %broadcast_in_dim.14), calls=%async_computation.5 | async-start | bytes 294912 | tf_op jit(solution)/shard_map/all_to_all | solution.py:31
  183.2 20.1 %all-to-all-start.6 = ((f32[32,2,2304]{2,1,0:T(2,128)}), f32[32,2,2304]{2,1,0:T(2,128)S(1)}, u32[]{:S(2)}, u32[]{:S(2)}) async-start(f32[32,2,2304]{2,1,0:T(2,128)} %broadcast_in_dim.15), calls=%async_computation.6 | async-start | bytes 1179648 | tf_op jit(solution)/shard_map/all_to_all | solution.py:31
  (18 other events, 101.9 us)

commit v3 on v2

v3 whole, which is shorter than its diff:
```python
import functools
import math

import jax
import jax.numpy as jnp
from jax import lax
from jax.experimental import pallas as pl
from jax.experimental.pallas import tpu as pltpu
from jax.sharding import Mesh
from jax.sharding import PartitionSpec as P

DP = ("xl", "z", "c")
TENSOR = ("y", "xh")
SWAP = [(0, 1), (1, 0)]
F32 = jnp.float32
BF16 = jnp.bfloat16


def dot(a, b, dims, precision=None):
    return lax.dot_general(a, b, (dims, ((), ())), precision=precision, preferred_element_type=F32)


def split_bf16(x):
    high = lax.reduce_precision(x, 8, 7)
    low = x - high
    return jnp.concatenate([high.astype(BF16), low.astype(BF16)], axis=0)


def share_out(x, axes):
    n = lax.axis_size(axes)
    return lax.all_to_all(jnp.broadcast_to(x[None], (n,) + x.shape), axes, 0, 0)


def pair(x, axis):
    other = lax.ppermute(x, axis, SWAP)
    first = lax.axis_index(axis) == 0
    return jnp.concatenate([jnp.where(first, x, other), jnp.where(first, other, x)], axis=0)


def sum_pair_halves(x, axis, dim):
    low, high = jnp.split(x, 2, axis=dim)
    first = lax.axis_index(axis) == 0
    return jnp.where(first, low, high) + lax.ppermute(jnp.where(first, high, low), axis, SWAP)


def shift(x, axis, by):
    n = lax.axis_size(axis)
    return lax.ppermute(x, axis, [(i, (i + by) % n) for i in range(n)])


def ring_order(n_z):
    return [k for far in range(1, n_z // 2) for k in (far, n_z - far)] + [0, n_z // 2]


def pack_kernel(*refs):
    *blocks, out_ref = refs
    block = blocks[0].shape[0]
    for k, ref in enumerate(blocks):
        out_ref[k * block : (k + 1) * block, :] = ref[...]


def pack(blocks):
    block, units = blocks[0].shape
    vmem = pl.BlockSpec(memory_space=pltpu.VMEM)
    return pl.pallas_call(
        pack_kernel,
        out_shape=jax.ShapeDtypeStruct((len(blocks) * block, units), BF16),
        in_specs=[vmem] * len(blocks),
        out_specs=vmem,
        compiler_params=pltpu.CompilerParams(vmem_limit_bytes=16 * 2**20),
        cost_estimate=pl.CostEstimate(flops=0, bytes_accessed=4 * len(blocks) * block * units, transcendentals=0),
    )(*blocks)


def columns_kernel(me_ref, own_ref, c_ref, columns_ref, *refs):
    *sources, out_ref, x_rows, both_rows, rest, last, products, sems, out_sems = refs
    width = columns_ref.shape[0]
    tokens, units = own_ref.shape
    block = last.shape[0] // 2
    top, bottom = pl.ds(0, tokens // 2), pl.ds(tokens // 2, tokens // 2)
    left, right = pl.ds(0, units // 2), pl.ds(units // 2, units // 2)
    targets = [rest.at[0], rest.at[1, :, left], rest.at[1, :, right]]
    targets += [x_rows, both_rows.at[top, :], both_rows.at[bottom, :]]
    brought = [pltpu.make_async_copy(x, y, sems.at[k]) for k, (x, y) in enumerate(zip(sources, targets))]
    for copy in brought:
        copy.start()
    sent = []

    def main(k, ref):
        products[k, :, :width] = dot(ref[...], columns_ref[...], ((1,), (1,))).astype(BF16)

    def finish(k, ref):
        products[k, :, width:] = dot(ref[...], last[...], ((1,), (1,))).astype(BF16)
        sent.append(pltpu.make_async_copy(products.at[k], out_ref.at[me_ref[0] ^ k], out_sems.at[k]))
        sent[-1].start()

    main(0, own_ref)
    for copy in brought[:3]:
        copy.wait()
    last[:block, :] = rest[0]
    last[block:, :] = rest[1]
    finish(0, own_ref)
    main(1, c_ref)
    finish(1, c_ref)
    brought[3].wait()
    main(2, x_rows)
    finish(2, x_rows)
    for copy in brought[4:]:
        copy.wait()
    main(3, both_rows)
    finish(3, both_rows)
    for copy in sent:
        copy.wait()


def column_products(rows, columns, rest, halves):
    tokens, units = rows[0].shape
    block = rest[0].shape[0]
    me = 2 * lax.axis_index("xl") + lax.axis_index("c")
    out = jax.ShapeDtypeStruct((4, tokens, columns.shape[0] + 2 * block), BF16)
    vmem = pl.BlockSpec(memory_space=pltpu.VMEM)
    hbm = pl.BlockSpec(memory_space=pltpu.HBM)
    return pl.pallas_call(
        columns_kernel,
        out_shape=out,
        in_specs=[pl.BlockSpec(memory_space=pltpu.SMEM)] + [vmem] * 3 + [hbm] * 6,
        out_specs=hbm,
        scratch_shapes=[
            pltpu.VMEM((tokens, units), BF16),
            pltpu.VMEM((tokens, units), BF16),
            pltpu.VMEM((2, block, units), BF16),
            pltpu.VMEM((2 * block, units), BF16),
            pltpu.VMEM(out.shape, BF16),
            pltpu.SemaphoreType.DMA((6,)),
            pltpu.SemaphoreType.DMA((4,)),
        ],
        compiler_params=pltpu.CompilerParams(vmem_limit_bytes=24 * 2**20),
    )(me.reshape(1), *rows, columns, *rest, *halves)


def norm_kernel(z_ref, parts_ref, gain_ref, teacher_ref, basis_ref, normed_ref, grad_ref, sent_ref, blocks, mixed_ref, *, tokens):
    n_z, _, _, two = blocks.shape
    block = two // 2
    share, feats = mixed_ref.shape
    n_t = parts_ref.shape[0] // 4
    for x in range(2):
        for c in range(2):
            total = jnp.zeros((share, n_z * block), F32)
            for t in range(n_t):
                total += parts_ref[(2 * x + c) * n_t + t].astype(F32)
            for at, k in enumerate(ring_order(n_z)):
                blocks[k, x, :, c * block : (c + 1) * block] = total[:, at * block : (at + 1) * block]
    for x in range(2):
        for z in range(n_z):
            at = (x * n_z + z) * two
            mixed_ref[:, at : at + two] = blocks[lax.rem(z - z_ref[0] + n_z, n_z), x]
    mixed = mixed_ref[...]
    gain = gain_ref[...]
    scale = lax.rsqrt(jnp.mean(mixed * mixed, axis=1, keepdims=True) + 1e-06)
    unit = mixed * scale
    normed_full = unit * gain
    normed_ref[...] = normed_full.astype(BF16)
    delta = (normed_full - teacher_ref[...].astype(F32)) * (gain / tokens)
    grad = (scale * (delta - unit * jnp.mean(delta * unit, axis=1, keepdims=True))).astype(BF16)
    grad_ref[...] = grad
    probe = dot(grad, basis_ref[...], ((1,), (1,))).astype(BF16)
    for t in range(n_t):
        sent_ref[t] = probe


def norm_head(parts, norm_gain, teacher, basis_t, tokens):
    share, feats = teacher.shape
    n_z = lax.axis_size("z")
    n_t = parts.shape[0] // 4
    vmem = pl.BlockSpec(memory_space=pltpu.VMEM)
    return pl.pallas_call(
        functools.partial(norm_kernel, tokens=tokens),
        out_shape=(
            jax.ShapeDtypeStruct((share, feats), BF16),
            jax.ShapeDtypeStruct((share, feats), BF16),
            jax.ShapeDtypeStruct((n_t, share, basis_t.shape[0]), BF16),
        ),
        in_specs=[pl.BlockSpec(memory_space=pltpu.SMEM)] + [vmem] * 4,
        out_specs=(vmem, vmem, vmem),
        scratch_shapes=[
            pltpu.VMEM((n_z, 2, share, feats // (2 * n_z)), F32),
            pltpu.VMEM((share, feats), F32),
        ],
        compiler_params=pltpu.CompilerParams(vmem_limit_bytes=32 * 2**20),
    )(lax.axis_index("z").reshape(1), parts, norm_gain.reshape(1, feats), teacher, basis_t)


def per_device(hidden, down_weight, norm_gain, teacher, error_memory, start_basis):
    memory = error_memory[0]
    tokens, units = hidden.shape
    feats, rank = start_basis.shape
    block = down_weight.shape[1]
    n_z = lax.axis_size("z")
    n_t = lax.axis_size(TENSOR)
    share = tokens // n_t
    all_units = units * n_t

    block_t = down_weight.T
    x_other = lax.ppermute(hidden, "xl", SWAP)
    c_other = lax.ppermute(hidden, "c", SWAP)
    both = [lax.ppermute(x, "c", SWAP) for x in jnp.split(x_other, 2, axis=0)]
    up, down = [block_t], [block_t]
    for _ in range(n_z // 2 - 1):
        up.append(shift(up[-1], "z", 1))
        down.append(shift(down[-1], "z", -1))
    columns = pack([down[k] if k < n_z // 2 else up[n_z - k] for k in ring_order(n_z)[:-2]])
    near = shift(columns[-block:, : units // 2], "z", 1)
    far = shift(columns[-2 * block : -block, units // 2 :], "z", -1)
    memory_term = dot(start_basis, memory, ((0,), (1,)))
    pieces = column_products((hidden, c_other), columns, (block_t, near, far), [x_other] + both)
    pieces = pieces.reshape(4 * n_t, share, n_z * block)
    parts = lax.all_to_all(pieces, ("xl", "c") + TENSOR, 0, 0)
    parts, memory_term = lax.optimization_barrier((parts, memory_term))

    wide_basis = jnp.pad(start_basis.T, ((0, -rank % 128), (0, 0)))
    normed, grad, probe = norm_head(parts, norm_gain, teacher, wide_basis, tokens)
    probe = lax.all_to_all(probe, TENSOR, 0, 0).reshape(tokens, -1)[:, :rank]

    term = memory_term + dot(probe, hidden, ((0,), (0,)))
    half = sum_pair_halves(term, "c", 0)
    pieces = lax.all_to_all(half.reshape(2 * n_z, -1, units), ("xl", "z"), 0, 0)
    left = pair(share_out(jnp.sum(pieces, axis=0), ("xl", "z")).reshape(half.shape), "c")

    left2 = split_bf16(left)
    gram = dot(left, left, ((1,), (1,)), lax.Precision.HIGHEST)
    image = dot(hidden, left2, ((1,), (1,)))
    image = (image[:, :rank] + image[:, rank:]).reshape(n_t, share, rank)
    message = jnp.concatenate([image, jnp.broadcast_to(gram[None], (n_t, rank, rank))], axis=1)
    message = jnp.sum(lax.all_to_all(message, TENSOR, 0, 0), axis=0)
    image = split_bf16(message[:share].T)
    gram = message[share:]
    pulled = dot(left2, memory, ((1,), (0,)))
    right = dot(image, grad, ((1,), (0,))) + pulled
    right = right[:rank] + right[rank:]

    half = sum_pair_halves(right, "c", 0)
    pieces = lax.all_to_all(half.reshape(2 * n_t, -1, feats), ("xl",) + TENSOR, 0, 0)
    lower = lax.linalg.cholesky(gram, symmetrize_input=False)
    pieces = share_out(jnp.sum(pieces, axis=0), "z")
    inverse = lax.linalg.triangular_solve(lower, jnp.eye(rank, dtype=F32), left_side=True, lower=True)
    left_basis = dot(left, inverse, ((0,), (1,)), lax.Precision.HIGHEST) * math.sqrt(all_units)
    left_basis = left_basis.astype(BF16)
    half = share_out(jnp.sum(pieces, axis=0), ("xl",) + TENSOR).reshape(half.shape)
    right_factor = dot(pair(half, "c"), inverse, ((0,), (1,)), lax.Precision.HIGHEST)
    return normed, left_basis, right_factor.astype(BF16)


def solution(mesh):
    fine = Mesh(mesh.devices.reshape(2, 8, 2, 4, 2), DP + TENSOR)
    in_specs = (
        P(DP, TENSOR),
        P(TENSOR, DP),
        P(),
        P(DP + TENSOR, None),
        P(DP, TENSOR, None),
        P(),
    )
    out_specs = (P(DP + TENSOR, None), P(TENSOR, None), P())
    return jax.shard_map(
        per_device, mesh=fine, in_specs=in_specs, out_specs=out_specs, check_vma=False
    )
```

time: 206 us -> 196 us (0.951)
  waiting for transfers between devices: 62.1 us -> 48.1 us
  starting transfers between devices: 54 us -> 57.7 us
  Pallas kernels: 11.9 us -> 9.37 us
    all_to_all x1 -> x2, waiting for transfers between devices: 18.2 us -> 9.51 us  [the longest x1 6.62 us: per_device(): probe = lax.all_to_all(probe, TENSOR, 0, 0).reshape(tokens, -1)[:, :rank]]
    ppermute x1 -> x2, starting transfers between devices: 2.96 us -> 7.46 us  [pair(): other = lax.ppermute(x, axis, SWAP)]
    all_to_all x2, starting transfers between devices: 11.8 us -> 7.27 us  [share_out(): return lax.all_to_all(jnp.broadcast_to(x[None], (n,) + x.shape), axes, 0, 0)]
    ppermute x8, waiting for transfers between devices: 15.9 us -> 19.9 us  [shift(): return lax.ppermute(x, axis, [(i, (i + by) % n) for i in range(n)])]
    ppermute x3 -> x2, waiting for transfers between devices: 5.86 us -> 2.42 us  [sum_pair_halves(): lax.ppermute(jnp.where(first, high, low), axis, SWAP)]
    all_to_all x2, waiting for transfers between devices: 6.63 us -> 3.5 us  [share_out(): return lax.all_to_all(jnp.broadcast_to(x[None], (n,) + x.shape), axes, 0, 0)]
    all_to_all x1 -> x2, starting transfers between devices: 3.7 us -> 6.76 us  [the longest x1 3.41 us: per_device(): message = jnp.sum(lax.all_to_all(message, TENSOR, 0, 0), axis=0)]
    pallas_call x1 -> x2, Pallas kernels: 10 us -> 7.78 us  [the longest x1 7.65 us: column_products(): pl.pallas_call(columns_kernel, out_shape=out, in_specs=[pl.BlockSpec(memo...]
  transfers between devices with their start and end apart: 22 -> 21, of which waited for: 13 -> 13; matrix products, arithmetic and copies ran while one was open for 11% -> 15% of each run, Pallas kernels for 0% -> 0%
where the time goes in v3:
time: 196 us; the launch traced here: 195 us
  starting transfers between devices  57.7 us (29%)
  waiting for transfers between devices  48.1 us (25%)
  blocking collectives  38.8 us (20%)
  matrix products  19.8 us (10%)
  other arithmetic  13.6 us (7%)
  Pallas kernels  9.37 us (5%)
  local copies, waits for them, and re-layouts  6.28 us (3%)
    ppermute x8, waiting for transfers between devices, shift(): return lax.ppermute(x, axis, [(i, (i + by) % n) for i in range(n)])  19.9 us
    dot_general x8, matrix products, dot(): lax.dot_general(a, b, (dims, ((), ())), precision=precision, preferred_el...  19.6 us
    ppermute x8, starting transfers between devices, shift(): return lax.ppermute(x, axis, [(i, (i + by) % n) for i in range(n)])  15 us
    all_to_all x1, blocking collectives, share_out(): return lax.all_to_all(jnp.broadcast_to(x[None], (n,) + x.shape), axes, 0, 0)  14.1 us
    all_to_all x1, blocking collectives, per_device(): pieces = lax.all_to_all(half.reshape(2 * n_z, -1, units), ('xl', 'z'), 0, 0)  13.4 us
    all_to_all x1, waiting for transfers between devices, per_device(): parts = lax.all_to_all(pieces, ('xl', 'c') + TENSOR, 0, 0)  11.5 us
    all_to_all x1, blocking collectives, per_device(): lax.all_to_all(half.reshape(2 * n_t, -1, feats), ('xl',) + TENSOR, 0, 0)  11.3 us
    all_to_all x1, starting transfers between devices, per_device(): parts = lax.all_to_all(pieces, ('xl', 'c') + TENSOR, 0, 0)  8.28 us
  transfers between devices with their start and end apart: 21, of which 13 were waited for; matrix products, arithmetic and copies ran while one was open for 15% of the time, Pallas kernels for 0%

profile of v3, /device:TPU:1, one launch (start us, length us, event | category | flops | bytes accessed | tf_op | source)
XLA Modules:
  0.0 194.7 jit_solution(11506721100986607488)
XLA Ops:
  2.8 5.6 %collective-permute-start.1 = (bf16[72,2304]{1,0:T(8,128)(2,1)}, bf16[72,2304]{1,0:T(8,128)(2,1)S(1)}, u32[]{:S(2)}, u32[]{:S(2)}) collective-permute-start(bf16[72,2304]{1,0:T(8,128)(2,1)} %bitcast.29), channel_id=1, source_target_pairs={{0,112},{16,0},{32,16},{48,32},{64,48},{80,64},{96,80},{112,96},{1... | collective-permute-start | bytes 995336 | tf_op jit(solution)/shard_map/ppermute | solution.py:48
  8.3 6.5 %collective-permute-done.1.refs_0_ = bf16[72,2304]{1,0:T(8,128)(2,1)S(1)} collective-permute-done((bf16[72,2304]{1,0:T(8,128)(2,1)}, bf16[72,2304]{1,0:T(8,128)(2,1)S(1)}, u32[]{:S(2)}, u32[]{:S(2)}) %collective-permute-start.1) | collective-permute-done | bytes 331808 | tf_op jit(solution)/shard_map/ppermute | solution.py:48
  14.8 3.3 %collective-permute-start.3 = (bf16[72,2304]{1,0:T(8,128)(2,1)S(1)}, bf16[72,2304]{1,0:T(8,128)(2,1)S(1)}, u32[]{:S(2)}, u32[]{:S(2)}) collective-permute-start(bf16[72,2304]{1,0:T(8,128)(2,1)S(1)} %collective-permute-done.1.refs_0_), channel_id=1, source_target_pairs={{0,112},{16,0},{32,16},{48,32},{64,48},{80,64},{96,80},{112,96},{1... | collective-permute-start | bytes 995336 | tf_op jit(solution)/shard_map/ppermute | solution.py:48
  18.1 5.2 %collective-permute-done.3.refs_2_ = bf16[72,2304]{1,0:T(8,128)(2,1)S(1)} collective-permute-done((bf16[72,2304]{1,0:T(8,128)(2,1)S(1)}, bf16[72,2304]{1,0:T(8,128)(2,1)S(1)}, u32[]{:S(2)}, u32[]{:S(2)}) %collective-permute-start.3) | collective-permute-done | bytes 331808 | tf_op jit(solution)/shard_map/ppermute | solution.py:48
  23.3 3.4 %collective-permute-start.5 = (bf16[72,2304]{1,0:T(8,128)(2,1)S(1)}, bf16[72,2304]{1,0:T(8,128)(2,1)S(1)}, u32[]{:S(2)}, u32[]{:S(2)}) collective-permute-start(bf16[72,2304]{1,0:T(8,128)(2,1)S(1)} %collective-permute-done.3.refs_2_), channel_id=1, source_target_pairs={{0,112},{16,0},{32,16},{48,32},{64,48},{80,64},{96,80},{112,96},{1... | collective-permute-start | bytes 995336 | tf_op jit(solution)/shard_map/ppermute | solution.py:48
  26.7 3.1 %collective-permute-start = (bf16[256,2304]{1,0:T(8,128)(2,1)}, bf16[256,2304]{1,0:T(8,128)(2,1)}, u32[]{:S(2)}, u32[]{:S(2)}) collective-permute-start(bf16[256,2304]{1,0:T(8,128)(2,1)} %own_ref.1), channel_id=1, source_target_pairs={{0,8},{8,0},{1,9},{9,1},{2,10},{10,2},{3,11},{11,3},{4,12},{12,4},... | collective-permute-start | bytes 3538952 | tf_op jit(solution)/shard_map/ppermute | solution.py:205
  35.5 4.2 %collective-permute-start.10 = (bf16[128,2304]{1,0:T(8,128)(2,1)}, bf16[128,2304]{1,0:T(8,128)(2,1)}, u32[]{:S(2)}, u32[]{:S(2)}) collective-permute-start(bf16[128,2304]{1,0:T(8,128)(2,1)} %get-tuple-element.16), channel_id=1, source_target_pairs={{0,8},{8,0},{1,9},{9,1},{2,10},{10,2},{3,11},{11,3},{4,12},{12,4},... | collective-permute-start | bytes 1769480 | tf_op jit(solution)/shard_map/ppermute | solution.py:206
  43.2 4.1 %collective-permute-done.7.refs_1_ = bf16[72,1152]{1,0:T(8,128)(2,1)} collective-permute-done((bf16[72,1152]{1,0:T(8,128)(2,1)}, bf16[72,1152]{1,0:T(8,128)(2,1)}, u32[]{:S(2)}, u32[]{:S(2)}) %collective-permute-start.7) | collective-permute-done | bytes 165920 | tf_op jit(solution)/shard_map/ppermute | solution.py:48
  48.7 7.7 %shard_map.86 = bf16[4,256,576]{2,1,0:T(8,128)(2,1)} custom-call(s32[1]{0:T(128)} %bitcast.1.me_ref, bf16[256,2304]{1,0:T(8,128)(2,1)S(1)} %copy-done, bf16[256,2304]{1,0:T(8,128)(2,1)} %collective-permute-done.c_ref, bf16[432,2304]{1,0:T(8,128)(2,1)S(1)} %shard_map.85.columns_ref, bf16[72,2304]{1,0:T(8,128)(2,1)S(1)} %bitcast.31, ...), custom_call_target="tpu_custom_call" | custom-call | tf_op jit(solution)/shard_map/pallas_call | solution.py:123
  56.3 8.3 %all-to-all-start = ((bf16[32,32,576]{2,1,0:T(8,128)(2,1)}), bf16[32,32,576]{2,1,0:T(8,128)(2,1)S(1)}, u32[]{:S(2)}, u32[]{:S(2)}) async-start(bf16[32,32,576]{2,1,0:T(8,128)(2,1)} %bitcast.3), calls=%async_computation | async-start | bytes 2621440 | tf_op jit(solution)/shard_map/all_to_all | solution.py:217
  64.7 8.3 %fusion.2 = f32[64,2304]{1,0:T(8,128)} fusion(bf16[2304,64]{0,1:T(8,128)(2,1)} %param.11, bf16[1,2304,2304]{2,1,0:T(8,128)(2,1)} %param.10), kind=kOutput, calls=%fused_computation.2 | convolution fusion | flops 679477248 | bytes 11501568 | tf_op jit(solution)/shard_map/dot_general | solution.py:20
  73.0 11.5 %all-to-all-done.parts_ref = bf16[32,32,576]{2,1,0:T(8,128)(2,1)S(1)} async-done(((bf16[32,32,576]{2,1,0:T(8,128)(2,1)}), bf16[32,32,576]{2,1,0:T(8,128)(2,1)S(1)}, u32[]{:S(2)}, u32[]{:S(2)}) %all-to-all-start) | async-done | bytes 1179680 | tf_op jit(solution)/shard_map/all_to_all | solution.py:217
  86.2 3.4 %all-to-all-start.1 = ((bf16[8,32,128]{2,1,0:T(8,128)(2,1)}), bf16[8,32,128]{2,1,0:T(8,128)(2,1)S(1)}, u32[]{:S(2)}, u32[]{:S(2)}) async-start(bf16[8,32,128]{2,1,0:T(8,128)(2,1)} %get-tuple-element.11), calls=%async_computation.1 | async-start | bytes 131072 | tf_op jit(solution)/shard_map/all_to_all | solution.py:222
  89.5 6.6 %all-to-all-done.1 = bf16[8,32,128]{2,1,0:T(8,128)(2,1)S(1)} async-done(((bf16[8,32,128]{2,1,0:T(8,128)(2,1)}), bf16[8,32,128]{2,1,0:T(8,128)(2,1)S(1)}, u32[]{:S(2)}, u32[]{:S(2)}) %all-to-all-start.1) | async-done | bytes 65568 | tf_op jit(solution)/shard_map/all_to_all | solution.py:222
  101.3 13.4 %all_to_all.40 = f32[16,2,2304]{2,1,0:T(2,128)S(1)} all-to-all(f32[16,2,2304]{2,1,0:T(2,128)S(1)} %reshape.53), channel_id=1, replica_groups=mesh['xl'=2,'z'=8,'c'=2,'y'=4,'xh'=2] {'xl','z'}, dimensions={0} | all-to-all | bytes 589824 | tf_op jit(solution)/shard_map/all_to_all | solution.py:226
  114.9 14.1 %all_to_all.41 = f32[16,2,2304]{2,1,0:T(2,128)S(1)} all-to-all(f32[16,2,2304]{2,1,0:T(2,128)S(1)} %broadcast_in_dim.8), channel_id=1, replica_groups=mesh['xl'=2,'z'=8,'c'=2,'y'=4,'xh'=2] {'xl','z'}, dimensions={0} | all-to-all | bytes 589824 | tf_op jit(solution)/shard_map/all_to_all | solution.py:31
  135.7 3.4 %all-to-all-start.4 = ((f32[8,96,64]{1,2,0:T(8,128)}), f32[8,96,64]{1,2,0:T(8,128)S(1)}, u32[]{:S(2)}, u32[]{:S(2)}) async-start(f32[8,96,64]{1,2,0:T(8,128)} %pad_maximum_fusion.6), calls=%async_computation.4 | async-start | bytes 524288 | tf_op jit(solution)/shard_map/all_to_all | solution.py:234
  139.2 5.6 %fusion = f32[128,2304]{1,0:T(8,128)S(1)} fusion(bf16[1,2304,2304]{2,1,0:T(8,128)(2,1)} %param.10, bf16[64,2304]{1,0:T(8,128)(2,1)S(1)} %get-tuple-element.20, bf16[64,2304]{1,0:T(8,128)(2,1)S(1)} %get-tuple-element.19), kind=kOutput, calls=%fused_computation | convolution fusion | flops 1360134144 | bytes 12386304 | tf_op jit(solution)/shard_map/dot_general | solution.py:20
  151.0 11.3 %all_to_all.42 = f32[16,2,2304]{2,1,0:T(2,128)S(1)} all-to-all(f32[16,2,2304]{2,1,0:T(2,128)S(1)} %reshape.56), channel_id=1, replica_groups=mesh['xl'=2,'z'=8,'c'=2,'y'=4,'xh'=2] {'xl','y','xh'}, dimensions={0} | all-to-all | bytes 589824 | tf_op jit(solution)/shard_map/all_to_all | solution.py:242
  163.1 3.7 %all-to-all-start.6 = ((f32[8,2,2304]{2,1,0:T(2,128)}), f32[8,2,2304]{2,1,0:T(2,128)S(1)}, u32[]{:S(2)}, u32[]{:S(2)}) async-start(f32[8,2,2304]{2,1,0:T(2,128)} %broadcast_in_dim.10), calls=%async_computation.6 | async-start | bytes 294912 | tf_op jit(solution)/shard_map/all_to_all | solution.py:31
  167.0 5.9 %cholesky.19 = f32[64,64]{1,0:T(8,128)S(1)} custom-call(f32[64,64]{1,0:T(8,128)S(1)} %copy.45), custom_call_target="Cholesky" | custom-call | tf_op jit(solution)/shard_map/cholesky | solution.py:243
  175.9 3.5 %all-to-all-start.7 = ((f32[16,2,2304]{2,1,0:T(2,128)}), f32[16,2,2304]{2,1,0:T(2,128)S(1)}, u32[]{:S(2)}, u32[]{:S(2)}) async-start(f32[16,2,2304]{2,1,0:T(2,128)} %broadcast_in_dim.11), calls=%async_computation.7 | async-start | bytes 589824 | tf_op jit(solution)/shard_map/all_to_all | solution.py:31
  180.7 4.9 %custom-call.5 = f32[1,64,64]{1,2,0:T(8,128)S(1)} custom-call(f32[1,64,64]{2,1,0:T(8,128)S(1)} %fusion.11), custom_call_target="InvertDiagBlocksLowerTriangular" | custom-call | tf_op jit(solution)/shard_map/triangular_solve | solution.py:245
  187.2 4.5 %collective-permute-start.15 = (f32[32,2304]{1,0:T(8,128)S(1)}, f32[32,2304]{1,0:T(8,128)S(1)}, u32[]{:S(2)}, u32[]{:S(2)}) collective-permute-start(f32[32,2304]{1,0:T(8,128)S(1)} %reshape.57), channel_id=1, source_target_pairs={{0,8},{8,0},{1,9},{9,1},{2,10},{10,2},{3,11},{11,3},{4,12},{12,4},... | collective-permute-start | bytes 884744 | tf_op jit(solution)/shard_map/ppermute | solution.py:35
  (84 shorter events, 42.3 us)
Async XLA Ops:
  0.6 33.5 %collective-permute-start.9 = (bf16[256,2304]{1,0:T(8,128)(2,1)}, bf16[256,2304]{1,0:T(8,128)(2,1)S(1)}, u32[]{:S(2)}, u32[]{:S(2)}) collective-permute-start(bf16[256,2304]{1,0:T(8,128)(2,1)} %own_ref.1), channel_id=1, source_target_pairs={{0,128},{128,0},{1,129},{129,1},{2,130},{130,2},{3,131},{131,3},{4... | collective-permute-start | bytes 3538952 | tf_op jit(solution)/shard_map/ppermute | solution.py:204
  2.8 12.0 %collective-permute-start.1 = (bf16[72,2304]{1,0:T(8,128)(2,1)}, bf16[72,2304]{1,0:T(8,128)(2,1)S(1)}, u32[]{:S(2)}, u32[]{:S(2)}) collective-permute-start(bf16[72,2304]{1,0:T(8,128)(2,1)} %bitcast.29), channel_id=1, source_target_pairs={{0,112},{16,0},{32,16},{48,32},{64,48},{80,64},{96,80},{112,96},{1... | collective-permute-start | bytes 995336 | tf_op jit(solution)/shard_map/ppermute | solution.py:48
  8.3 9.8 %collective-permute-start.2 = (bf16[72,2304]{1,0:T(8,128)(2,1)}, bf16[72,2304]{1,0:T(8,128)(2,1)S(1)}, u32[]{:S(2)}, u32[]{:S(2)}) collective-permute-start(bf16[72,2304]{1,0:T(8,128)(2,1)} %bitcast.30), channel_id=1, source_target_pairs={{0,16},{16,32},{32,48},{48,64},{64,80},{80,96},{96,112},{112,0},{1... | collective-permute-start | bytes 995336 | tf_op jit(solution)/shard_map/ppermute | solution.py:48
  14.8 8.5 %collective-permute-start.3 = (bf16[72,2304]{1,0:T(8,128)(2,1)S(1)}, bf16[72,2304]{1,0:T(8,128)(2,1)S(1)}, u32[]{:S(2)}, u32[]{:S(2)}) collective-permute-start(bf16[72,2304]{1,0:T(8,128)(2,1)S(1)} %collective-permute-done.1.refs_0_), channel_id=1, source_target_pairs={{0,112},{16,0},{32,16},{48,32},{64,48},{80,64},{96,80},{112,96},{1... | collective-permute-start | bytes 995336 | tf_op jit(solution)/shard_map/ppermute | solution.py:48
  18.1 8.6 %collective-permute-start.4 = (bf16[72,2304]{1,0:T(8,128)(2,1)S(1)}, bf16[72,2304]{1,0:T(8,128)(2,1)S(1)}, u32[]{:S(2)}, u32[]{:S(2)}) collective-permute-start(bf16[72,2304]{1,0:T(8,128)(2,1)S(1)} %collective-permute-done.2.refs_1_), channel_id=1, source_target_pairs={{0,16},{16,32},{32,48},{48,64},{64,80},{80,96},{96,112},{112,0},{1... | collective-permute-start | bytes 995336 | tf_op jit(solution)/shard_map/ppermute | solution.py:48
  23.3 7.7 %collective-permute-start.5 = (bf16[72,2304]{1,0:T(8,128)(2,1)S(1)}, bf16[72,2304]{1,0:T(8,128)(2,1)S(1)}, u32[]{:S(2)}, u32[]{:S(2)}) collective-permute-start(bf16[72,2304]{1,0:T(8,128)(2,1)S(1)} %collective-permute-done.3.refs_2_), channel_id=1, source_target_pairs={{0,112},{16,0},{32,16},{48,32},{64,48},{80,64},{96,80},{112,96},{1... | collective-permute-start | bytes 995336 | tf_op jit(solution)/shard_map/ppermute | solution.py:48
  26.7 7.2 %collective-permute-start.6 = (bf16[72,2304]{1,0:T(8,128)(2,1)S(1)}, bf16[72,2304]{1,0:T(8,128)(2,1)S(1)}, u32[]{:S(2)}, u32[]{:S(2)}) collective-permute-start(bf16[72,2304]{1,0:T(8,128)(2,1)S(1)} %collective-permute-done.4.refs_3_), channel_id=1, source_target_pairs={{0,16},{16,32},{32,48},{48,64},{64,80},{80,96},{96,112},{112,0},{1... | collective-permute-start | bytes 995336 | tf_op jit(solution)/shard_map/ppermute | solution.py:48
  26.7 20.6 %collective-permute-start = (bf16[256,2304]{1,0:T(8,128)(2,1)}, bf16[256,2304]{1,0:T(8,128)(2,1)}, u32[]{:S(2)}, u32[]{:S(2)}) collective-permute-start(bf16[256,2304]{1,0:T(8,128)(2,1)} %own_ref.1), channel_id=1, source_target_pairs={{0,8},{8,0},{1,9},{9,1},{2,10},{10,2},{3,11},{11,3},{4,12},{12,4},... | collective-permute-start | bytes 3538952 | tf_op jit(solution)/shard_map/ppermute | solution.py:205
  34.1 13.3 %copy-start = (bf16[256,2304]{1,0:T(8,128)(2,1)S(1)}, bf16[256,2304]{1,0:T(8,128)(2,1)}, u32[]{:S(2)}) copy-start(bf16[256,2304]{1,0:T(8,128)(2,1)} %own_ref.1) | copy-start | bytes 3538948
  34.1 13.3 %copy-start.3 = (bf16[2304,72]{0,1:T(8,128)(2,1)S(1)}, bf16[2304,72]{0,1:T(8,128)(2,1)}, u32[]{:S(2)}) copy-start(bf16[2304,72]{0,1:T(8,128)(2,1)} %param.7) | copy-start | bytes 995332
  35.5 11.8 %collective-permute-start.10 = (bf16[128,2304]{1,0:T(8,128)(2,1)}, bf16[128,2304]{1,0:T(8,128)(2,1)}, u32[]{:S(2)}, u32[]{:S(2)}) collective-permute-start(bf16[128,2304]{1,0:T(8,128)(2,1)} %get-tuple-element.16), channel_id=1, source_target_pairs={{0,8},{8,0},{1,9},{9,1},{2,10},{10,2},{3,11},{11,3},{4,12},{12,4},... | collective-permute-start | bytes 1769480 | tf_op jit(solution)/shard_map/ppermute | solution.py:206
  39.8 7.6 %collective-permute-start.11 = (bf16[128,2304]{1,0:T(8,128)(2,1)}, bf16[128,2304]{1,0:T(8,128)(2,1)}, u32[]{:S(2)}, u32[]{:S(2)}) collective-permute-start(bf16[128,2304]{1,0:T(8,128)(2,1)} %get-tuple-element.15), channel_id=1, source_target_pairs={{0,8},{8,0},{1,9},{9,1},{2,10},{10,2},{3,11},{11,3},{4,12},{12,4},... | collective-permute-start | bytes 1769480 | tf_op jit(solution)/shard_map/ppermute | solution.py:206
  40.5 6.8 %collective-permute-start.7 = (bf16[72,1152]{1,0:T(8,128)(2,1)}, bf16[72,1152]{1,0:T(8,128)(2,1)}, u32[]{:S(2)}, u32[]{:S(2)}) collective-permute-start(bf16[72,1152]{1,0:T(8,128)(2,1)} %get-tuple-element.14), channel_id=1, source_target_pairs={{0,16},{16,32},{32,48},{48,64},{64,80},{80,96},{96,112},{112,0},{1... | collective-permute-start | bytes 497672 | tf_op jit(solution)/shard_map/ppermute | solution.py:48
  40.5 6.8 %collective-permute-start.8 = (bf16[72,1152]{1,0:T(8,128)(2,1)}, bf16[72,1152]{1,0:T(8,128)(2,1)}, u32[]{:S(2)}, u32[]{:S(2)}) collective-permute-start(bf16[72,1152]{1,0:T(8,128)(2,1)} %get-tuple-element.13), channel_id=1, source_target_pairs={{0,112},{16,0},{32,16},{48,32},{64,48},{80,64},{96,80},{112,96},{1... | collective-permute-start | bytes 497672 | tf_op jit(solution)/shard_map/ppermute | solution.py:48
  56.3 28.2 %all-to-all-start = ((bf16[32,32,576]{2,1,0:T(8,128)(2,1)}), bf16[32,32,576]{2,1,0:T(8,128)(2,1)S(1)}, u32[]{:S(2)}, u32[]{:S(2)}) async-start(bf16[32,32,576]{2,1,0:T(8,128)(2,1)} %bitcast.3), calls=%async_computation | async-start | bytes 2621440 | tf_op jit(solution)/shard_map/all_to_all | solution.py:217
  64.7 19.9 %copy-start.4 = (bf16[32,2304]{1,0:T(8,128)(2,1)S(1)}, bf16[32,2304]{1,0:T(8,128)(2,1)}, u32[]{:S(2)}) copy-start(bf16[32,2304]{1,0:T(8,128)(2,1)} %teacher_ref.1) | copy-start | bytes 442372
  86.2 10.0 %all-to-all-start.1 = ((bf16[8,32,128]{2,1,0:T(8,128)(2,1)}), bf16[8,32,128]{2,1,0:T(8,128)(2,1)S(1)}, u32[]{:S(2)}, u32[]{:S(2)}) async-start(bf16[8,32,128]{2,1,0:T(8,128)(2,1)} %get-tuple-element.11), calls=%async_computation.1 | async-start | bytes 131072 | tf_op jit(solution)/shard_map/all_to_all | solution.py:222
  97.6 3.5 %collective-permute-start.12 = (f32[32,2304]{1,0:T(8,128)S(1)}, f32[32,2304]{1,0:T(8,128)S(1)}, u32[]{:S(2)}, u32[]{:S(2)}) collective-permute-start(f32[32,2304]{1,0:T(8,128)S(1)} %slice_select_fusion.1), channel_id=1, source_target_pairs={{0,8},{8,0},{1,9},{9,1},{2,10},{10,2},{3,11},{11,3},{4,12},{12,4},... | collective-permute-start | bytes 884744 | tf_op jit(solution)/shard_map/ppermute | solution.py:43
  129.2 4.2 %collective-permute-start.13 = (f32[32,2304]{1,0:T(8,128)S(1)}, f32[32,2304]{1,0:T(8,128)S(1)}, u32[]{:S(2)}, u32[]{:S(2)}) collective-permute-start(f32[32,2304]{1,0:T(8,128)S(1)} %reshape.54), channel_id=1, source_target_pairs={{0,8},{8,0},{1,9},{9,1},{2,10},{10,2},{3,11},{11,3},{4,12},{12,4},... | collective-permute-start | bytes 884744 | tf_op jit(solution)/shard_map/ppermute | solution.py:35
  135.7 11.9 %all-to-all-start.4 = ((f32[8,96,64]{1,2,0:T(8,128)}), f32[8,96,64]{1,2,0:T(8,128)S(1)}, u32[]{:S(2)}, u32[]{:S(2)}) async-start(f32[8,96,64]{1,2,0:T(8,128)} %pad_maximum_fusion.6), calls=%async_computation.4 | async-start | bytes 524288 | tf_op jit(solution)/shard_map/all_to_all | solution.py:234
  148.3 2.5 %collective-permute-start.14 = (f32[32,2304]{1,0:T(8,128)S(1)}, f32[32,2304]{1,0:T(8,128)S(1)}, u32[]{:S(2)}, u32[]{:S(2)}) collective-permute-start(f32[32,2304]{1,0:T(8,128)S(1)} %slice_select_fusion), channel_id=1, source_target_pairs={{0,8},{8,0},{1,9},{9,1},{2,10},{10,2},{3,11},{11,3},{4,12},{12,4},... | collective-permute-start | bytes 884744 | tf_op jit(solution)/shard_map/ppermute | solution.py:43
  163.1 11.9 %all-to-all-start.6 = ((f32[8,2,2304]{2,1,0:T(2,128)}), f32[8,2,2304]{2,1,0:T(2,128)S(1)}, u32[]{:S(2)}, u32[]{:S(2)}) async-start(f32[8,2,2304]{2,1,0:T(2,128)} %broadcast_in_dim.10), calls=%async_computation.6 | async-start | bytes 294912 | tf_op jit(solution)/shard_map/all_to_all | solution.py:31
  175.9 11.1 %all-to-all-start.7 = ((f32[16,2,2304]{2,1,0:T(2,128)}), f32[16,2,2304]{2,1,0:T(2,128)S(1)}, u32[]{:S(2)}, u32[]{:S(2)}) async-start(f32[16,2,2304]{2,1,0:T(2,128)} %broadcast_in_dim.11), calls=%async_computation.7 | async-start | bytes 589824 | tf_op jit(solution)/shard_map/all_to_all | solution.py:31
  187.2 6.1 %collective-permute-start.15 = (f32[32,2304]{1,0:T(8,128)S(1)}, f32[32,2304]{1,0:T(8,128)S(1)}, u32[]{:S(2)}, u32[]{:S(2)}) collective-permute-start(f32[32,2304]{1,0:T(8,128)S(1)} %reshape.57), channel_id=1, source_target_pairs={{0,8},{8,0},{1,9},{9,1},{2,10},{10,2},{3,11},{11,3},{4,12},{12,4},... | collective-permute-start | bytes 884744 | tf_op jit(solution)/shard_map/ppermute | solution.py:35
  (4 other events, 19.4 us)

commit v4 on v3

--- a/solution.py
+++ b/solution.py
@@ -49,38 +49,20 @@
 
 
 def ring_order(n_z):
-    return [k for far in range(1, n_z // 2) for k in (far, n_z - far)] + [0, n_z // 2]
-
-
-def pack_kernel(*refs):
-    *blocks, out_ref = refs
-    block = blocks[0].shape[0]
-    for k, ref in enumerate(blocks):
-        out_ref[k * block : (k + 1) * block, :] = ref[...]
-
-
-def pack(blocks):
-    block, units = blocks[0].shape
-    vmem = pl.BlockSpec(memory_space=pltpu.VMEM)
-    return pl.pallas_call(
-        pack_kernel,
-        out_shape=jax.ShapeDtypeStruct((len(blocks) * block, units), BF16),
-        in_specs=[vmem] * len(blocks),
-        out_specs=vmem,
-        compiler_params=pltpu.CompilerParams(vmem_limit_bytes=16 * 2**20),
-        cost_estimate=pl.CostEstimate(flops=0, bytes_accessed=4 * len(blocks) * block * units, transcendentals=0),
-    )(*blocks)
+    return [0] + [k for far in range(1, n_z // 2) for k in (far, n_z - far)] + [n_z // 2]
 
 
 def columns_kernel(me_ref, own_ref, c_ref, columns_ref, *refs):
-    *sources, out_ref, x_rows, both_rows, rest, last, products, sems, out_sems = refs
+    *sources, out_ref, x_rows, both_rows, last, products, sems, out_sems = refs
     width = columns_ref.shape[0]
     tokens, units = own_ref.shape
-    block = last.shape[0] // 2
-    top, bottom = pl.ds(0, tokens // 2), pl.ds(tokens // 2, tokens // 2)
     left, right = pl.ds(0, units // 2), pl.ds(units // 2, units // 2)
-    targets = [rest.at[0], rest.at[1, :, left], rest.at[1, :, right]]
-    targets += [x_rows, both_rows.at[top, :], both_rows.at[bottom, :]]
+    targets = [last.at[:, left], last.at[:, right]]
+    targets += [x_rows]
+    at = 0
+    for ref in sources[3:]:
+        targets.append(both_rows.at[at : at + ref.shape[0], :])
+        at += ref.shape[0]
     brought = [pltpu.make_async_copy(x, y, sems.at[k]) for k, (x, y) in enumerate(zip(sources, targets))]
     for copy in brought:
         copy.start()
@@ -95,17 +77,15 @@
         sent[-1].start()
 
     main(0, own_ref)
-    for copy in brought[:3]:
+    for copy in brought[:2]:
         copy.wait()
-    last[:block, :] = rest[0]
-    last[block:, :] = rest[1]
     finish(0, own_ref)
     main(1, c_ref)
     finish(1, c_ref)
-    brought[3].wait()
+    brought[2].wait()
     main(2, x_rows)
     finish(2, x_rows)
-    for copy in brought[4:]:
+    for copy in brought[3:]:
         copy.wait()
     main(3, both_rows)
     finish(3, both_rows)
@@ -117,21 +97,20 @@
     tokens, units = rows[0].shape
     block = rest[0].shape[0]
     me = 2 * lax.axis_index("xl") + lax.axis_index("c")
-    out = jax.ShapeDtypeStruct((4, tokens, columns.shape[0] + 2 * block), BF16)
+    out = jax.ShapeDtypeStruct((4, tokens, columns.shape[0] + block), BF16)
     vmem = pl.BlockSpec(memory_space=pltpu.VMEM)
     hbm = pl.BlockSpec(memory_space=pltpu.HBM)
     return pl.pallas_call(
         columns_kernel,
         out_shape=out,
-        in_specs=[pl.BlockSpec(memory_space=pltpu.SMEM)] + [vmem] * 3 + [hbm] * 6,
+        in_specs=[pl.BlockSpec(memory_space=pltpu.SMEM)] + [vmem] * 3 + [hbm] * (len(rest) + len(halves)),
         out_specs=hbm,
         scratch_shapes=[
             pltpu.VMEM((tokens, units), BF16),
             pltpu.VMEM((tokens, units), BF16),
-            pltpu.VMEM((2, block, units), BF16),
-            pltpu.VMEM((2 * block, units), BF16),
+            pltpu.VMEM((block, units), BF16),
             pltpu.VMEM(out.shape, BF16),
-            pltpu.SemaphoreType.DMA((6,)),
+            pltpu.SemaphoreType.DMA((len(rest) + len(halves),)),
             pltpu.SemaphoreType.DMA((4,)),
         ],
         compiler_params=pltpu.CompilerParams(vmem_limit_bytes=24 * 2**20),
@@ -208,11 +187,11 @@
     for _ in range(n_z // 2 - 1):
         up.append(shift(up[-1], "z", 1))
         down.append(shift(down[-1], "z", -1))
-    columns = pack([down[k] if k < n_z // 2 else up[n_z - k] for k in ring_order(n_z)[:-2]])
-    near = shift(columns[-block:, : units // 2], "z", 1)
-    far = shift(columns[-2 * block : -block, units // 2 :], "z", -1)
+    columns = jnp.concatenate([down[k] if k < n_z // 2 else up[n_z - k] for k in ring_order(n_z)[:-1]], axis=0)
+    near = shift(up[-1][:, : units // 2], "z", 1)
+    far = shift(down[-1][:, units // 2 :], "z", -1)
     memory_term = dot(start_basis, memory, ((0,), (1,)))
-    pieces = column_products((hidden, c_other), columns, (block_t, near, far), [x_other] + both)
+    pieces = column_products((hidden, c_other), columns, (near, far), [x_other] + both)
     pieces = pieces.reshape(4 * n_t, share, n_z * block)
     parts = lax.all_to_all(pieces, ("xl", "c") + TENSOR, 0, 0)
     parts, memory_term = lax.optimization_barrier((parts, memory_term))
@@ -223,8 +202,8 @@
 
     term = memory_term + dot(probe, hidden, ((0,), (0,)))
     half = sum_pair_halves(term, "c", 0)
-    pieces = lax.all_to_all(half.reshape(2 * n_z, -1, units), ("xl", "z"), 0, 0)
-    left = pair(share_out(jnp.sum(pieces, axis=0), ("xl", "z")).reshape(half.shape), "c")
+    pieces = lax.all_to_all(half.astype(BF16).reshape(2 * n_z, -1, units), ("xl", "z"), 0, 0)
+    left = pair(share_out(jnp.sum(pieces.astype(F32), axis=0), ("xl", "z")).reshape(half.shape), "c")
 
     left2 = split_bf16(left)
     gram = dot(left, left, ((1,), (1,)), lax.Precision.HIGHEST)

time: 196 us -> 189 us (0.964)
  waiting for transfers between devices: 48.1 us -> 42.4 us
  local copies, waits for them, and re-layouts: 6.28 us -> 9.1 us
  blocking collectives: 38.8 us -> 36 us
    ppermute x8, waiting for transfers between devices: 19.9 us -> 13.3 us  [shift(): return lax.ppermute(x, axis, [(i, (i + by) % n) for i in range(n)])]
    unnamed x16, local copies, waits for them, and re-layouts: 1.74 us -> 5.67 us
  transfers between devices with their start and end apart: 21 -> 21, of which waited for: 13 -> 13; matrix products, arithmetic and copies ran while one was open for 15% -> 18% of each run, Pallas kernels for 0% -> 0%
where the time goes in v4:
time: 189 us; the launch traced here: 188 us
  starting transfers between devices  55.9 us (30%)
  waiting for transfers between devices  42.4 us (22%)
  blocking collectives  36 us (19%)
  matrix products  19.8 us (10%)
  other arithmetic  13.6 us (7%)
  Pallas kernels  10.1 us (5%)
  local copies, waits for them, and re-layouts  9.1 us (5%)
    dot_general x8, matrix products, dot(): lax.dot_general(a, b, (dims, ((), ())), precision=precision, preferred_el...  19.6 us
    ppermute x8, starting transfers between devices, shift(): return lax.ppermute(x, axis, [(i, (i + by) % n) for i in range(n)])  16 us
    ppermute x8, waiting for transfers between devices, shift(): return lax.ppermute(x, axis, [(i, (i + by) % n) for i in range(n)])  13.3 us
    all_to_all x1, blocking collectives, share_out(): return lax.all_to_all(jnp.broadcast_to(x[None], (n,) + x.shape), axes, 0, 0)  13 us
    all_to_all x1, blocking collectives, per_device(): lax.all_to_all(half.astype(BF16).reshape(2 * n_z, -1, units), ('xl', 'z')...  11.7 us
    all_to_all x1, waiting for transfers between devices, per_device(): parts = lax.all_to_all(pieces, ('xl', 'c') + TENSOR, 0, 0)  11.5 us
    all_to_all x1, blocking collectives, per_device(): lax.all_to_all(half.reshape(2 * n_t, -1, feats), ('xl',) + TENSOR, 0, 0)  11.3 us
    pallas_call x1, Pallas kernels, column_products(): pl.pallas_call(columns_kernel, out_shape=out, in_specs=[pl.BlockSpec(memo...  8.56 us
  transfers between devices with their start and end apart: 21, of which 13 were waited for; matrix products, arithmetic and copies ran while one was open for 18% of the time, Pallas kernels for 0%

profile of v4, /device:TPU:1, one launch (start us, length us, event | category | flops | bytes accessed | tf_op | source)
XLA Modules:
  0.0 187.9 jit_solution(5517266038544783612)
XLA Ops:
  0.6 6.5 %collective-permute-start.1 = (bf16[72,2304]{1,0:T(8,128)(2,1)}, bf16[72,2304]{1,0:T(8,128)(2,1)S(1)}, u32[]{:S(2)}, u32[]{:S(2)}) collective-permute-start(bf16[72,2304]{1,0:T(8,128)(2,1)} %bitcast.32), channel_id=1, source_target_pairs={{0,112},{16,0},{32,16},{48,32},{64,48},{80,64},{96,80},{112,96},{1... | collective-permute-start | bytes 995336 | tf_op jit(solution)/shard_map/ppermute | solution.py:48
  13.9 3.3 %collective-permute-start.3 = (bf16[72,2304]{1,0:T(8,128)(2,1)S(1)}, bf16[72,2304]{1,0:T(8,128)(2,1)S(1)}, u32[]{:S(2)}, u32[]{:S(2)}) collective-permute-start(bf16[72,2304]{1,0:T(8,128)(2,1)S(1)} %collective-permute-done.1), channel_id=1, source_target_pairs={{0,112},{16,0},{32,16},{48,32},{64,48},{80,64},{96,80},{112,96},{1... | collective-permute-start | bytes 995336 | tf_op jit(solution)/shard_map/ppermute | solution.py:48
  18.7 4.0 %collective-permute-done.3 = bf16[72,2304]{1,0:T(8,128)(2,1)S(1)} collective-permute-done((bf16[72,2304]{1,0:T(8,128)(2,1)S(1)}, bf16[72,2304]{1,0:T(8,128)(2,1)S(1)}, u32[]{:S(2)}, u32[]{:S(2)}) %collective-permute-start.3) | collective-permute-done | bytes 331808 | tf_op jit(solution)/shard_map/ppermute | solution.py:48
  22.7 3.4 %collective-permute-start.5 = (bf16[72,2304]{1,0:T(8,128)(2,1)S(1)}, bf16[72,2304]{1,0:T(8,128)(2,1)S(1)}, u32[]{:S(2)}, u32[]{:S(2)}) collective-permute-start(bf16[72,2304]{1,0:T(8,128)(2,1)S(1)} %collective-permute-done.3), channel_id=1, source_target_pairs={{0,112},{16,0},{32,16},{48,32},{64,48},{80,64},{96,80},{112,96},{1... | collective-permute-start | bytes 995336 | tf_op jit(solution)/shard_map/ppermute | solution.py:48
  28.1 6.2 %collective-permute-done.6 = bf16[72,2304]{1,0:T(8,128)(2,1)S(1)} collective-permute-done((bf16[72,2304]{1,0:T(8,128)(2,1)S(1)}, bf16[72,2304]{1,0:T(8,128)(2,1)S(1)}, u32[]{:S(2)}, u32[]{:S(2)}) %collective-permute-start.6) | collective-permute-done | bytes 331808 | tf_op jit(solution)/shard_map/ppermute | solution.py:48
  37.3 4.3 %collective-permute-start.10 = (bf16[128,2304]{1,0:T(8,128)(2,1)S(1)}, bf16[128,2304]{1,0:T(8,128)(2,1)S(1)}, u32[]{:S(2)}, u32[]{:S(2)}) collective-permute-start(bf16[128,2304]{1,0:T(8,128)(2,1)S(1)} %get-tuple-element.14), channel_id=1, source_target_pairs={{0,8},{8,0},{1,9},{9,1},{2,10},{10,2},{3,11},{11,3},{4,12},{12,4},... | collective-permute-start | bytes 1769480 | tf_op jit(solution)/shard_map/ppermute | solution.py:185
  44.1 8.6 %shard_map.85 = bf16[4,256,576]{2,1,0:T(8,128)(2,1)} custom-call(s32[1]{0:T(128)} %bitcast.1.me_ref, bf16[256,2304]{1,0:T(8,128)(2,1)S(1)} %copy-done, bf16[256,2304]{1,0:T(8,128)(2,1)} %collective-permute-done.c_ref, bf16[504,2304]{1,0:T(8,128)(2,1)} %constant_dynamic-update-slice_fusion.columns_ref, bf16[72,1152]{1,0:T(8,128)(2,1)S(1)} %collective-permute-done.7.refs_0_, ...), custom_call_target="tpu_custom_call" | custom-call | tf_op jit(solution)/shard_map/pallas_call | solution.py:103
  52.7 8.0 %all-to-all-start = ((bf16[32,32,576]{2,1,0:T(8,128)(2,1)}), bf16[32,32,576]{2,1,0:T(8,128)(2,1)S(1)}, u32[]{:S(2)}, u32[]{:S(2)}) async-start(bf16[32,32,576]{2,1,0:T(8,128)(2,1)} %bitcast.3), calls=%async_computation | async-start | bytes 2621440 | tf_op jit(solution)/shard_map/all_to_all | solution.py:196
  60.8 8.3 %fusion.2 = f32[64,2304]{1,0:T(8,128)} fusion(bf16[2304,64]{0,1:T(8,128)(2,1)} %param.11, bf16[1,2304,2304]{2,1,0:T(8,128)(2,1)} %param.10), kind=kOutput, calls=%fused_computation.2 | convolution fusion | flops 679477248 | bytes 11501568 | tf_op jit(solution)/shard_map/dot_general | solution.py:20
  69.2 11.5 %all-to-all-done.parts_ref = bf16[32,32,576]{2,1,0:T(8,128)(2,1)S(1)} async-done(((bf16[32,32,576]{2,1,0:T(8,128)(2,1)}), bf16[32,32,576]{2,1,0:T(8,128)(2,1)S(1)}, u32[]{:S(2)}, u32[]{:S(2)}) %all-to-all-start) | async-done | bytes 1179680 | tf_op jit(solution)/shard_map/all_to_all | solution.py:196
  82.3 3.4 %all-to-all-start.1 = ((bf16[8,32,128]{2,1,0:T(8,128)(2,1)}), bf16[8,32,128]{2,1,0:T(8,128)(2,1)S(1)}, u32[]{:S(2)}, u32[]{:S(2)}) async-start(bf16[8,32,128]{2,1,0:T(8,128)(2,1)} %get-tuple-element.11), calls=%async_computation.1 | async-start | bytes 131072 | tf_op jit(solution)/shard_map/all_to_all | solution.py:201
  85.6 6.6 %all-to-all-done.1 = bf16[8,32,128]{2,1,0:T(8,128)(2,1)S(1)} async-done(((bf16[8,32,128]{2,1,0:T(8,128)(2,1)}), bf16[8,32,128]{2,1,0:T(8,128)(2,1)S(1)}, u32[]{:S(2)}, u32[]{:S(2)}) %all-to-all-start.1) | async-done | bytes 65568 | tf_op jit(solution)/shard_map/all_to_all | solution.py:201
  97.3 11.7 %all_to_all.40 = bf16[16,2,2304]{2,1,0:T(2,128)(2,1)S(1)} all-to-all(bf16[16,2,2304]{2,1,0:T(2,128)(2,1)S(1)} %reshape.53), channel_id=1, replica_groups=mesh['xl'=2,'z'=8,'c'=2,'y'=4,'xh'=2] {'xl','z'}, dimensions={0} | all-to-all | bytes 294912 | tf_op jit(solution)/shard_map/all_to_all | solution.py:205
  109.2 13.0 %all_to_all.41 = f32[16,2,2304]{2,1,0:T(2,128)S(1)} all-to-all(f32[16,2,2304]{2,1,0:T(2,128)S(1)} %broadcast_in_dim.8), channel_id=1, replica_groups=mesh['xl'=2,'z'=8,'c'=2,'y'=4,'xh'=2] {'xl','z'}, dimensions={0} | all-to-all | bytes 589824 | tf_op jit(solution)/shard_map/all_to_all | solution.py:31
  122.4 2.9 %collective-permute-start.13 = (f32[32,2304]{1,0:T(8,128)S(1)}, f32[32,2304]{1,0:T(8,128)S(1)}, u32[]{:S(2)}, u32[]{:S(2)}) collective-permute-start(f32[32,2304]{1,0:T(8,128)S(1)} %reshape.54), channel_id=1, source_target_pairs={{0,8},{8,0},{1,9},{9,1},{2,10},{10,2},{3,11},{11,3},{4,12},{12,4},... | collective-permute-start | bytes 884744 | tf_op jit(solution)/shard_map/ppermute | solution.py:35
  128.9 3.4 %all-to-all-start.4 = ((f32[8,96,64]{1,2,0:T(8,128)}), f32[8,96,64]{1,2,0:T(8,128)S(1)}, u32[]{:S(2)}, u32[]{:S(2)}) async-start(f32[8,96,64]{1,2,0:T(8,128)} %pad_maximum_fusion.6), calls=%async_computation.4 | async-start | bytes 524288 | tf_op jit(solution)/shard_map/all_to_all | solution.py:213
  132.4 5.6 %fusion = f32[128,2304]{1,0:T(8,128)S(1)} fusion(bf16[1,2304,2304]{2,1,0:T(8,128)(2,1)} %param.10, bf16[64,2304]{1,0:T(8,128)(2,1)S(1)} %get-tuple-element.18, bf16[64,2304]{1,0:T(8,128)(2,1)S(1)} %get-tuple-element.17), kind=kOutput, calls=%fused_computation | convolution fusion | flops 1360134144 | bytes 12386304 | tf_op jit(solution)/shard_map/dot_general | solution.py:20
  137.9 2.9 %all-to-all-done.4 = f32[8,96,64]{1,2,0:T(8,128)S(1)} async-done(((f32[8,96,64]{1,2,0:T(8,128)}), f32[8,96,64]{1,2,0:T(8,128)S(1)}, u32[]{:S(2)}, u32[]{:S(2)}) %all-to-all-start.4) | async-done | bytes 196640 | tf_op jit(solution)/shard_map/all_to_all | solution.py:213
  144.2 11.3 %all_to_all.42 = f32[16,2,2304]{2,1,0:T(2,128)S(1)} all-to-all(f32[16,2,2304]{2,1,0:T(2,128)S(1)} %reshape.56), channel_id=1, replica_groups=mesh['xl'=2,'z'=8,'c'=2,'y'=4,'xh'=2] {'xl','y','xh'}, dimensions={0} | all-to-all | bytes 589824 | tf_op jit(solution)/shard_map/all_to_all | solution.py:221
  156.3 3.7 %all-to-all-start.6 = ((f32[8,2,2304]{2,1,0:T(2,128)}), f32[8,2,2304]{2,1,0:T(2,128)S(1)}, u32[]{:S(2)}, u32[]{:S(2)}) async-start(f32[8,2,2304]{2,1,0:T(2,128)} %broadcast_in_dim.10), calls=%async_computation.6 | async-start | bytes 294912 | tf_op jit(solution)/shard_map/all_to_all | solution.py:31
  160.2 5.9 %cholesky.19 = f32[64,64]{1,0:T(8,128)S(1)} custom-call(f32[64,64]{1,0:T(8,128)S(1)} %copy.45), custom_call_target="Cholesky" | custom-call | tf_op jit(solution)/shard_map/cholesky | solution.py:222
  169.1 3.5 %all-to-all-start.7 = ((f32[16,2,2304]{2,1,0:T(2,128)}), f32[16,2,2304]{2,1,0:T(2,128)S(1)}, u32[]{:S(2)}, u32[]{:S(2)}) async-start(f32[16,2,2304]{2,1,0:T(2,128)} %broadcast_in_dim.11), calls=%async_computation.7 | async-start | bytes 589824 | tf_op jit(solution)/shard_map/all_to_all | solution.py:31
  174.0 4.9 %custom-call.5 = f32[1,64,64]{1,2,0:T(8,128)S(1)} custom-call(f32[1,64,64]{2,1,0:T(8,128)S(1)} %fusion.11), custom_call_target="InvertDiagBlocksLowerTriangular" | custom-call | tf_op jit(solution)/shard_map/triangular_solve | solution.py:224
  180.4 4.5 %collective-permute-start.15 = (f32[32,2304]{1,0:T(8,128)S(1)}, f32[32,2304]{1,0:T(8,128)S(1)}, u32[]{:S(2)}, u32[]{:S(2)}) collective-permute-start(f32[32,2304]{1,0:T(8,128)S(1)} %reshape.57), channel_id=1, source_target_pairs={{0,8},{8,0},{1,9},{9,1},{2,10},{10,2},{3,11},{11,3},{4,12},{12,4},... | collective-permute-start | bytes 884744 | tf_op jit(solution)/shard_map/ppermute | solution.py:35
  (85 shorter events, 39.5 us)
Async XLA Ops:
  0.6 13.3 %collective-permute-start.1 = (bf16[72,2304]{1,0:T(8,128)(2,1)}, bf16[72,2304]{1,0:T(8,128)(2,1)S(1)}, u32[]{:S(2)}, u32[]{:S(2)}) collective-permute-start(bf16[72,2304]{1,0:T(8,128)(2,1)} %bitcast.32), channel_id=1, source_target_pairs={{0,112},{16,0},{32,16},{48,32},{64,48},{80,64},{96,80},{112,96},{1... | collective-permute-start | bytes 995336 | tf_op jit(solution)/shard_map/ppermute | solution.py:48
  7.1 10.8 %collective-permute-start.2 = (bf16[72,2304]{1,0:T(8,128)(2,1)}, bf16[72,2304]{1,0:T(8,128)(2,1)S(1)}, u32[]{:S(2)}, u32[]{:S(2)}) collective-permute-start(bf16[72,2304]{1,0:T(8,128)(2,1)} %bitcast.33), channel_id=1, source_target_pairs={{0,16},{16,32},{32,48},{48,64},{64,80},{80,96},{96,112},{112,0},{1... | collective-permute-start | bytes 995336 | tf_op jit(solution)/shard_map/ppermute | solution.py:48
  7.1 30.1 %collective-permute-start.9 = (bf16[256,2304]{1,0:T(8,128)(2,1)}, bf16[256,2304]{1,0:T(8,128)(2,1)S(1)}, u32[]{:S(2)}, u32[]{:S(2)}) collective-permute-start(bf16[256,2304]{1,0:T(8,128)(2,1)} %own_ref.1), channel_id=1, source_target_pairs={{0,128},{128,0},{1,129},{129,1},{2,130},{130,2},{3,131},{131,3},{4... | collective-permute-start | bytes 3538952 | tf_op jit(solution)/shard_map/ppermute | solution.py:183
  8.3 34.9 %collective-permute-start = (bf16[256,2304]{1,0:T(8,128)(2,1)}, bf16[256,2304]{1,0:T(8,128)(2,1)}, u32[]{:S(2)}, u32[]{:S(2)}) collective-permute-start(bf16[256,2304]{1,0:T(8,128)(2,1)} %own_ref.1), channel_id=1, source_target_pairs={{0,8},{8,0},{1,9},{9,1},{2,10},{10,2},{3,11},{11,3},{4,12},{12,4},... | collective-permute-start | bytes 3538952 | tf_op jit(solution)/shard_map/ppermute | solution.py:184
  13.9 8.8 %collective-permute-start.3 = (bf16[72,2304]{1,0:T(8,128)(2,1)S(1)}, bf16[72,2304]{1,0:T(8,128)(2,1)S(1)}, u32[]{:S(2)}, u32[]{:S(2)}) collective-permute-start(bf16[72,2304]{1,0:T(8,128)(2,1)S(1)} %collective-permute-done.1), channel_id=1, source_target_pairs={{0,112},{16,0},{32,16},{48,32},{64,48},{80,64},{96,80},{112,96},{1... | collective-permute-start | bytes 995336 | tf_op jit(solution)/shard_map/ppermute | solution.py:48
  17.9 8.7 %collective-permute-start.4 = (bf16[72,2304]{1,0:T(8,128)(2,1)S(1)}, bf16[72,2304]{1,0:T(8,128)(2,1)S(1)}, u32[]{:S(2)}, u32[]{:S(2)}) collective-permute-start(bf16[72,2304]{1,0:T(8,128)(2,1)S(1)} %collective-permute-done.2), channel_id=1, source_target_pairs={{0,16},{16,32},{32,48},{48,64},{64,80},{80,96},{96,112},{112,0},{1... | collective-permute-start | bytes 995336 | tf_op jit(solution)/shard_map/ppermute | solution.py:48
  22.7 11.7 %collective-permute-start.5 = (bf16[72,2304]{1,0:T(8,128)(2,1)S(1)}, bf16[72,2304]{1,0:T(8,128)(2,1)S(1)}, u32[]{:S(2)}, u32[]{:S(2)}) collective-permute-start(bf16[72,2304]{1,0:T(8,128)(2,1)S(1)} %collective-permute-done.3), channel_id=1, source_target_pairs={{0,112},{16,0},{32,16},{48,32},{64,48},{80,64},{96,80},{112,96},{1... | collective-permute-start | bytes 995336 | tf_op jit(solution)/shard_map/ppermute | solution.py:48
  26.6 7.8 %collective-permute-start.6 = (bf16[72,2304]{1,0:T(8,128)(2,1)S(1)}, bf16[72,2304]{1,0:T(8,128)(2,1)S(1)}, u32[]{:S(2)}, u32[]{:S(2)}) collective-permute-start(bf16[72,2304]{1,0:T(8,128)(2,1)S(1)} %collective-permute-done.4), channel_id=1, source_target_pairs={{0,16},{16,32},{32,48},{48,64},{64,80},{80,96},{96,112},{112,0},{1... | collective-permute-start | bytes 995336 | tf_op jit(solution)/shard_map/ppermute | solution.py:48
  28.1 16.0 %copy-start = (bf16[256,2304]{1,0:T(8,128)(2,1)S(1)}, bf16[256,2304]{1,0:T(8,128)(2,1)}, u32[]{:S(2)}) copy-start(bf16[256,2304]{1,0:T(8,128)(2,1)} %own_ref.1) | copy-start | bytes 3538948
  34.4 8.9 %collective-permute-start.7 = (bf16[72,1152]{1,0:T(8,128)(2,1)S(1)}, bf16[72,1152]{1,0:T(8,128)(2,1)S(1)}, u32[]{:S(2)}, u32[]{:S(2)}) collective-permute-start(bf16[72,1152]{1,0:T(8,128)(2,1)S(1)} %slice.43), channel_id=1, source_target_pairs={{0,16},{16,32},{32,48},{48,64},{64,80},{80,96},{96,112},{112,0},{1... | collective-permute-start | bytes 497672 | tf_op jit(solution)/shard_map/ppermute | solution.py:48
  34.5 8.8 %collective-permute-start.8 = (bf16[72,1152]{1,0:T(8,128)(2,1)S(1)}, bf16[72,1152]{1,0:T(8,128)(2,1)S(1)}, u32[]{:S(2)}, u32[]{:S(2)}) collective-permute-start(bf16[72,1152]{1,0:T(8,128)(2,1)S(1)} %slice.44), channel_id=1, source_target_pairs={{0,112},{16,0},{32,16},{48,32},{64,48},{80,64},{96,80},{112,96},{1... | collective-permute-start | bytes 497672 | tf_op jit(solution)/shard_map/ppermute | solution.py:48
  37.3 5.9 %collective-permute-start.10 = (bf16[128,2304]{1,0:T(8,128)(2,1)S(1)}, bf16[128,2304]{1,0:T(8,128)(2,1)S(1)}, u32[]{:S(2)}, u32[]{:S(2)}) collective-permute-start(bf16[128,2304]{1,0:T(8,128)(2,1)S(1)} %get-tuple-element.14), channel_id=1, source_target_pairs={{0,8},{8,0},{1,9},{9,1},{2,10},{10,2},{3,11},{11,3},{4,12},{12,4},... | collective-permute-start | bytes 1769480 | tf_op jit(solution)/shard_map/ppermute | solution.py:185
  41.7 2.5 %collective-permute-start.11 = (bf16[128,2304]{1,0:T(8,128)(2,1)S(1)}, bf16[128,2304]{1,0:T(8,128)(2,1)S(1)}, u32[]{:S(2)}, u32[]{:S(2)}) collective-permute-start(bf16[128,2304]{1,0:T(8,128)(2,1)S(1)} %get-tuple-element.13), channel_id=1, source_target_pairs={{0,8},{8,0},{1,9},{9,1},{2,10},{10,2},{3,11},{11,3},{4,12},{12,4},... | collective-permute-start | bytes 1769480 | tf_op jit(solution)/shard_map/ppermute | solution.py:185
  52.7 8.1 %copy-start.2 = (bf16[2304,64]{0,1:T(8,128)(2,1)S(1)}, bf16[2304,64]{0,1:T(8,128)(2,1)}, u32[]{:S(2)}) copy-start(bf16[2304,64]{0,1:T(8,128)(2,1)} %param.11) | copy-start | bytes 884740
  52.7 28.0 %all-to-all-start = ((bf16[32,32,576]{2,1,0:T(8,128)(2,1)}), bf16[32,32,576]{2,1,0:T(8,128)(2,1)S(1)}, u32[]{:S(2)}, u32[]{:S(2)}) async-start(bf16[32,32,576]{2,1,0:T(8,128)(2,1)} %bitcast.3), calls=%async_computation | async-start | bytes 2621440 | tf_op jit(solution)/shard_map/all_to_all | solution.py:196
  60.8 19.9 %copy-start.1 = (bf16[32,2304]{1,0:T(8,128)(2,1)S(1)}, bf16[32,2304]{1,0:T(8,128)(2,1)}, u32[]{:S(2)}) copy-start(bf16[32,2304]{1,0:T(8,128)(2,1)} %teacher_ref.1) | copy-start | bytes 442372
  82.3 10.0 %all-to-all-start.1 = ((bf16[8,32,128]{2,1,0:T(8,128)(2,1)}), bf16[8,32,128]{2,1,0:T(8,128)(2,1)S(1)}, u32[]{:S(2)}, u32[]{:S(2)}) async-start(bf16[8,32,128]{2,1,0:T(8,128)(2,1)} %get-tuple-element.11), calls=%async_computation.1 | async-start | bytes 131072 | tf_op jit(solution)/shard_map/all_to_all | solution.py:201
  93.7 3.5 %collective-permute-start.12 = (f32[32,2304]{1,0:T(8,128)S(1)}, f32[32,2304]{1,0:T(8,128)S(1)}, u32[]{:S(2)}, u32[]{:S(2)}) collective-permute-start(f32[32,2304]{1,0:T(8,128)S(1)} %slice_select_fusion.1), channel_id=1, source_target_pairs={{0,8},{8,0},{1,9},{9,1},{2,10},{10,2},{3,11},{11,3},{4,12},{12,4},... | collective-permute-start | bytes 884744 | tf_op jit(solution)/shard_map/ppermute | solution.py:43
  122.4 4.2 %collective-permute-start.13 = (f32[32,2304]{1,0:T(8,128)S(1)}, f32[32,2304]{1,0:T(8,128)S(1)}, u32[]{:S(2)}, u32[]{:S(2)}) collective-permute-start(f32[32,2304]{1,0:T(8,128)S(1)} %reshape.54), channel_id=1, source_target_pairs={{0,8},{8,0},{1,9},{9,1},{2,10},{10,2},{3,11},{11,3},{4,12},{12,4},... | collective-permute-start | bytes 884744 | tf_op jit(solution)/shard_map/ppermute | solution.py:35
  128.9 11.9 %all-to-all-start.4 = ((f32[8,96,64]{1,2,0:T(8,128)}), f32[8,96,64]{1,2,0:T(8,128)S(1)}, u32[]{:S(2)}, u32[]{:S(2)}) async-start(f32[8,96,64]{1,2,0:T(8,128)} %pad_maximum_fusion.6), calls=%async_computation.4 | async-start | bytes 524288 | tf_op jit(solution)/shard_map/all_to_all | solution.py:213
  141.5 2.5 %collective-permute-start.14 = (f32[32,2304]{1,0:T(8,128)S(1)}, f32[32,2304]{1,0:T(8,128)S(1)}, u32[]{:S(2)}, u32[]{:S(2)}) collective-permute-start(f32[32,2304]{1,0:T(8,128)S(1)} %slice_select_fusion), channel_id=1, source_target_pairs={{0,8},{8,0},{1,9},{9,1},{2,10},{10,2},{3,11},{11,3},{4,12},{12,4},... | collective-permute-start | bytes 884744 | tf_op jit(solution)/shard_map/ppermute | solution.py:43
  156.3 11.9 %all-to-all-start.6 = ((f32[8,2,2304]{2,1,0:T(2,128)}), f32[8,2,2304]{2,1,0:T(2,128)S(1)}, u32[]{:S(2)}, u32[]{:S(2)}) async-start(f32[8,2,2304]{2,1,0:T(2,128)} %broadcast_in_dim.10), calls=%async_computation.6 | async-start | bytes 294912 | tf_op jit(solution)/shard_map/all_to_all | solution.py:31
  169.1 11.1 %all-to-all-start.7 = ((f32[16,2,2304]{2,1,0:T(2,128)}), f32[16,2,2304]{2,1,0:T(2,128)S(1)}, u32[]{:S(2)}, u32[]{:S(2)}) async-start(f32[16,2,2304]{2,1,0:T(2,128)} %broadcast_in_dim.11), calls=%async_computation.7 | async-start | bytes 589824 | tf_op jit(solution)/shard_map/all_to_all | solution.py:31
  180.4 6.1 %collective-permute-start.15 = (f32[32,2304]{1,0:T(8,128)S(1)}, f32[32,2304]{1,0:T(8,128)S(1)}, u32[]{:S(2)}, u32[]{:S(2)}) collective-permute-start(f32[32,2304]{1,0:T(8,128)S(1)} %reshape.57), channel_id=1, source_target_pairs={{0,8},{8,0},{1,9},{9,1},{2,10},{10,2},{3,11},{11,3},{4,12},{12,4},... | collective-permute-start | bytes 884744 | tf_op jit(solution)/shard_map/ppermute | solution.py:35
  (1 other events, 8.1 us)

commit v5 on v4

--- a/solution.py
+++ b/solution.py
@@ -52,15 +52,16 @@
     return [0] + [k for far in range(1, n_z // 2) for k in (far, n_z - far)] + [n_z // 2]
 
 
-def columns_kernel(me_ref, own_ref, c_ref, columns_ref, *refs):
-    *sources, out_ref, x_rows, both_rows, last, products, sems, out_sems = refs
-    width = columns_ref.shape[0]
+def columns_kernel(me_ref, own_ref, c_ref, first_ref, second_ref, *refs):
+    *sources, out_ref, x_rows, both_rows, rest, last, products, sems, out_sems = refs
+    block = rest.shape[1]
+    start, width = first_ref.shape[0], first_ref.shape[0] + second_ref.shape[0]
     tokens, units = own_ref.shape
     left, right = pl.ds(0, units // 2), pl.ds(units // 2, units // 2)
-    targets = [last.at[:, left], last.at[:, right]]
+    targets = [rest.at[0], rest.at[1, :, left], rest.at[1, :, right]]
     targets += [x_rows]
     at = 0
-    for ref in sources[3:]:
+    for ref in sources[4:]:
         targets.append(both_rows.at[at : at + ref.shape[0], :])
         at += ref.shape[0]
     brought = [pltpu.make_async_copy(x, y, sems.at[k]) for k, (x, y) in enumerate(zip(sources, targets))]
@@ -69,7 +70,8 @@
     sent = []
 
     def main(k, ref):
-        products[k, :, :width] = dot(ref[...], columns_ref[...], ((1,), (1,))).astype(BF16)
+        products[k, :, :start] = dot(ref[...], first_ref[...], ((1,), (1,))).astype(BF16)
+        products[k, :, start:width] = dot(ref[...], second_ref[...], ((1,), (1,))).astype(BF16)
 
     def finish(k, ref):
         products[k, :, width:] = dot(ref[...], last[...], ((1,), (1,))).astype(BF16)
@@ -77,15 +79,17 @@
         sent[-1].start()
 
     main(0, own_ref)
-    for copy in brought[:2]:
+    for copy in brought[:3]:
         copy.wait()
+    last[:block, :] = rest[0]
+    last[block:, :] = rest[1]
     finish(0, own_ref)
     main(1, c_ref)
     finish(1, c_ref)
-    brought[2].wait()
+    brought[3].wait()
     main(2, x_rows)
     finish(2, x_rows)
-    for copy in brought[3:]:
+    for copy in brought[4:]:
         copy.wait()
     main(3, both_rows)
     finish(3, both_rows)
@@ -97,24 +101,25 @@
     tokens, units = rows[0].shape
     block = rest[0].shape[0]
     me = 2 * lax.axis_index("xl") + lax.axis_index("c")
-    out = jax.ShapeDtypeStruct((4, tokens, columns.shape[0] + block), BF16)
+    out = jax.ShapeDtypeStruct((4, tokens, sum(x.shape[0] for x in columns) + 2 * block), BF16)
     vmem = pl.BlockSpec(memory_space=pltpu.VMEM)
     hbm = pl.BlockSpec(memory_space=pltpu.HBM)
     return pl.pallas_call(
         columns_kernel,
         out_shape=out,
-        in_specs=[pl.BlockSpec(memory_space=pltpu.SMEM)] + [vmem] * 3 + [hbm] * (len(rest) + len(halves)),
+        in_specs=[pl.BlockSpec(memory_space=pltpu.SMEM)] + [vmem] * 4 + [hbm] * (len(rest) + len(halves)),
         out_specs=hbm,
         scratch_shapes=[
             pltpu.VMEM((tokens, units), BF16),
             pltpu.VMEM((tokens, units), BF16),
-            pltpu.VMEM((block, units), BF16),
+            pltpu.VMEM((2, block, units), BF16),
+            pltpu.VMEM((2 * block, units), BF16),
             pltpu.VMEM(out.shape, BF16),
             pltpu.SemaphoreType.DMA((len(rest) + len(halves),)),
             pltpu.SemaphoreType.DMA((4,)),
         ],
         compiler_params=pltpu.CompilerParams(vmem_limit_bytes=24 * 2**20),
-    )(me.reshape(1), *rows, columns, *rest, *halves)
+    )(me.reshape(1), *rows, *columns, *rest, *halves)
 
 
 def norm_kernel(z_ref, parts_ref, gain_ref, teacher_ref, basis_ref, normed_ref, grad_ref, sent_ref, blocks, mixed_ref, *, tokens):
@@ -187,11 +192,13 @@
     for _ in range(n_z // 2 - 1):
         up.append(shift(up[-1], "z", 1))
         down.append(shift(down[-1], "z", -1))
-    columns = jnp.concatenate([down[k] if k < n_z // 2 else up[n_z - k] for k in ring_order(n_z)[:-1]], axis=0)
+    brought = [down[k] if k < n_z // 2 else up[n_z - k] for k in ring_order(n_z)[:-1]]
+    middle = n_z // 2 - 1
+    columns = [jnp.concatenate(x, axis=0) for x in (brought[:middle], brought[middle:-1])]
     near = shift(up[-1][:, : units // 2], "z", 1)
     far = shift(down[-1][:, units // 2 :], "z", -1)
     memory_term = dot(start_basis, memory, ((0,), (1,)))
-    pieces = column_products((hidden, c_other), columns, (near, far), [x_other] + both)
+    pieces = column_products((hidden, c_other), columns, (brought[-1], near, far), [x_other] + both)
     pieces = pieces.reshape(4 * n_t, share, n_z * block)
     parts = lax.all_to_all(pieces, ("xl", "c") + TENSOR, 0, 0)
     parts, memory_term = lax.optimization_barrier((parts, memory_term))

time: 189 us -> 188 us (level)
  local copies, waits for them, and re-layouts: 9.1 us -> 2.85 us
  starting transfers between devices: 55.9 us -> 59.4 us
  waiting for transfers between devices: 42.4 us -> 44.7 us
    unnamed x16 -> x12, local copies, waits for them, and re-layouts: 5.67 us -> 0.17 us
    all_to_all x1, starting transfers between devices: 8.01 us -> 12.3 us  [per_device(): parts = lax.all_to_all(pieces, ('xl', 'c') + TENSOR, 0, 0)]
    ppermute x8, waiting for transfers between devices: 13.3 us -> 15.8 us  [shift(): return lax.ppermute(x, axis, [(i, (i + by) % n) for i in range(n)])]
  transfers between devices with their start and end apart: 21 -> 21, of which waited for: 13 -> 13; matrix products, arithmetic and copies ran while one was open for 18% -> 15% of each run, Pallas kernels for 0% -> 0%
where the time goes in v5:
time: 188 us; the launch traced here: 187 us
  starting transfers between devices  59.4 us (32%)
  waiting for transfers between devices  44.7 us (24%)
  blocking collectives  36 us (19%)
  matrix products  19.8 us (11%)
  other arithmetic  13.7 us (7%)
  Pallas kernels  9.62 us (5%)
  local copies, waits for them, and re-layouts  2.85 us (2%)
    dot_general x8, matrix products, dot(): lax.dot_general(a, b, (dims, ((), ())), precision=precision, preferred_el...  19.6 us
    ppermute x8, waiting for transfers between devices, shift(): return lax.ppermute(x, axis, [(i, (i + by) % n) for i in range(n)])  15.8 us
    ppermute x8, starting transfers between devices, shift(): return lax.ppermute(x, axis, [(i, (i + by) % n) for i in range(n)])  15.1 us
    all_to_all x1, blocking collectives, share_out(): return lax.all_to_all(jnp.broadcast_to(x[None], (n,) + x.shape), axes, 0, 0)  13 us
    all_to_all x1, starting transfers between devices, per_device(): parts = lax.all_to_all(pieces, ('xl', 'c') + TENSOR, 0, 0)  12.3 us
    all_to_all x1, blocking collectives, per_device(): lax.all_to_all(half.astype(BF16).reshape(2 * n_z, -1, units), ('xl', 'z')...  11.7 us
    all_to_all x1, waiting for transfers between devices, per_device(): parts = lax.all_to_all(pieces, ('xl', 'c') + TENSOR, 0, 0)  11.5 us
    all_to_all x1, blocking collectives, per_device(): lax.all_to_all(half.reshape(2 * n_t, -1, feats), ('xl',) + TENSOR, 0, 0)  11.3 us
  transfers between devices with their start and end apart: 21, of which 13 were waited for; matrix products, arithmetic and copies ran while one was open for 15% of the time, Pallas kernels for 0%

profile of v5, /device:TPU:1, one launch (start us, length us, event | category | flops | bytes accessed | tf_op | source)
XLA Modules:
  0.0 187.1 jit_solution(11758110032274152129)
XLA Ops:
  2.8 5.6 %collective-permute-start.1 = (bf16[72,2304]{1,0:T(8,128)(2,1)}, bf16[72,2304]{1,0:T(8,128)(2,1)S(1)}, u32[]{:S(2)}, u32[]{:S(2)}) collective-permute-start(bf16[72,2304]{1,0:T(8,128)(2,1)} %bitcast.31), channel_id=1, source_target_pairs={{0,112},{16,0},{32,16},{48,32},{64,48},{80,64},{96,80},{112,96},{1... | collective-permute-start | bytes 995336 | tf_op jit(solution)/shard_map/ppermute | solution.py:48
  8.3 6.5 %collective-permute-done.1 = bf16[72,2304]{1,0:T(8,128)(2,1)S(1)} collective-permute-done((bf16[72,2304]{1,0:T(8,128)(2,1)}, bf16[72,2304]{1,0:T(8,128)(2,1)S(1)}, u32[]{:S(2)}, u32[]{:S(2)}) %collective-permute-start.1) | collective-permute-done | bytes 331808 | tf_op jit(solution)/shard_map/ppermute | solution.py:48
  14.8 3.3 %collective-permute-start.3 = (bf16[72,2304]{1,0:T(8,128)(2,1)S(1)}, bf16[72,2304]{1,0:T(8,128)(2,1)S(1)}, u32[]{:S(2)}, u32[]{:S(2)}) collective-permute-start(bf16[72,2304]{1,0:T(8,128)(2,1)S(1)} %collective-permute-done.1), channel_id=1, source_target_pairs={{0,112},{16,0},{32,16},{48,32},{64,48},{80,64},{96,80},{112,96},{1... | collective-permute-start | bytes 995336 | tf_op jit(solution)/shard_map/ppermute | solution.py:48
  20.3 3.1 %collective-permute-done.3 = bf16[72,2304]{1,0:T(8,128)(2,1)S(1)} collective-permute-done((bf16[72,2304]{1,0:T(8,128)(2,1)S(1)}, bf16[72,2304]{1,0:T(8,128)(2,1)S(1)}, u32[]{:S(2)}, u32[]{:S(2)}) %collective-permute-start.3) | collective-permute-done | bytes 331808 | tf_op jit(solution)/shard_map/ppermute | solution.py:48
  23.3 3.4 %collective-permute-start.5 = (bf16[72,2304]{1,0:T(8,128)(2,1)S(1)}, bf16[72,2304]{1,0:T(8,128)(2,1)S(1)}, u32[]{:S(2)}, u32[]{:S(2)}) collective-permute-start(bf16[72,2304]{1,0:T(8,128)(2,1)S(1)} %collective-permute-done.3), channel_id=1, source_target_pairs={{0,112},{16,0},{32,16},{48,32},{64,48},{80,64},{96,80},{112,96},{1... | collective-permute-start | bytes 995336 | tf_op jit(solution)/shard_map/ppermute | solution.py:48
  30.2 3.7 %collective-permute-done.6.refs_0_ = bf16[72,2304]{1,0:T(8,128)(2,1)S(1)} collective-permute-done((bf16[72,2304]{1,0:T(8,128)(2,1)S(1)}, bf16[72,2304]{1,0:T(8,128)(2,1)S(1)}, u32[]{:S(2)}, u32[]{:S(2)}) %collective-permute-start.6) | collective-permute-done | bytes 331808 | tf_op jit(solution)/shard_map/ppermute | solution.py:48
  39.5 8.0 %shard_map.85 = bf16[4,256,576]{2,1,0:T(8,128)(2,1)} custom-call(s32[1]{0:T(128)} %bitcast.1.me_ref, bf16[256,2304]{1,0:T(8,128)(2,1)S(1)} %copy-done, bf16[256,2304]{1,0:T(8,128)(2,1)} %collective-permute-done.c_ref, bf16[216,2304]{1,0:T(8,128)(2,1)S(1)} %pad_maximum_fusion.first_ref, bf16[216,2304]{1,0:T(8,128)(2,1)S(1)} %pad_maximum_fusion.1.second_ref, ...), custom_call_target="tpu_custom_call" | custom-call | tf_op jit(solution)/shard_map/pallas_call | solution.py:107
  47.5 12.3 %all-to-all-start = ((bf16[32,32,576]{2,1,0:T(8,128)(2,1)}), bf16[32,32,576]{2,1,0:T(8,128)(2,1)S(1)}, u32[]{:S(2)}, u32[]{:S(2)}) async-start(bf16[32,32,576]{2,1,0:T(8,128)(2,1)} %bitcast.3), calls=%async_computation | async-start | bytes 2621440 | tf_op jit(solution)/shard_map/all_to_all | solution.py:203
  60.0 8.3 %fusion.2 = f32[64,2304]{1,0:T(8,128)} fusion(bf16[2304,64]{0,1:T(8,128)(2,1)} %param.11, bf16[1,2304,2304]{2,1,0:T(8,128)(2,1)} %param.10), kind=kOutput, calls=%fused_computation.2 | convolution fusion | flops 679477248 | bytes 11501568 | tf_op jit(solution)/shard_map/dot_general | solution.py:20
  68.3 11.5 %all-to-all-done.parts_ref = bf16[32,32,576]{2,1,0:T(8,128)(2,1)S(1)} async-done(((bf16[32,32,576]{2,1,0:T(8,128)(2,1)}), bf16[32,32,576]{2,1,0:T(8,128)(2,1)S(1)}, u32[]{:S(2)}, u32[]{:S(2)}) %all-to-all-start) | async-done | bytes 1179680 | tf_op jit(solution)/shard_map/all_to_all | solution.py:203
  81.4 3.4 %all-to-all-start.1 = ((bf16[8,32,128]{2,1,0:T(8,128)(2,1)}), bf16[8,32,128]{2,1,0:T(8,128)(2,1)S(1)}, u32[]{:S(2)}, u32[]{:S(2)}) async-start(bf16[8,32,128]{2,1,0:T(8,128)(2,1)} %get-tuple-element.11), calls=%async_computation.1 | async-start | bytes 131072 | tf_op jit(solution)/shard_map/all_to_all | solution.py:208
  84.8 6.6 %all-to-all-done.1 = bf16[8,32,128]{2,1,0:T(8,128)(2,1)S(1)} async-done(((bf16[8,32,128]{2,1,0:T(8,128)(2,1)}), bf16[8,32,128]{2,1,0:T(8,128)(2,1)S(1)}, u32[]{:S(2)}, u32[]{:S(2)}) %all-to-all-start.1) | async-done | bytes 65568 | tf_op jit(solution)/shard_map/all_to_all | solution.py:208
  96.4 11.7 %all_to_all.40 = bf16[16,2,2304]{2,1,0:T(2,128)(2,1)S(1)} all-to-all(bf16[16,2,2304]{2,1,0:T(2,128)(2,1)S(1)} %reshape.53), channel_id=1, replica_groups=mesh['xl'=2,'z'=8,'c'=2,'y'=4,'xh'=2] {'xl','z'}, dimensions={0} | all-to-all | bytes 294912 | tf_op jit(solution)/shard_map/all_to_all | solution.py:212
  108.3 13.0 %all_to_all.41 = f32[16,2,2304]{2,1,0:T(2,128)S(1)} all-to-all(f32[16,2,2304]{2,1,0:T(2,128)S(1)} %broadcast_in_dim.8), channel_id=1, replica_groups=mesh['xl'=2,'z'=8,'c'=2,'y'=4,'xh'=2] {'xl','z'}, dimensions={0} | all-to-all | bytes 589824 | tf_op jit(solution)/shard_map/all_to_all | solution.py:31
  121.5 2.9 %collective-permute-start.13 = (f32[32,2304]{1,0:T(8,128)S(1)}, f32[32,2304]{1,0:T(8,128)S(1)}, u32[]{:S(2)}, u32[]{:S(2)}) collective-permute-start(f32[32,2304]{1,0:T(8,128)S(1)} %reshape.54), channel_id=1, source_target_pairs={{0,8},{8,0},{1,9},{9,1},{2,10},{10,2},{3,11},{11,3},{4,12},{12,4},... | collective-permute-start | bytes 884744 | tf_op jit(solution)/shard_map/ppermute | solution.py:35
  128.1 3.4 %all-to-all-start.4 = ((f32[8,96,64]{1,2,0:T(8,128)}), f32[8,96,64]{1,2,0:T(8,128)S(1)}, u32[]{:S(2)}, u32[]{:S(2)}) async-start(f32[8,96,64]{1,2,0:T(8,128)} %pad_maximum_fusion.8), calls=%async_computation.4 | async-start | bytes 524288 | tf_op jit(solution)/shard_map/all_to_all | solution.py:220
  131.5 5.6 %fusion = f32[128,2304]{1,0:T(8,128)S(1)} fusion(bf16[1,2304,2304]{2,1,0:T(8,128)(2,1)} %param.10, bf16[64,2304]{1,0:T(8,128)(2,1)S(1)} %get-tuple-element.18, bf16[64,2304]{1,0:T(8,128)(2,1)S(1)} %get-tuple-element.17), kind=kOutput, calls=%fused_computation | convolution fusion | flops 1360134144 | bytes 12386304 | tf_op jit(solution)/shard_map/dot_general | solution.py:20
  137.1 2.9 %all-to-all-done.4 = f32[8,96,64]{1,2,0:T(8,128)S(1)} async-done(((f32[8,96,64]{1,2,0:T(8,128)}), f32[8,96,64]{1,2,0:T(8,128)S(1)}, u32[]{:S(2)}, u32[]{:S(2)}) %all-to-all-start.4) | async-done | bytes 196640 | tf_op jit(solution)/shard_map/all_to_all | solution.py:220
  143.4 11.3 %all_to_all.42 = f32[16,2,2304]{2,1,0:T(2,128)S(1)} all-to-all(f32[16,2,2304]{2,1,0:T(2,128)S(1)} %reshape.56), channel_id=1, replica_groups=mesh['xl'=2,'z'=8,'c'=2,'y'=4,'xh'=2] {'xl','y','xh'}, dimensions={0} | all-to-all | bytes 589824 | tf_op jit(solution)/shard_map/all_to_all | solution.py:228
  155.5 3.7 %all-to-all-start.6 = ((f32[8,2,2304]{2,1,0:T(2,128)}), f32[8,2,2304]{2,1,0:T(2,128)S(1)}, u32[]{:S(2)}, u32[]{:S(2)}) async-start(f32[8,2,2304]{2,1,0:T(2,128)} %broadcast_in_dim.10), calls=%async_computation.6 | async-start | bytes 294912 | tf_op jit(solution)/shard_map/all_to_all | solution.py:31
  159.4 5.9 %cholesky.19 = f32[64,64]{1,0:T(8,128)S(1)} custom-call(f32[64,64]{1,0:T(8,128)S(1)} %copy.45), custom_call_target="Cholesky" | custom-call | tf_op jit(solution)/shard_map/cholesky | solution.py:229
  168.3 3.5 %all-to-all-start.7 = ((f32[16,2,2304]{2,1,0:T(2,128)}), f32[16,2,2304]{2,1,0:T(2,128)S(1)}, u32[]{:S(2)}, u32[]{:S(2)}) async-start(f32[16,2,2304]{2,1,0:T(2,128)} %broadcast_in_dim.11), calls=%async_computation.7 | async-start | bytes 589824 | tf_op jit(solution)/shard_map/all_to_all | solution.py:31
  173.1 4.9 %custom-call.5 = f32[1,64,64]{1,2,0:T(8,128)S(1)} custom-call(f32[1,64,64]{2,1,0:T(8,128)S(1)} %fusion.11), custom_call_target="InvertDiagBlocksLowerTriangular" | custom-call | tf_op jit(solution)/shard_map/triangular_solve | solution.py:231
  179.6 4.5 %collective-permute-start.15 = (f32[32,2304]{1,0:T(8,128)S(1)}, f32[32,2304]{1,0:T(8,128)S(1)}, u32[]{:S(2)}, u32[]{:S(2)}) collective-permute-start(f32[32,2304]{1,0:T(8,128)S(1)} %reshape.57), channel_id=1, source_target_pairs={{0,8},{8,0},{1,9},{9,1},{2,10},{10,2},{3,11},{11,3},{4,12},{12,4},... | collective-permute-start | bytes 884744 | tf_op jit(solution)/shard_map/ppermute | solution.py:35
  (82 shorter events, 37.1 us)
Async XLA Ops:
  0.6 26.8 %collective-permute-start.9 = (bf16[256,2304]{1,0:T(8,128)(2,1)}, bf16[256,2304]{1,0:T(8,128)(2,1)S(1)}, u32[]{:S(2)}, u32[]{:S(2)}) collective-permute-start(bf16[256,2304]{1,0:T(8,128)(2,1)} %own_ref.1), channel_id=1, source_target_pairs={{0,128},{128,0},{1,129},{129,1},{2,130},{130,2},{3,131},{131,3},{4... | collective-permute-start | bytes 3538952 | tf_op jit(solution)/shard_map/ppermute | solution.py:188
  2.8 12.0 %collective-permute-start.1 = (bf16[72,2304]{1,0:T(8,128)(2,1)}, bf16[72,2304]{1,0:T(8,128)(2,1)S(1)}, u32[]{:S(2)}, u32[]{:S(2)}) collective-permute-start(bf16[72,2304]{1,0:T(8,128)(2,1)} %bitcast.31), channel_id=1, source_target_pairs={{0,112},{16,0},{32,16},{48,32},{64,48},{80,64},{96,80},{112,96},{1... | collective-permute-start | bytes 995336 | tf_op jit(solution)/shard_map/ppermute | solution.py:48
  8.3 9.8 %collective-permute-start.2 = (bf16[72,2304]{1,0:T(8,128)(2,1)}, bf16[72,2304]{1,0:T(8,128)(2,1)S(1)}, u32[]{:S(2)}, u32[]{:S(2)}) collective-permute-start(bf16[72,2304]{1,0:T(8,128)(2,1)} %bitcast.32), channel_id=1, source_target_pairs={{0,16},{16,32},{32,48},{48,64},{64,80},{80,96},{96,112},{112,0},{1... | collective-permute-start | bytes 995336 | tf_op jit(solution)/shard_map/ppermute | solution.py:48
  14.8 8.5 %collective-permute-start.3 = (bf16[72,2304]{1,0:T(8,128)(2,1)S(1)}, bf16[72,2304]{1,0:T(8,128)(2,1)S(1)}, u32[]{:S(2)}, u32[]{:S(2)}) collective-permute-start(bf16[72,2304]{1,0:T(8,128)(2,1)S(1)} %collective-permute-done.1), channel_id=1, source_target_pairs={{0,112},{16,0},{32,16},{48,32},{64,48},{80,64},{96,80},{112,96},{1... | collective-permute-start | bytes 995336 | tf_op jit(solution)/shard_map/ppermute | solution.py:48
  18.1 8.6 %collective-permute-start.4 = (bf16[72,2304]{1,0:T(8,128)(2,1)S(1)}, bf16[72,2304]{1,0:T(8,128)(2,1)S(1)}, u32[]{:S(2)}, u32[]{:S(2)}) collective-permute-start(bf16[72,2304]{1,0:T(8,128)(2,1)S(1)} %collective-permute-done.2), channel_id=1, source_target_pairs={{0,16},{16,32},{32,48},{48,64},{64,80},{80,96},{96,112},{112,0},{1... | collective-permute-start | bytes 995336 | tf_op jit(solution)/shard_map/ppermute | solution.py:48
  18.1 21.3 %collective-permute-start = (bf16[256,2304]{1,0:T(8,128)(2,1)}, bf16[256,2304]{1,0:T(8,128)(2,1)}, u32[]{:S(2)}, u32[]{:S(2)}) collective-permute-start(bf16[256,2304]{1,0:T(8,128)(2,1)} %own_ref.1), channel_id=1, source_target_pairs={{0,8},{8,0},{1,9},{9,1},{2,10},{10,2},{3,11},{11,3},{4,12},{12,4},... | collective-permute-start | bytes 3538952 | tf_op jit(solution)/shard_map/ppermute | solution.py:189
  23.3 10.7 %collective-permute-start.5 = (bf16[72,2304]{1,0:T(8,128)(2,1)S(1)}, bf16[72,2304]{1,0:T(8,128)(2,1)S(1)}, u32[]{:S(2)}, u32[]{:S(2)}) collective-permute-start(bf16[72,2304]{1,0:T(8,128)(2,1)S(1)} %collective-permute-done.3), channel_id=1, source_target_pairs={{0,112},{16,0},{32,16},{48,32},{64,48},{80,64},{96,80},{112,96},{1... | collective-permute-start | bytes 995336 | tf_op jit(solution)/shard_map/ppermute | solution.py:48
  26.7 7.2 %collective-permute-start.6 = (bf16[72,2304]{1,0:T(8,128)(2,1)S(1)}, bf16[72,2304]{1,0:T(8,128)(2,1)S(1)}, u32[]{:S(2)}, u32[]{:S(2)}) collective-permute-start(bf16[72,2304]{1,0:T(8,128)(2,1)S(1)} %collective-permute-done.4), channel_id=1, source_target_pairs={{0,16},{16,32},{32,48},{48,64},{64,80},{80,96},{96,112},{112,0},{1... | collective-permute-start | bytes 995336 | tf_op jit(solution)/shard_map/ppermute | solution.py:48
  27.5 11.9 %collective-permute-start.10 = (bf16[128,2304]{1,0:T(8,128)(2,1)S(1)}, bf16[128,2304]{1,0:T(8,128)(2,1)S(1)}, u32[]{:S(2)}, u32[]{:S(2)}) collective-permute-start(bf16[128,2304]{1,0:T(8,128)(2,1)S(1)} %get-tuple-element.14), channel_id=1, source_target_pairs={{0,8},{8,0},{1,9},{9,1},{2,10},{10,2},{3,11},{11,3},{4,12},{12,4},... | collective-permute-start | bytes 1769480 | tf_op jit(solution)/shard_map/ppermute | solution.py:190
  30.1 9.4 %collective-permute-start.11 = (bf16[128,2304]{1,0:T(8,128)(2,1)S(1)}, bf16[128,2304]{1,0:T(8,128)(2,1)S(1)}, u32[]{:S(2)}, u32[]{:S(2)}) collective-permute-start(bf16[128,2304]{1,0:T(8,128)(2,1)S(1)} %get-tuple-element.13), channel_id=1, source_target_pairs={{0,8},{8,0},{1,9},{9,1},{2,10},{10,2},{3,11},{11,3},{4,12},{12,4},... | collective-permute-start | bytes 1769480 | tf_op jit(solution)/shard_map/ppermute | solution.py:190
  34.0 5.5 %collective-permute-start.7 = (bf16[72,1152]{1,0:T(8,128)(2,1)S(1)}, bf16[72,1152]{1,0:T(8,128)(2,1)S(1)}, u32[]{:S(2)}, u32[]{:S(2)}) collective-permute-start(bf16[72,1152]{1,0:T(8,128)(2,1)S(1)} %slice.43), channel_id=1, source_target_pairs={{0,16},{16,32},{32,48},{48,64},{64,80},{80,96},{96,112},{112,0},{1... | collective-permute-start | bytes 497672 | tf_op jit(solution)/shard_map/ppermute | solution.py:48
  34.1 5.4 %collective-permute-start.8 = (bf16[72,1152]{1,0:T(8,128)(2,1)S(1)}, bf16[72,1152]{1,0:T(8,128)(2,1)S(1)}, u32[]{:S(2)}, u32[]{:S(2)}) collective-permute-start(bf16[72,1152]{1,0:T(8,128)(2,1)S(1)} %slice.44), channel_id=1, source_target_pairs={{0,112},{16,0},{32,16},{48,32},{64,48},{80,64},{96,80},{112,96},{1... | collective-permute-start | bytes 497672 | tf_op jit(solution)/shard_map/ppermute | solution.py:48
  47.5 12.4 %copy-start.4 = (f32[2304]{0:T(1024)S(1)}, f32[2304]{0:T(1024)}, u32[]{:S(2)}) copy-start(f32[2304]{0:T(1024)} %param.8) | copy-start | bytes 27652
  47.5 12.4 %copy-start.2 = (bf16[2304,64]{0,1:T(8,128)(2,1)S(1)}, bf16[2304,64]{0,1:T(8,128)(2,1)}, u32[]{:S(2)}) copy-start(bf16[2304,64]{0,1:T(8,128)(2,1)} %param.11) | copy-start | bytes 884740
  47.5 32.3 %all-to-all-start = ((bf16[32,32,576]{2,1,0:T(8,128)(2,1)}), bf16[32,32,576]{2,1,0:T(8,128)(2,1)S(1)}, u32[]{:S(2)}, u32[]{:S(2)}) async-start(bf16[32,32,576]{2,1,0:T(8,128)(2,1)} %bitcast.3), calls=%async_computation | async-start | bytes 2621440 | tf_op jit(solution)/shard_map/all_to_all | solution.py:203
  60.0 19.9 %copy-start.1 = (bf16[32,2304]{1,0:T(8,128)(2,1)S(1)}, bf16[32,2304]{1,0:T(8,128)(2,1)}, u32[]{:S(2)}) copy-start(bf16[32,2304]{1,0:T(8,128)(2,1)} %teacher_ref.1) | copy-start | bytes 442372
  81.4 10.0 %all-to-all-start.1 = ((bf16[8,32,128]{2,1,0:T(8,128)(2,1)}), bf16[8,32,128]{2,1,0:T(8,128)(2,1)S(1)}, u32[]{:S(2)}, u32[]{:S(2)}) async-start(bf16[8,32,128]{2,1,0:T(8,128)(2,1)} %get-tuple-element.11), calls=%async_computation.1 | async-start | bytes 131072 | tf_op jit(solution)/shard_map/all_to_all | solution.py:208
  92.9 3.5 %collective-permute-start.12 = (f32[32,2304]{1,0:T(8,128)S(1)}, f32[32,2304]{1,0:T(8,128)S(1)}, u32[]{:S(2)}, u32[]{:S(2)}) collective-permute-start(f32[32,2304]{1,0:T(8,128)S(1)} %slice_select_fusion.1), channel_id=1, source_target_pairs={{0,8},{8,0},{1,9},{9,1},{2,10},{10,2},{3,11},{11,3},{4,12},{12,4},... | collective-permute-start | bytes 884744 | tf_op jit(solution)/shard_map/ppermute | solution.py:43
  121.5 4.2 %collective-permute-start.13 = (f32[32,2304]{1,0:T(8,128)S(1)}, f32[32,2304]{1,0:T(8,128)S(1)}, u32[]{:S(2)}, u32[]{:S(2)}) collective-permute-start(f32[32,2304]{1,0:T(8,128)S(1)} %reshape.54), channel_id=1, source_target_pairs={{0,8},{8,0},{1,9},{9,1},{2,10},{10,2},{3,11},{11,3},{4,12},{12,4},... | collective-permute-start | bytes 884744 | tf_op jit(solution)/shard_map/ppermute | solution.py:35
  128.1 11.9 %all-to-all-start.4 = ((f32[8,96,64]{1,2,0:T(8,128)}), f32[8,96,64]{1,2,0:T(8,128)S(1)}, u32[]{:S(2)}, u32[]{:S(2)}) async-start(f32[8,96,64]{1,2,0:T(8,128)} %pad_maximum_fusion.8), calls=%async_computation.4 | async-start | bytes 524288 | tf_op jit(solution)/shard_map/all_to_all | solution.py:220
  140.6 2.5 %collective-permute-start.14 = (f32[32,2304]{1,0:T(8,128)S(1)}, f32[32,2304]{1,0:T(8,128)S(1)}, u32[]{:S(2)}, u32[]{:S(2)}) collective-permute-start(f32[32,2304]{1,0:T(8,128)S(1)} %slice_select_fusion), channel_id=1, source_target_pairs={{0,8},{8,0},{1,9},{9,1},{2,10},{10,2},{3,11},{11,3},{4,12},{12,4},... | collective-permute-start | bytes 884744 | tf_op jit(solution)/shard_map/ppermute | solution.py:43
  155.5 11.9 %all-to-all-start.6 = ((f32[8,2,2304]{2,1,0:T(2,128)}), f32[8,2,2304]{2,1,0:T(2,128)S(1)}, u32[]{:S(2)}, u32[]{:S(2)}) async-start(f32[8,2,2304]{2,1,0:T(2,128)} %broadcast_in_dim.10), calls=%async_computation.6 | async-start | bytes 294912 | tf_op jit(solution)/shard_map/all_to_all | solution.py:31
  168.3 11.1 %all-to-all-start.7 = ((f32[16,2,2304]{2,1,0:T(2,128)}), f32[16,2,2304]{2,1,0:T(2,128)S(1)}, u32[]{:S(2)}, u32[]{:S(2)}) async-start(f32[16,2,2304]{2,1,0:T(2,128)} %broadcast_in_dim.11), calls=%async_computation.7 | async-start | bytes 589824 | tf_op jit(solution)/shard_map/all_to_all | solution.py:31
  179.6 6.1 %collective-permute-start.15 = (f32[32,2304]{1,0:T(8,128)S(1)}, f32[32,2304]{1,0:T(8,128)S(1)}, u32[]{:S(2)}, u32[]{:S(2)}) collective-permute-start(f32[32,2304]{1,0:T(8,128)S(1)} %reshape.57), channel_id=1, source_target_pairs={{0,8},{8,0},{1,9},{9,1},{2,10},{10,2},{3,11},{11,3},{4,12},{12,4},... | collective-permute-start | bytes 884744 | tf_op jit(solution)/shard_map/ppermute | solution.py:35
  (2 other events, 15.4 us)

commit v6 on v5

--- a/solution.py
+++ b/solution.py
@@ -229,10 +229,10 @@
     lower = lax.linalg.cholesky(gram, symmetrize_input=False)
     pieces = share_out(jnp.sum(pieces, axis=0), "z")
     inverse = lax.linalg.triangular_solve(lower, jnp.eye(rank, dtype=F32), left_side=True, lower=True)
-    left_basis = dot(left, inverse, ((0,), (1,)), lax.Precision.HIGHEST) * math.sqrt(all_units)
+    left_basis = dot(left, inverse, ((0,), (1,)), lax.Precision.HIGH) * math.sqrt(all_units)
     left_basis = left_basis.astype(BF16)
     half = share_out(jnp.sum(pieces, axis=0), ("xl",) + TENSOR).reshape(half.shape)
-    right_factor = dot(pair(half, "c"), inverse, ((0,), (1,)), lax.Precision.HIGHEST)
+    right_factor = dot(pair(half, "c"), inverse, ((0,), (1,)), lax.Precision.HIGH)
     return normed, left_basis, right_factor.astype(BF16)
 
 

time: 188 us -> 187 us (level)
  no operation moved by 1% of the time
where the time goes in v6:
time: 187 us
  starting transfers between devices  59.4 us (32%)
  waiting for transfers between devices  44.7 us (24%)
  blocking collectives  36 us (19%)
  matrix products  19.3 us (10%)
  other arithmetic  13.7 us (7%)
  Pallas kernels  9.62 us (5%)
  local copies, waits for them, and re-layouts  2.85 us (2%)
    dot_general x8, matrix products, dot(): lax.dot_general(a, b, (dims, ((), ())), precision=precision, preferred_el...  19.1 us
    ppermute x8, waiting for transfers between devices, shift(): return lax.ppermute(x, axis, [(i, (i + by) % n) for i in range(n)])  15.8 us
    ppermute x8, starting transfers between devices, shift(): return lax.ppermute(x, axis, [(i, (i + by) % n) for i in range(n)])  15.1 us
    all_to_all x1, blocking collectives, share_out(): return lax.all_to_all(jnp.broadcast_to(x[None], (n,) + x.shape), axes, 0, 0)  13 us
    all_to_all x1, starting transfers between devices, per_device(): parts = lax.all_to_all(pieces, ('xl', 'c') + TENSOR, 0, 0)  12.3 us
    all_to_all x1, blocking collectives, per_device(): lax.all_to_all(half.astype(BF16).reshape(2 * n_z, -1, units), ('xl', 'z')...  11.7 us
    all_to_all x1, waiting for transfers between devices, per_device(): parts = lax.all_to_all(pieces, ('xl', 'c') + TENSOR, 0, 0)  11.5 us
    all_to_all x1, blocking collectives, per_device(): lax.all_to_all(half.reshape(2 * n_t, -1, feats), ('xl',) + TENSOR, 0, 0)  11.3 us
  transfers between devices with their start and end apart: 21, of which 13 were waited for; matrix products, arithmetic and copies ran while one was open for 15% of the time, Pallas kernels for 0%

profile of v6, /device:TPU:1, one launch (start us, length us, event | category | flops | bytes accessed | tf_op | source)
XLA Modules:
  0.0 186.5 jit_solution(12017754477556044566)
XLA Ops:
  2.8 5.6 %collective-permute-start.1 = (bf16[72,2304]{1,0:T(8,128)(2,1)}, bf16[72,2304]{1,0:T(8,128)(2,1)S(1)}, u32[]{:S(2)}, u32[]{:S(2)}) collective-permute-start(bf16[72,2304]{1,0:T(8,128)(2,1)} %bitcast.31), channel_id=1, source_target_pairs={{0,112},{16,0},{32,16},{48,32},{64,48},{80,64},{96,80},{112,96},{1... | collective-permute-start | bytes 995336 | tf_op jit(solution)/shard_map/ppermute | solution.py:48
  8.3 6.5 %collective-permute-done.1 = bf16[72,2304]{1,0:T(8,128)(2,1)S(1)} collective-permute-done((bf16[72,2304]{1,0:T(8,128)(2,1)}, bf16[72,2304]{1,0:T(8,128)(2,1)S(1)}, u32[]{:S(2)}, u32[]{:S(2)}) %collective-permute-start.1) | collective-permute-done | bytes 331808 | tf_op jit(solution)/shard_map/ppermute | solution.py:48
  14.8 3.3 %collective-permute-start.3 = (bf16[72,2304]{1,0:T(8,128)(2,1)S(1)}, bf16[72,2304]{1,0:T(8,128)(2,1)S(1)}, u32[]{:S(2)}, u32[]{:S(2)}) collective-permute-start(bf16[72,2304]{1,0:T(8,128)(2,1)S(1)} %collective-permute-done.1), channel_id=1, source_target_pairs={{0,112},{16,0},{32,16},{48,32},{64,48},{80,64},{96,80},{112,96},{1... | collective-permute-start | bytes 995336 | tf_op jit(solution)/shard_map/ppermute | solution.py:48
  20.3 3.1 %collective-permute-done.3 = bf16[72,2304]{1,0:T(8,128)(2,1)S(1)} collective-permute-done((bf16[72,2304]{1,0:T(8,128)(2,1)S(1)}, bf16[72,2304]{1,0:T(8,128)(2,1)S(1)}, u32[]{:S(2)}, u32[]{:S(2)}) %collective-permute-start.3) | collective-permute-done | bytes 331808 | tf_op jit(solution)/shard_map/ppermute | solution.py:48
  23.3 3.4 %collective-permute-start.5 = (bf16[72,2304]{1,0:T(8,128)(2,1)S(1)}, bf16[72,2304]{1,0:T(8,128)(2,1)S(1)}, u32[]{:S(2)}, u32[]{:S(2)}) collective-permute-start(bf16[72,2304]{1,0:T(8,128)(2,1)S(1)} %collective-permute-done.3), channel_id=1, source_target_pairs={{0,112},{16,0},{32,16},{48,32},{64,48},{80,64},{96,80},{112,96},{1... | collective-permute-start | bytes 995336 | tf_op jit(solution)/shard_map/ppermute | solution.py:48
  30.2 3.7 %collective-permute-done.6.refs_0_ = bf16[72,2304]{1,0:T(8,128)(2,1)S(1)} collective-permute-done((bf16[72,2304]{1,0:T(8,128)(2,1)S(1)}, bf16[72,2304]{1,0:T(8,128)(2,1)S(1)}, u32[]{:S(2)}, u32[]{:S(2)}) %collective-permute-start.6) | collective-permute-done | bytes 331808 | tf_op jit(solution)/shard_map/ppermute | solution.py:48
  39.5 8.0 %shard_map.85 = bf16[4,256,576]{2,1,0:T(8,128)(2,1)} custom-call(s32[1]{0:T(128)} %bitcast.1.me_ref, bf16[256,2304]{1,0:T(8,128)(2,1)S(1)} %copy-done, bf16[256,2304]{1,0:T(8,128)(2,1)} %collective-permute-done.c_ref, bf16[216,2304]{1,0:T(8,128)(2,1)S(1)} %pad_maximum_fusion.first_ref, bf16[216,2304]{1,0:T(8,128)(2,1)S(1)} %pad_maximum_fusion.1.second_ref, ...), custom_call_target="tpu_custom_call" | custom-call | tf_op jit(solution)/shard_map/pallas_call | solution.py:107
  47.5 12.3 %all-to-all-start = ((bf16[32,32,576]{2,1,0:T(8,128)(2,1)}), bf16[32,32,576]{2,1,0:T(8,128)(2,1)S(1)}, u32[]{:S(2)}, u32[]{:S(2)}) async-start(bf16[32,32,576]{2,1,0:T(8,128)(2,1)} %bitcast.3), calls=%async_computation | async-start | bytes 2621440 | tf_op jit(solution)/shard_map/all_to_all | solution.py:203
  60.0 8.3 %fusion.2 = f32[64,2304]{1,0:T(8,128)} fusion(bf16[2304,64]{0,1:T(8,128)(2,1)} %param.11, bf16[1,2304,2304]{2,1,0:T(8,128)(2,1)} %param.10), kind=kOutput, calls=%fused_computation.2 | convolution fusion | flops 679477248 | bytes 11501568 | tf_op jit(solution)/shard_map/dot_general | solution.py:20
  68.3 11.5 %all-to-all-done.parts_ref = bf16[32,32,576]{2,1,0:T(8,128)(2,1)S(1)} async-done(((bf16[32,32,576]{2,1,0:T(8,128)(2,1)}), bf16[32,32,576]{2,1,0:T(8,128)(2,1)S(1)}, u32[]{:S(2)}, u32[]{:S(2)}) %all-to-all-start) | async-done | bytes 1179680 | tf_op jit(solution)/shard_map/all_to_all | solution.py:203
  81.4 3.4 %all-to-all-start.1 = ((bf16[8,32,128]{2,1,0:T(8,128)(2,1)}), bf16[8,32,128]{2,1,0:T(8,128)(2,1)S(1)}, u32[]{:S(2)}, u32[]{:S(2)}) async-start(bf16[8,32,128]{2,1,0:T(8,128)(2,1)} %get-tuple-element.11), calls=%async_computation.1 | async-start | bytes 131072 | tf_op jit(solution)/shard_map/all_to_all | solution.py:208
  84.8 6.6 %all-to-all-done.1 = bf16[8,32,128]{2,1,0:T(8,128)(2,1)S(1)} async-done(((bf16[8,32,128]{2,1,0:T(8,128)(2,1)}), bf16[8,32,128]{2,1,0:T(8,128)(2,1)S(1)}, u32[]{:S(2)}, u32[]{:S(2)}) %all-to-all-start.1) | async-done | bytes 65568 | tf_op jit(solution)/shard_map/all_to_all | solution.py:208
  96.4 11.7 %all_to_all.40 = bf16[16,2,2304]{2,1,0:T(2,128)(2,1)S(1)} all-to-all(bf16[16,2,2304]{2,1,0:T(2,128)(2,1)S(1)} %reshape.53), channel_id=1, replica_groups=mesh['xl'=2,'z'=8,'c'=2,'y'=4,'xh'=2] {'xl','z'}, dimensions={0} | all-to-all | bytes 294912 | tf_op jit(solution)/shard_map/all_to_all | solution.py:212
  108.3 13.0 %all_to_all.41 = f32[16,2,2304]{2,1,0:T(2,128)S(1)} all-to-all(f32[16,2,2304]{2,1,0:T(2,128)S(1)} %broadcast_in_dim.8), channel_id=1, replica_groups=mesh['xl'=2,'z'=8,'c'=2,'y'=4,'xh'=2] {'xl','z'}, dimensions={0} | all-to-all | bytes 589824 | tf_op jit(solution)/shard_map/all_to_all | solution.py:31
  121.5 2.9 %collective-permute-start.13 = (f32[32,2304]{1,0:T(8,128)S(1)}, f32[32,2304]{1,0:T(8,128)S(1)}, u32[]{:S(2)}, u32[]{:S(2)}) collective-permute-start(f32[32,2304]{1,0:T(8,128)S(1)} %reshape.54), channel_id=1, source_target_pairs={{0,8},{8,0},{1,9},{9,1},{2,10},{10,2},{3,11},{11,3},{4,12},{12,4},... | collective-permute-start | bytes 884744 | tf_op jit(solution)/shard_map/ppermute | solution.py:35
  128.1 3.4 %all-to-all-start.4 = ((f32[8,96,64]{1,2,0:T(8,128)}), f32[8,96,64]{1,2,0:T(8,128)S(1)}, u32[]{:S(2)}, u32[]{:S(2)}) async-start(f32[8,96,64]{1,2,0:T(8,128)} %pad_maximum_fusion.8), calls=%async_computation.4 | async-start | bytes 524288 | tf_op jit(solution)/shard_map/all_to_all | solution.py:220
  131.5 5.6 %fusion = f32[128,2304]{1,0:T(8,128)S(1)} fusion(bf16[1,2304,2304]{2,1,0:T(8,128)(2,1)} %param.10, bf16[64,2304]{1,0:T(8,128)(2,1)S(1)} %get-tuple-element.18, bf16[64,2304]{1,0:T(8,128)(2,1)S(1)} %get-tuple-element.17), kind=kOutput, calls=%fused_computation | convolution fusion | flops 1360134144 | bytes 12386304 | tf_op jit(solution)/shard_map/dot_general | solution.py:20
  137.1 2.9 %all-to-all-done.4 = f32[8,96,64]{1,2,0:T(8,128)S(1)} async-done(((f32[8,96,64]{1,2,0:T(8,128)}), f32[8,96,64]{1,2,0:T(8,128)S(1)}, u32[]{:S(2)}, u32[]{:S(2)}) %all-to-all-start.4) | async-done | bytes 196640 | tf_op jit(solution)/shard_map/all_to_all | solution.py:220
  143.4 11.3 %all_to_all.42 = f32[16,2,2304]{2,1,0:T(2,128)S(1)} all-to-all(f32[16,2,2304]{2,1,0:T(2,128)S(1)} %reshape.56), channel_id=1, replica_groups=mesh['xl'=2,'z'=8,'c'=2,'y'=4,'xh'=2] {'xl','y','xh'}, dimensions={0} | all-to-all | bytes 589824 | tf_op jit(solution)/shard_map/all_to_all | solution.py:228
  155.5 3.7 %all-to-all-start.6 = ((f32[8,2,2304]{2,1,0:T(2,128)}), f32[8,2,2304]{2,1,0:T(2,128)S(1)}, u32[]{:S(2)}, u32[]{:S(2)}) async-start(f32[8,2,2304]{2,1,0:T(2,128)} %broadcast_in_dim.10), calls=%async_computation.6 | async-start | bytes 294912 | tf_op jit(solution)/shard_map/all_to_all | solution.py:31
  159.4 5.9 %cholesky.19 = f32[64,64]{1,0:T(8,128)S(1)} custom-call(f32[64,64]{1,0:T(8,128)S(1)} %copy.45), custom_call_target="Cholesky" | custom-call | tf_op jit(solution)/shard_map/cholesky | solution.py:229
  168.3 3.5 %all-to-all-start.7 = ((f32[16,2,2304]{2,1,0:T(2,128)}), f32[16,2,2304]{2,1,0:T(2,128)S(1)}, u32[]{:S(2)}, u32[]{:S(2)}) async-start(f32[16,2,2304]{2,1,0:T(2,128)} %broadcast_in_dim.11), calls=%async_computation.7 | async-start | bytes 589824 | tf_op jit(solution)/shard_map/all_to_all | solution.py:31
  173.1 4.9 %custom-call.5 = f32[1,64,64]{1,2,0:T(8,128)S(1)} custom-call(f32[1,64,64]{2,1,0:T(8,128)S(1)} %fusion.11), custom_call_target="InvertDiagBlocksLowerTriangular" | custom-call | tf_op jit(solution)/shard_map/triangular_solve | solution.py:231
  179.6 4.5 %collective-permute-start.15 = (f32[32,2304]{1,0:T(8,128)S(1)}, f32[32,2304]{1,0:T(8,128)S(1)}, u32[]{:S(2)}, u32[]{:S(2)}) collective-permute-start(f32[32,2304]{1,0:T(8,128)S(1)} %reshape.57), channel_id=1, source_target_pairs={{0,8},{8,0},{1,9},{9,1},{2,10},{10,2},{3,11},{11,3},{4,12},{12,4},... | collective-permute-start | bytes 884744 | tf_op jit(solution)/shard_map/ppermute | solution.py:35
  (82 shorter events, 36.5 us)
Async XLA Ops:
  0.6 26.8 %collective-permute-start.9 = (bf16[256,2304]{1,0:T(8,128)(2,1)}, bf16[256,2304]{1,0:T(8,128)(2,1)S(1)}, u32[]{:S(2)}, u32[]{:S(2)}) collective-permute-start(bf16[256,2304]{1,0:T(8,128)(2,1)} %own_ref.1), channel_id=1, source_target_pairs={{0,128},{128,0},{1,129},{129,1},{2,130},{130,2},{3,131},{131,3},{4... | collective-permute-start | bytes 3538952 | tf_op jit(solution)/shard_map/ppermute | solution.py:188
  2.8 12.0 %collective-permute-start.1 = (bf16[72,2304]{1,0:T(8,128)(2,1)}, bf16[72,2304]{1,0:T(8,128)(2,1)S(1)}, u32[]{:S(2)}, u32[]{:S(2)}) collective-permute-start(bf16[72,2304]{1,0:T(8,128)(2,1)} %bitcast.31), channel_id=1, source_target_pairs={{0,112},{16,0},{32,16},{48,32},{64,48},{80,64},{96,80},{112,96},{1... | collective-permute-start | bytes 995336 | tf_op jit(solution)/shard_map/ppermute | solution.py:48
  8.3 9.8 %collective-permute-start.2 = (bf16[72,2304]{1,0:T(8,128)(2,1)}, bf16[72,2304]{1,0:T(8,128)(2,1)S(1)}, u32[]{:S(2)}, u32[]{:S(2)}) collective-permute-start(bf16[72,2304]{1,0:T(8,128)(2,1)} %bitcast.32), channel_id=1, source_target_pairs={{0,16},{16,32},{32,48},{48,64},{64,80},{80,96},{96,112},{112,0},{1... | collective-permute-start | bytes 995336 | tf_op jit(solution)/shard_map/ppermute | solution.py:48
  14.8 8.5 %collective-permute-start.3 = (bf16[72,2304]{1,0:T(8,128)(2,1)S(1)}, bf16[72,2304]{1,0:T(8,128)(2,1)S(1)}, u32[]{:S(2)}, u32[]{:S(2)}) collective-permute-start(bf16[72,2304]{1,0:T(8,128)(2,1)S(1)} %collective-permute-done.1), channel_id=1, source_target_pairs={{0,112},{16,0},{32,16},{48,32},{64,48},{80,64},{96,80},{112,96},{1... | collective-permute-start | bytes 995336 | tf_op jit(solution)/shard_map/ppermute | solution.py:48
  18.1 8.6 %collective-permute-start.4 = (bf16[72,2304]{1,0:T(8,128)(2,1)S(1)}, bf16[72,2304]{1,0:T(8,128)(2,1)S(1)}, u32[]{:S(2)}, u32[]{:S(2)}) collective-permute-start(bf16[72,2304]{1,0:T(8,128)(2,1)S(1)} %collective-permute-done.2), channel_id=1, source_target_pairs={{0,16},{16,32},{32,48},{48,64},{64,80},{80,96},{96,112},{112,0},{1... | collective-permute-start | bytes 995336 | tf_op jit(solution)/shard_map/ppermute | solution.py:48
  18.1 21.3 %collective-permute-start = (bf16[256,2304]{1,0:T(8,128)(2,1)}, bf16[256,2304]{1,0:T(8,128)(2,1)}, u32[]{:S(2)}, u32[]{:S(2)}) collective-permute-start(bf16[256,2304]{1,0:T(8,128)(2,1)} %own_ref.1), channel_id=1, source_target_pairs={{0,8},{8,0},{1,9},{9,1},{2,10},{10,2},{3,11},{11,3},{4,12},{12,4},... | collective-permute-start | bytes 3538952 | tf_op jit(solution)/shard_map/ppermute | solution.py:189
  23.3 10.7 %collective-permute-start.5 = (bf16[72,2304]{1,0:T(8,128)(2,1)S(1)}, bf16[72,2304]{1,0:T(8,128)(2,1)S(1)}, u32[]{:S(2)}, u32[]{:S(2)}) collective-permute-start(bf16[72,2304]{1,0:T(8,128)(2,1)S(1)} %collective-permute-done.3), channel_id=1, source_target_pairs={{0,112},{16,0},{32,16},{48,32},{64,48},{80,64},{96,80},{112,96},{1... | collective-permute-start | bytes 995336 | tf_op jit(solution)/shard_map/ppermute | solution.py:48
  26.7 7.2 %collective-permute-start.6 = (bf16[72,2304]{1,0:T(8,128)(2,1)S(1)}, bf16[72,2304]{1,0:T(8,128)(2,1)S(1)}, u32[]{:S(2)}, u32[]{:S(2)}) collective-permute-start(bf16[72,2304]{1,0:T(8,128)(2,1)S(1)} %collective-permute-done.4), channel_id=1, source_target_pairs={{0,16},{16,32},{32,48},{48,64},{64,80},{80,96},{96,112},{112,0},{1... | collective-permute-start | bytes 995336 | tf_op jit(solution)/shard_map/ppermute | solution.py:48
  27.5 11.9 %collective-permute-start.10 = (bf16[128,2304]{1,0:T(8,128)(2,1)S(1)}, bf16[128,2304]{1,0:T(8,128)(2,1)S(1)}, u32[]{:S(2)}, u32[]{:S(2)}) collective-permute-start(bf16[128,2304]{1,0:T(8,128)(2,1)S(1)} %get-tuple-element.14), channel_id=1, source_target_pairs={{0,8},{8,0},{1,9},{9,1},{2,10},{10,2},{3,11},{11,3},{4,12},{12,4},... | collective-permute-start | bytes 1769480 | tf_op jit(solution)/shard_map/ppermute | solution.py:190
  30.1 9.4 %collective-permute-start.11 = (bf16[128,2304]{1,0:T(8,128)(2,1)S(1)}, bf16[128,2304]{1,0:T(8,128)(2,1)S(1)}, u32[]{:S(2)}, u32[]{:S(2)}) collective-permute-start(bf16[128,2304]{1,0:T(8,128)(2,1)S(1)} %get-tuple-element.13), channel_id=1, source_target_pairs={{0,8},{8,0},{1,9},{9,1},{2,10},{10,2},{3,11},{11,3},{4,12},{12,4},... | collective-permute-start | bytes 1769480 | tf_op jit(solution)/shard_map/ppermute | solution.py:190
  34.0 5.5 %collective-permute-start.7 = (bf16[72,1152]{1,0:T(8,128)(2,1)S(1)}, bf16[72,1152]{1,0:T(8,128)(2,1)S(1)}, u32[]{:S(2)}, u32[]{:S(2)}) collective-permute-start(bf16[72,1152]{1,0:T(8,128)(2,1)S(1)} %slice.43), channel_id=1, source_target_pairs={{0,16},{16,32},{32,48},{48,64},{64,80},{80,96},{96,112},{112,0},{1... | collective-permute-start | bytes 497672 | tf_op jit(solution)/shard_map/ppermute | solution.py:48
  34.1 5.4 %collective-permute-start.8 = (bf16[72,1152]{1,0:T(8,128)(2,1)S(1)}, bf16[72,1152]{1,0:T(8,128)(2,1)S(1)}, u32[]{:S(2)}, u32[]{:S(2)}) collective-permute-start(bf16[72,1152]{1,0:T(8,128)(2,1)S(1)} %slice.44), channel_id=1, source_target_pairs={{0,112},{16,0},{32,16},{48,32},{64,48},{80,64},{96,80},{112,96},{1... | collective-permute-start | bytes 497672 | tf_op jit(solution)/shard_map/ppermute | solution.py:48
  47.5 12.4 %copy-start.4 = (f32[2304]{0:T(1024)S(1)}, f32[2304]{0:T(1024)}, u32[]{:S(2)}) copy-start(f32[2304]{0:T(1024)} %param.8) | copy-start | bytes 27652
  47.5 12.4 %copy-start.2 = (bf16[2304,64]{0,1:T(8,128)(2,1)S(1)}, bf16[2304,64]{0,1:T(8,128)(2,1)}, u32[]{:S(2)}) copy-start(bf16[2304,64]{0,1:T(8,128)(2,1)} %param.11) | copy-start | bytes 884740
  47.5 32.3 %all-to-all-start = ((bf16[32,32,576]{2,1,0:T(8,128)(2,1)}), bf16[32,32,576]{2,1,0:T(8,128)(2,1)S(1)}, u32[]{:S(2)}, u32[]{:S(2)}) async-start(bf16[32,32,576]{2,1,0:T(8,128)(2,1)} %bitcast.3), calls=%async_computation | async-start | bytes 2621440 | tf_op jit(solution)/shard_map/all_to_all | solution.py:203
  60.0 19.9 %copy-start.1 = (bf16[32,2304]{1,0:T(8,128)(2,1)S(1)}, bf16[32,2304]{1,0:T(8,128)(2,1)}, u32[]{:S(2)}) copy-start(bf16[32,2304]{1,0:T(8,128)(2,1)} %teacher_ref.1) | copy-start | bytes 442372
  81.4 10.0 %all-to-all-start.1 = ((bf16[8,32,128]{2,1,0:T(8,128)(2,1)}), bf16[8,32,128]{2,1,0:T(8,128)(2,1)S(1)}, u32[]{:S(2)}, u32[]{:S(2)}) async-start(bf16[8,32,128]{2,1,0:T(8,128)(2,1)} %get-tuple-element.11), calls=%async_computation.1 | async-start | bytes 131072 | tf_op jit(solution)/shard_map/all_to_all | solution.py:208
  92.9 3.5 %collective-permute-start.12 = (f32[32,2304]{1,0:T(8,128)S(1)}, f32[32,2304]{1,0:T(8,128)S(1)}, u32[]{:S(2)}, u32[]{:S(2)}) collective-permute-start(f32[32,2304]{1,0:T(8,128)S(1)} %slice_select_fusion.1), channel_id=1, source_target_pairs={{0,8},{8,0},{1,9},{9,1},{2,10},{10,2},{3,11},{11,3},{4,12},{12,4},... | collective-permute-start | bytes 884744 | tf_op jit(solution)/shard_map/ppermute | solution.py:43
  121.5 4.2 %collective-permute-start.13 = (f32[32,2304]{1,0:T(8,128)S(1)}, f32[32,2304]{1,0:T(8,128)S(1)}, u32[]{:S(2)}, u32[]{:S(2)}) collective-permute-start(f32[32,2304]{1,0:T(8,128)S(1)} %reshape.54), channel_id=1, source_target_pairs={{0,8},{8,0},{1,9},{9,1},{2,10},{10,2},{3,11},{11,3},{4,12},{12,4},... | collective-permute-start | bytes 884744 | tf_op jit(solution)/shard_map/ppermute | solution.py:35
  128.1 11.9 %all-to-all-start.4 = ((f32[8,96,64]{1,2,0:T(8,128)}), f32[8,96,64]{1,2,0:T(8,128)S(1)}, u32[]{:S(2)}, u32[]{:S(2)}) async-start(f32[8,96,64]{1,2,0:T(8,128)} %pad_maximum_fusion.8), calls=%async_computation.4 | async-start | bytes 524288 | tf_op jit(solution)/shard_map/all_to_all | solution.py:220
  140.6 2.5 %collective-permute-start.14 = (f32[32,2304]{1,0:T(8,128)S(1)}, f32[32,2304]{1,0:T(8,128)S(1)}, u32[]{:S(2)}, u32[]{:S(2)}) collective-permute-start(f32[32,2304]{1,0:T(8,128)S(1)} %slice_select_fusion), channel_id=1, source_target_pairs={{0,8},{8,0},{1,9},{9,1},{2,10},{10,2},{3,11},{11,3},{4,12},{12,4},... | collective-permute-start | bytes 884744 | tf_op jit(solution)/shard_map/ppermute | solution.py:43
  155.5 11.9 %all-to-all-start.6 = ((f32[8,2,2304]{2,1,0:T(2,128)}), f32[8,2,2304]{2,1,0:T(2,128)S(1)}, u32[]{:S(2)}, u32[]{:S(2)}) async-start(f32[8,2,2304]{2,1,0:T(2,128)} %broadcast_in_dim.10), calls=%async_computation.6 | async-start | bytes 294912 | tf_op jit(solution)/shard_map/all_to_all | solution.py:31
  168.3 11.1 %all-to-all-start.7 = ((f32[16,2,2304]{2,1,0:T(2,128)}), f32[16,2,2304]{2,1,0:T(2,128)S(1)}, u32[]{:S(2)}, u32[]{:S(2)}) async-start(f32[16,2,2304]{2,1,0:T(2,128)} %broadcast_in_dim.11), calls=%async_computation.7 | async-start | bytes 589824 | tf_op jit(solution)/shard_map/all_to_all | solution.py:31
  179.6 5.8 %collective-permute-start.15 = (f32[32,2304]{1,0:T(8,128)S(1)}, f32[32,2304]{1,0:T(8,128)S(1)}, u32[]{:S(2)}, u32[]{:S(2)}) collective-permute-start(f32[32,2304]{1,0:T(8,128)S(1)} %reshape.57), channel_id=1, source_target_pairs={{0,8},{8,0},{1,9},{9,1},{2,10},{10,2},{3,11},{11,3},{4,12},{12,4},... | collective-permute-start | bytes 884744 | tf_op jit(solution)/shard_map/ppermute | solution.py:35
  (2 other events, 15.4 us)
